TPU v7x, 512 devices: a whole 4x4x16 slice. The times are simulated.
512 devices in a mesh: dp: 8 (over y, core), seq: 64 (over x, z).
Axes of the slice: x: 4, y: 4, z: 16, core: 2. Of those that a mesh axis runs over, the one named last changes fastest.
Arguments:
- queries: bfloat16 [8, 16384, 384], P('dp', 'seq'), may hold values from -6 to 6
- keys: bfloat16 [8, 16384, 384], P('dp', 'seq'), may hold values from -6 to 6
- values: bfloat16 [8, 16384, 384], P('dp', 'seq'), may hold values from -6 to 6
- outputs: bfloat16 [8, 16384, 384], P('dp', 'seq'), may hold values from -16 to 16
- d_final: bfloat16 [8, 16384, 768], P('dp', 'seq'), may hold values from -6 to 6
- stats: float32 [8, 16384, 8], P('dp', 'seq'), may hold values from 6.5 to 8
- w_out: bfloat16 [384, 768], replicated, may hold values from -0.21875 to 0.21875
Outputs:
- d_queries: bfloat16 [8, 16384, 384], P('dp', 'seq')
- d_keys: bfloat16 [8, 16384, 384], P('dp', 'seq')
- d_values: bfloat16 [8, 16384, 384], P('dp', 'seq')
- grad_weight: float32 [384, 768], P('seq')
All inputs are finite; a program needn't handle non-finite values.
Results may differ from a plain program's by a relative error of at most 0.0057.
Values may be sent and summed in bfloat16 or wider, within the bound.
No kernel may reach another device: no remote copies, remote signals or barrier semaphores. Data moves between devices by JAX's collectives and lax.ppermute only.
A program may use at most 64 MiB of HBM per device.

v0:
```python
import jax
import jax.numpy as jnp
from jax import lax
from jax.sharding import PartitionSpec as P

GROUP = 8


def swapped(shard, axis, distance):
    return lax.ppermute(shard, axis, [(i, i ^ 1 << distance) for i in range(lax.axis_size(axis))])


def pick(x, stride, heads):
    shaped = x.reshape(x.shape[0] // stride, stride, heads, x.shape[-1])
    return jnp.stack([shaped[:, h % stride, h, :] for h in range(heads)], axis=1)


def place(y, stride, heads, rows):
    shaped = jnp.zeros((rows // stride, stride, heads, y.shape[-1]), jnp.float32)
    for h in range(heads):
        shaped = shaped.at[:, h % stride, h, :].set(y[:, h, :])
    return shaped.reshape(rows, heads, y.shape[-1])


def set_backward(query, d_out, lse, delta, keys, values, scale):
    scores = jnp.einsum("nhc,mhc->hnm", query, keys, preferred_element_type=jnp.float32) * scale
    probs = jnp.exp(scores - jnp.transpose(lse)[:, :, None])
    d_probs = jnp.einsum("nhc,mhc->hnm", d_out, values, preferred_element_type=jnp.float32)
    d_scores = (probs * (d_probs - jnp.transpose(delta)[:, :, None])).astype(jnp.bfloat16)
    probs_low = probs.astype(jnp.bfloat16)
    d_query = jnp.einsum("hnm,mhc->nhc", d_scores, keys, preferred_element_type=jnp.float32) * scale
    d_key = jnp.einsum("hnm,nhc->mhc", d_scores, query, preferred_element_type=jnp.float32) * scale
    d_value = jnp.einsum("hnm,nhc->mhc", probs_low, d_out, preferred_element_type=jnp.float32)
    return (d_query, d_key, d_value)


def group_collect(block, bits):
    where = lax.axis_index("seq")
    gathered = block
    for bit in range(bits):
        other = swapped(gathered, "seq", bit)
        high = where >> bit & 1
        gathered = jnp.where(
            high == 1,
            jnp.concatenate([other, gathered], axis=1),
            jnp.concatenate([gathered, other], axis=1),
        )
    return gathered


def group_return(grads, bits):
    where = lax.axis_index("seq")
    current = grads
    for bit in reversed(range(bits)):
        half = current.shape[1] // 2
        lower = current[:, :half]
        upper = current[:, half:]
        high = where >> bit & 1
        keep = jnp.where(high == 1, upper, lower)
        send = jnp.where(high == 1, lower, upper)
        current = keep + swapped(send, "seq", bit)
    return current


def on_device(queries, keys, values, outputs, d_final, stats, w_out):
    query2 = queries[0]
    key2 = keys[0]
    value2 = values[0]
    output2 = outputs[0]
    upstream = d_final[0]
    lse = stats[0]
    rows = query2.shape[0]
    width = query2.shape[1]
    heads = lse.shape[1]
    size = width // heads
    scale = float(size) ** (-0.5)
    seq_count = lax.axis_size("seq")
    d_out = lax.dot_general(
        upstream, w_out, (((1,), (1,)), ((), ())), preferred_element_type=jnp.float32
    ).astype(jnp.bfloat16)
    query3 = query2.reshape(rows, heads, size)
    key3 = key2.reshape(rows, heads, size)
    value3 = value2.reshape(rows, heads, size)
    dout3 = d_out.reshape(rows, heads, size)
    delta = jnp.sum(
        dout3.astype(jnp.float32) * output2.reshape(rows, heads, size).astype(jnp.float32), axis=-1
    )
    full = lax.dot_general(
        output2, upstream, (((0,), (0,)), ((), ())), preferred_element_type=jnp.float32
    )
    summed = lax.psum(full, "dp")
    grad_weight = lax.psum_scatter(summed, "seq", scatter_dimension=0, tiled=True)
    dq0, dk0, dv0 = set_backward(query3, dout3, lse, delta, key3, value3, scale)
    total_q = dq0
    total_k = dk0
    total_v = dv0

    def level_inputs(stride):
        return (
            pick(query3, stride, heads),
            pick(dout3, stride, heads),
            pick(lse[:, :, None], stride, heads)[..., 0],
            pick(delta[:, :, None], stride, heads)[..., 0],
            pick(key3, stride, heads),
            pick(value3, stride, heads),
        )

    group_bits = GROUP.bit_length() - 1
    pq, pd, pl, pdl, pk, pv = level_inputs(GROUP)
    count = rows // GROUP
    pair = jnp.stack([pk.reshape(count, width), pv.reshape(count, width)])
    remote = group_collect(pair, group_bits)
    dq1, dk1, dv1 = set_backward(
        pq,
        pd,
        pl,
        pdl,
        remote[0].reshape(-1, heads, size),
        remote[1].reshape(-1, heads, size),
        scale,
    )
    back = group_return(jnp.stack([dk1.reshape(-1, width), dv1.reshape(-1, width)]), group_bits)
    total_q = total_q + place(dq1, GROUP, heads, rows)
    total_k = total_k + place(back[0].reshape(count, heads, size), GROUP, heads, rows)
    total_v = total_v + place(back[1].reshape(count, heads, size), GROUP, heads, rows)
    fq, fd, fl, fdl, fk, fv = level_inputs(seq_count)
    far_count = rows // seq_count
    far_pair = jnp.stack([fk.reshape(far_count, width), fv.reshape(far_count, width)])
    far_remote = lax.all_gather(far_pair, "seq", axis=1, tiled=True)
    dq2, dk2, dv2 = set_backward(
        fq,
        fd,
        fl,
        fdl,
        far_remote[0].reshape(-1, heads, size),
        far_remote[1].reshape(-1, heads, size),
        scale,
    )
    far_terms = jnp.stack([dk2.reshape(-1, width), dv2.reshape(-1, width)])
    far_back = lax.psum_scatter(far_terms, "seq", scatter_dimension=1, tiled=True)
    total_q = total_q + place(dq2, seq_count, heads, rows)
    total_k = total_k + place(far_back[0].reshape(far_count, heads, size), seq_count, heads, rows)
    total_v = total_v + place(far_back[1].reshape(far_count, heads, size), seq_count, heads, rows)
    d_queries = total_q.reshape(1, rows, width).astype(jnp.bfloat16)
    d_keys = total_k.reshape(1, rows, width).astype(jnp.bfloat16)
    d_values = total_v.reshape(1, rows, width).astype(jnp.bfloat16)
    return (d_queries, d_keys, d_values, grad_weight)


def solution(mesh):
    placed = (
        P("dp", "seq", None),
        P("dp", "seq", None),
        P("dp", "seq", None),
        P("dp", "seq", None),
        P("dp", "seq", None),
        P("dp", "seq", None),
        P(),
    )
    return jax.shard_map(
        on_device,
        mesh=mesh,
        in_specs=placed,
        out_specs=(
            P("dp", "seq", None),
            P("dp", "seq", None),
            P("dp", "seq", None),
            P("seq", None),
        ),
        check_vma=False,
    )
```

profile of v0, /device:TPU:1, one launch (start us, length us, event | category | flops | bytes accessed | tf_op | source)
XLA Modules:
  0.0 623.7 jit_solution(2512236024374545083)
XLA Ops:
  8.8 131.2 %fusion = f32[8,768]{1,0:T(8,128)} fusion(f32[384,768]{1,0:T(8,128)S(1)} %fusion.28), kind=kCustom, calls=%all-reduce-scatter | all-reduce-scatter fusion | flops 393217 | bytes 1206272
  154.1 73.2 %all_gather.3 = bf16[2,256,384]{2,0,1:T(2,128)(2,1)S(1)} all-gather(bf16[2,4,384]{2,0,1:T(2,128)(2,1)S(1)} %copy.1023), channel_id=1, replica_groups=mesh['dp'=8,'seq'=64] {'seq'}, dimensions={1}, use_global_device_ids=true | all-gather | bytes 399360 | tf_op jit(solution)/shard_map/all_gather | solution.py:129
  246.3 3.7 collective-permute-start.21
  251.0 5.9 collective-permute-start.16
  256.9 6.2 collective-permute-start.15
  263.1 2.8 collective-permute-start.1
  266.5 7.4 %collective-permute-start.14 = (f32[8,768]{1,0:T(8,128)}, f32[8,768]{1,0:T(8,128)S(1)}, u32[]{:S(2)}, u32[]{:S(2)}) collective-permute-start(f32[8,768]{1,0:T(8,128)} %fusion), channel_id=1, source_target_pairs={{0,9},{1,10},{2,11},{3,12},{4,13},{5,14},{6,15},{7,16},{8,17},{9,1... | collective-permute-start | bytes 73736
  274.0 7.2 %collective-permute-start.13 = (f32[8,768]{1,0:T(8,128)}, f32[8,768]{1,0:T(8,128)S(1)}, u32[]{:S(2)}, u32[]{:S(2)}) collective-permute-start(f32[8,768]{1,0:T(8,128)} %fusion), channel_id=1, source_target_pairs={{0,8},{1,9},{2,10},{3,11},{4,12},{5,13},{6,14},{7,15},{8,16},{9,17... | collective-permute-start | bytes 73736
  281.2 5.6 collective-permute-start.12
  286.9 7.5 %collective-permute-start.11 = (f32[8,768]{1,0:T(8,128)}, f32[8,768]{1,0:T(8,128)S(1)}, u32[]{:S(2)}, u32[]{:S(2)}) collective-permute-start(f32[8,768]{1,0:T(8,128)} %fusion), channel_id=1, source_target_pairs={{0,6},{1,7},{2,8},{3,9},{4,10},{5,11},{6,12},{7,13},{8,14},{9,15},... | collective-permute-start | bytes 73736
  294.4 6.5 %collective-permute-start.10 = (f32[8,768]{1,0:T(8,128)}, f32[8,768]{1,0:T(8,128)S(1)}, u32[]{:S(2)}, u32[]{:S(2)}) collective-permute-start(f32[8,768]{1,0:T(8,128)} %fusion), channel_id=1, source_target_pairs={{0,5},{1,6},{2,7},{3,8},{4,9},{5,10},{6,11},{7,12},{8,13},{9,14},{... | collective-permute-start | bytes 73736
  301.1 5.0 collective-permute-start.9
  306.1 3.4 collective-permute-start.8
  311.4 4.2 collective-permute-start.6
  315.6 2.1 collective-permute-start.2
  318.8 2.3 copy.1056
  321.1 2.4 reshape.1814
  325.5 23.5 %concatenate.120 = f32[134,768]{1,0:T(8,128)} concatenate(f32[6,768]{1,0:T(8,128)S(1)} %copy-done.23, f32[8,768]{1,0:T(8,128)} %collective-permute-done.20, f32[8,768]{1,0:T(8,128)} %collective-permute-done.19, f32[8,768]{1,0:T(8,128)} %collective-permute-done.18, f32[8,768]{1,0:T(8,128)} %collective-permute-done.17, f32[8,768]{1,0:T(8,128)S(1)} %copy-done.25, ...), dimensions={0} | concatenate | bytes 823296
  349.8 77.5 %psum.8 = f32[6,768]{1,0:T(8,128)} all-reduce(f32[6,768]{1,0:T(8,128)S(1)} %constant_dynamic-slice_fusion), channel_id=1, replica_groups=mesh['dp'=8,'seq'=64] {'dp'}, use_global_device_ids=true, to_apply=%region_2.0 | all-reduce | flops 4608 | bytes 36864 | tf_op jit(solution)/shard_map/psum | solution.py:91
  444.1 7.2 %collective-permute-start.3 = (f32[2,128,384]{2,1,0:T(8,128)}, f32[2,128,384]{2,1,0:T(8,128)}, u32[]{:S(2)}, u32[]{:S(2)}) collective-permute-start(f32[2,128,384]{2,1,0:T(8,128)} %broadcast_select_fusion), channel_id=1, source_target_pairs={{0,4},{1,5},{2,6},{3,7},{4,0},{5,1},{6,2},{7,3},{8,12},{9,13},{10,... | collective-permute-start | bytes 1179656 | tf_op jit(solution)/shard_map/ppermute | solution.py:10
  453.2 2.3 copy.1002
  455.5 2.6 fusion.12
  459.9 25.7 %collective-permute-done.3 = f32[2,128,384]{2,1,0:T(8,128)} collective-permute-done((f32[2,128,384]{2,1,0:T(8,128)}, f32[2,128,384]{2,1,0:T(8,128)}, u32[]{:S(2)}, u32[]{:S(2)}) %collective-permute-start.3) | collective-permute-done | bytes 393248 | tf_op jit(solution)/shard_map/ppermute | solution.py:10
  490.2 85.7 %all-reduce.11.cloned.1.call-done = f32[2,256,384]{2,1,0:T(8,128)} async-done(((f32[2,256,384]{2,1,0:T(8,128)}), f32[2,256,384]{2,1,0:T(8,128)}) %all-reduce.11.cloned.1.call-update) | async-done | bytes 786448
  582.2 2.3 copy.1063
  584.5 2.4 reshape.1832
  593.4 3.0 collective-permute-start.5
  596.9 2.3 copy.1066
  599.2 2.3 reshape.1850
  603.9 2.3 copy.1060
  608.0 2.3 copy.1065
  610.4 2.4 fusion.11
  (404 shorter events, 86.3 us)
Async XLA Ops:
  7.2 141.7 %copy-start = (bf16[384,768]{1,0:T(8,128)(2,1)S(1)}, bf16[384,768]{1,0:T(8,128)(2,1)}, u32[]{:S(2)}) copy-start(bf16[384,768]{1,0:T(8,128)(2,1)} %param.109) | copy-start | bytes 1769476
  7.2 141.7 %copy-start.7 = (bf16[1,256,768]{2,1,0:T(8,128)(2,1)S(1)}, bf16[1,256,768]{2,1,0:T(8,128)(2,1)}, u32[]{:S(2)}) copy-start(bf16[1,256,768]{2,1,0:T(8,128)(2,1)} %param.107) | copy-start | bytes 1179652
  7.2 140.4 %copy-start.9 = (bf16[1,256,384]{2,1,0:T(8,128)(2,1)S(1)}, bf16[1,256,384]{2,1,0:T(8,128)(2,1)}, u32[]{:S(2)}) copy-start(bf16[1,256,384]{2,1,0:T(8,128)(2,1)} %param.106) | copy-start | bytes 589828
  7.2 140.5 %copy-start.19 = (f32[1,256,8]{1,2,0:T(8,128)S(1)}, f32[1,256,8]{1,2,0:T(8,128)}, u32[]{:S(2)}) copy-start(f32[1,256,8]{1,2,0:T(8,128)} %param.108) | copy-start | bytes 24580
  7.2 142.2 %copy-start.13 = (bf16[1,256,384]{2,1,0:T(8,128)(2,1)S(1)}, bf16[1,256,384]{2,1,0:T(8,128)(2,1)}, u32[]{:S(2)}) copy-start(bf16[1,256,384]{2,1,0:T(8,128)(2,1)} %param.103) | copy-start | bytes 589828
  7.2 568.6 %all-reduce.11.cloned.1.call-start = ((), (), s32[]{:S(2)}) async-start(), calls=%async_computation | async-start | bytes 1572864
  8.8 140.8 %copy-start.10 = (bf16[1,256,384]{2,1,0:T(8,128)(2,1)S(1)}, bf16[1,256,384]{2,1,0:T(8,128)(2,1)}, u32[]{:S(2)}) copy-start(bf16[1,256,384]{2,1,0:T(8,128)(2,1)} %param.104) | copy-start | bytes 589828
  8.8 140.9 %copy-start.11 = (bf16[1,256,384]{2,1,0:T(8,128)(2,1)S(1)}, bf16[1,256,384]{2,1,0:T(8,128)(2,1)}, u32[]{:S(2)}) copy-start(bf16[1,256,384]{2,1,0:T(8,128)(2,1)} %param.105) | copy-start | bytes 589828
  140.1 116.8 %collective-permute-start.20 = (f32[8,768]{1,0:T(8,128)}, f32[8,768]{1,0:T(8,128)}, u32[]{:S(2)}, u32[]{:S(2)}) collective-permute-start(f32[8,768]{1,0:T(8,128)} %fusion), channel_id=1, source_target_pairs={{0,15},{1,16},{2,17},{3,18},{4,19},{5,20},{6,21},{7,22},{8,23},{9,... | collective-permute-start | bytes 73736
  142.0 121.2 %collective-permute-start.19 = (f32[8,768]{1,0:T(8,128)}, f32[8,768]{1,0:T(8,128)}, u32[]{:S(2)}, u32[]{:S(2)}) collective-permute-start(f32[8,768]{1,0:T(8,128)} %fusion), channel_id=1, source_target_pairs={{0,14},{1,15},{2,16},{3,17},{4,18},{5,19},{6,20},{7,21},{8,22},{9,... | collective-permute-start | bytes 73736
  143.8 122.7 %collective-permute-start.18 = (f32[8,768]{1,0:T(8,128)}, f32[8,768]{1,0:T(8,128)}, u32[]{:S(2)}, u32[]{:S(2)}) collective-permute-start(f32[8,768]{1,0:T(8,128)} %fusion), channel_id=1, source_target_pairs={{0,13},{1,14},{2,15},{3,16},{4,17},{5,18},{6,19},{7,20},{8,21},{9,... | collective-permute-start | bytes 73736
  145.7 128.3 %collective-permute-start.17 = (f32[8,768]{1,0:T(8,128)}, f32[8,768]{1,0:T(8,128)}, u32[]{:S(2)}, u32[]{:S(2)}) collective-permute-start(f32[8,768]{1,0:T(8,128)} %fusion), channel_id=1, source_target_pairs={{0,12},{1,13},{2,14},{3,15},{4,16},{5,17},{6,18},{7,19},{8,20},{9,... | collective-permute-start | bytes 73736
  236.7 9.6 %collective-permute-start = (bf16[2,32,384]{2,1,0:T(8,128)(2,1)}, bf16[2,32,384]{2,1,0:T(8,128)(2,1)}, u32[]{:S(2)}, u32[]{:S(2)}) collective-permute-start(bf16[2,32,384]{2,1,0:T(8,128)(2,1)} %constant_dynamic-update-slice_fusion.16), channel_id=1, source_target_pairs={{0,1},{1,0},{2,3},{3,2},{4,5},{5,4},{6,7},{7,6},{8,9},{9,8},{10,11... | collective-permute-start | bytes 147464 | tf_op jit(solution)/shard_map/ppermute | solution.py:10
  246.3 4.6 collective-permute-start.21
  251.0 30.2 %collective-permute-start.16 = (f32[8,768]{1,0:T(8,128)}, f32[8,768]{1,0:T(8,128)S(1)}, u32[]{:S(2)}, u32[]{:S(2)}) collective-permute-start(f32[8,768]{1,0:T(8,128)} %fusion), channel_id=1, source_target_pairs={{0,11},{1,12},{2,13},{3,14},{4,15},{5,16},{6,17},{7,18},{8,19},{9,... | collective-permute-start | bytes 73736
  256.9 29.9 %collective-permute-start.15 = (f32[8,768]{1,0:T(8,128)}, f32[8,768]{1,0:T(8,128)S(1)}, u32[]{:S(2)}, u32[]{:S(2)}) collective-permute-start(f32[8,768]{1,0:T(8,128)} %fusion), channel_id=1, source_target_pairs={{0,10},{1,11},{2,12},{3,13},{4,14},{5,15},{6,16},{7,17},{8,18},{9,... | collective-permute-start | bytes 73736
  263.1 31.3 %collective-permute-start.1 = (bf16[2,64,384]{2,1,0:T(8,128)(2,1)S(1)}, bf16[2,64,384]{2,1,0:T(8,128)(2,1)S(1)}, u32[]{:S(2)}, u32[]{:S(2)}) collective-permute-start(bf16[2,64,384]{2,1,0:T(8,128)(2,1)S(1)} %maximum_select_fusion.2), channel_id=1, source_target_pairs={{0,2},{1,3},{2,0},{3,1},{4,6},{5,7},{6,4},{7,5},{8,10},{9,11},{10,... | collective-permute-start | bytes 294920 | tf_op jit(solution)/shard_map/ppermute | solution.py:10
  266.5 34.5 %collective-permute-start.14 = (f32[8,768]{1,0:T(8,128)}, f32[8,768]{1,0:T(8,128)S(1)}, u32[]{:S(2)}, u32[]{:S(2)}) collective-permute-start(f32[8,768]{1,0:T(8,128)} %fusion), channel_id=1, source_target_pairs={{0,9},{1,10},{2,11},{3,12},{4,13},{5,14},{6,15},{7,16},{8,17},{9,1... | collective-permute-start | bytes 73736
  274.0 32.1 %collective-permute-start.13 = (f32[8,768]{1,0:T(8,128)}, f32[8,768]{1,0:T(8,128)S(1)}, u32[]{:S(2)}, u32[]{:S(2)}) collective-permute-start(f32[8,768]{1,0:T(8,128)} %fusion), channel_id=1, source_target_pairs={{0,8},{1,9},{2,10},{3,11},{4,12},{5,13},{6,14},{7,15},{8,16},{9,17... | collective-permute-start | bytes 73736
  281.2 28.3 %collective-permute-start.12 = (f32[8,768]{1,0:T(8,128)}, f32[8,768]{1,0:T(8,128)S(1)}, u32[]{:S(2)}, u32[]{:S(2)}) collective-permute-start(f32[8,768]{1,0:T(8,128)} %fusion), channel_id=1, source_target_pairs={{0,7},{1,8},{2,9},{3,10},{4,11},{5,12},{6,13},{7,14},{8,15},{9,16}... | collective-permute-start | bytes 73736
  286.9 24.5 %collective-permute-start.11 = (f32[8,768]{1,0:T(8,128)}, f32[8,768]{1,0:T(8,128)S(1)}, u32[]{:S(2)}, u32[]{:S(2)}) collective-permute-start(f32[8,768]{1,0:T(8,128)} %fusion), channel_id=1, source_target_pairs={{0,6},{1,7},{2,8},{3,9},{4,10},{5,11},{6,12},{7,13},{8,14},{9,15},... | collective-permute-start | bytes 73736
  294.4 21.1 %collective-permute-start.10 = (f32[8,768]{1,0:T(8,128)}, f32[8,768]{1,0:T(8,128)S(1)}, u32[]{:S(2)}, u32[]{:S(2)}) collective-permute-start(f32[8,768]{1,0:T(8,128)} %fusion), channel_id=1, source_target_pairs={{0,5},{1,6},{2,7},{3,8},{4,9},{5,10},{6,11},{7,12},{8,13},{9,14},{... | collective-permute-start | bytes 73736
  301.0 126.3 %copy-start.15 = (bf16[2,128,384]{2,1,0:T(8,128)(2,1)}, bf16[2,128,384]{2,1,0:T(8,128)(2,1)S(1)}, u32[]{:S(2)}) copy-start(bf16[2,128,384]{2,1,0:T(8,128)(2,1)S(1)} %maximum_select_fusion.1) | copy-start | bytes 589828
  301.1 24.4 %collective-permute-start.9 = (f32[8,768]{1,0:T(8,128)}, f32[8,768]{1,0:T(8,128)}, u32[]{:S(2)}, u32[]{:S(2)}) collective-permute-start(f32[8,768]{1,0:T(8,128)} %fusion), channel_id=1, source_target_pairs={{0,4},{1,5},{2,6},{3,7},{4,8},{5,9},{6,10},{7,11},{8,12},{9,13},{1... | collective-permute-start | bytes 73736
  306.1 19.3 %collective-permute-start.8 = (f32[8,768]{1,0:T(8,128)}, f32[8,768]{1,0:T(8,128)}, u32[]{:S(2)}, u32[]{:S(2)}) collective-permute-start(f32[8,768]{1,0:T(8,128)} %fusion), channel_id=1, source_target_pairs={{0,3},{1,4},{2,5},{3,6},{4,7},{5,8},{6,9},{7,10},{8,11},{9,12},{10... | collective-permute-start | bytes 73736
  309.5 16.0 %collective-permute-start.7 = (f32[8,768]{1,0:T(8,128)}, f32[8,768]{1,0:T(8,128)}, u32[]{:S(2)}, u32[]{:S(2)}) collective-permute-start(f32[8,768]{1,0:T(8,128)} %fusion), channel_id=1, source_target_pairs={{0,2},{1,3},{2,4},{3,5},{4,6},{5,7},{6,8},{7,9},{8,10},{9,11},{10,... | collective-permute-start | bytes 73736
  311.4 14.1 %collective-permute-start.6 = (f32[8,768]{1,0:T(8,128)}, f32[8,768]{1,0:T(8,128)}, u32[]{:S(2)}, u32[]{:S(2)}) collective-permute-start(f32[8,768]{1,0:T(8,128)} %fusion), channel_id=1, source_target_pairs={{0,1},{1,2},{2,3},{3,4},{4,5},{5,6},{6,7},{7,8},{8,9},{9,10},{10,1... | collective-permute-start | bytes 73736
  315.6 111.7 %collective-permute-start.2 = (bf16[2,128,384]{2,1,0:T(8,128)(2,1)S(1)}, bf16[2,128,384]{2,1,0:T(8,128)(2,1)}, u32[]{:S(2)}, u32[]{:S(2)}) collective-permute-start(bf16[2,128,384]{2,1,0:T(8,128)(2,1)S(1)} %maximum_select_fusion.1), channel_id=1, source_target_pairs={{0,4},{1,5},{2,6},{3,7},{4,0},{5,1},{6,2},{7,3},{8,12},{9,13},{10,... | collective-permute-start | bytes 589832 | tf_op jit(solution)/shard_map/ppermute | solution.py:10
  321.1 111.8 %copy-start.41 = (f32[32,8,1]{0,2,1:T(1,128)S(1)}, f32[32,8,1]{0,2,1:T(1,128)}, u32[]{:S(2)}) copy-start(f32[32,8,1]{0,2,1:T(1,128)} %copy-done.40) | copy-start | bytes 3076
  444.1 41.5 %collective-permute-start.3 = (f32[2,128,384]{2,1,0:T(8,128)}, f32[2,128,384]{2,1,0:T(8,128)}, u32[]{:S(2)}, u32[]{:S(2)}) collective-permute-start(f32[2,128,384]{2,1,0:T(8,128)} %broadcast_select_fusion), channel_id=1, source_target_pairs={{0,4},{1,5},{2,6},{3,7},{4,0},{5,1},{6,2},{7,3},{8,12},{9,13},{10,... | collective-permute-start | bytes 1179656 | tf_op jit(solution)/shard_map/ppermute | solution.py:10
  488.2 103.4 %collective-permute-start.4 = (f32[2,64,384]{2,1,0:T(8,128)}, f32[2,64,384]{2,1,0:T(8,128)}, u32[]{:S(2)}, u32[]{:S(2)}) collective-permute-start(f32[2,64,384]{2,1,0:T(8,128)} %slice_select_fusion), channel_id=1, source_target_pairs={{0,2},{1,3},{2,0},{3,1},{4,6},{5,7},{6,4},{7,5},{8,10},{9,11},{10,... | collective-permute-start | bytes 589832 | tf_op jit(solution)/shard_map/ppermute | solution.py:10
  593.4 8.2 %collective-permute-start.5 = (f32[2,32,384]{2,1,0:T(8,128)S(1)}, f32[2,32,384]{2,1,0:T(8,128)S(1)}, u32[]{:S(2)}, u32[]{:S(2)}) collective-permute-start(f32[2,32,384]{2,1,0:T(8,128)S(1)} %slice_select_fusion.1), channel_id=1, source_target_pairs={{0,1},{1,0},{2,3},{3,2},{4,5},{5,4},{6,7},{7,6},{8,9},{9,8},{10,11... | collective-permute-start | bytes 294920 | tf_op jit(solution)/shard_map/ppermute | solution.py:10
  (35 other events, 548.7 us)
Sparse Core Ops, SparseCore 0:
  233.9 341.9 all-reduce.10
where the time goes:
time: 636 us; the launch traced here: 624 us
  blocking collectives  282 us (44%)
  waiting for transfers between devices  111 us (17%)
  local copies, waits for them, and re-layouts  96.5 us (15%)
  starting transfers between devices  91 us (14%)
  matrix products  17.9 us (3%)
  between operations  16.9 us (3%)
  other arithmetic  8.04 us (1%)
    unnamed x1, blocking collectives  131 us
    unnamed x18, waiting for transfers between devices  85.8 us
    psum x1, blocking collectives, on_device(): summed = lax.psum(full, 'dp')  77.5 us
    all_gather x1, blocking collectives, on_device(): far_remote = lax.all_gather(far_pair, 'seq', axis=1, tiled=True)  73.2 us
    unnamed x17, starting transfers between devices  72.1 us
    unnamed x208, local copies, waits for them, and re-layouts  38 us
    ppermute x6, waiting for transfers between devices, swapped(): lax.ppermute(shard, axis, [(i, i ^ 1 << distance) for i in range(lax.axis...  25.7 us
    scatter x54, local copies, waits for them, and re-layouts, place(): shaped = shaped.at[:, h % stride, h, :].set(y[:, h, :])  23.4 us
  transfers between devices with their start and end apart: 23, of which 2 were waited for; matrix products, arithmetic and copies ran while one was open for 16% of the time, Pallas kernels for 0%

commit v1 on v0

v1 whole, which is shorter than its diff:
```python
import functools

import jax
import jax.numpy as jnp
from jax import lax
from jax.experimental import pallas as pl
from jax.experimental.pallas import tpu as pltpu
from jax.sharding import PartitionSpec as P

HEADS = 8
HD = 48
GROUP = 8
BF = jnp.bfloat16
F32 = jnp.float32


def iota(shape, dim):
    return lax.broadcasted_iota(jnp.int32, shape, dim)


def dot(a, b, ca, cb):
    return lax.dot_general(a, b, (((ca,), (cb,)), ((), ())), preferred_element_type=F32)


def split(x):
    hi = x.astype(BF)
    return hi, (x - hi.astype(F32)).astype(BF)


def eye(n):
    return (iota((n, n), 0) == iota((n, n), 1)).astype(BF)


def packed_token(p):
    return 64 * (p & 3) + 8 * ((p >> 2) & 7) + (p >> 5)


def spread(part, shape, lane_dim, channel_dim):
    return (iota(shape, lane_dim) == HD * part + lax.rem(iota(shape, channel_dim), HD)).astype(BF)


def own_head(rows, width):
    return lax.div(iota((rows, width), 1), HD) == (iota((rows, width), 0) & (GROUP - 1))


def one_hot(rows, cols, row_of):
    return (iota((rows, cols), 0) == row_of(iota((rows, cols), 1))).astype(BF)


def pre_kernel(q_ref, k_ref, v_ref, o_ref, dy_ref, lse_ref, w_ref, pay_ref, top_ref, do_ref, delta_ref):
    rows, width = q_ref.shape
    d_out = dot(dy_ref[...], w_ref[...], 1, 1).astype(BF)
    do_ref[...] = d_out
    hi, lo = split(d_out.astype(F32) * o_ref[...].astype(F32))
    heads = (lax.div(iota((width, 128), 0), HD) == iota((width, 128), 1)).astype(BF)
    delta = dot(hi, heads, 1, 0) + dot(lo, heads, 1, 0)
    delta_ref[...] = delta[:, :HEADS]
    mine = own_head(rows, width)
    pay = jnp.zeros((rows, 256), F32)
    for part, x in enumerate((q_ref[...], k_ref[...], v_ref[...], d_out)):
        pay += dot(jnp.where(mine, x, jnp.zeros_like(x)), spread(part, (width, 256), 1, 0), 1, 0)
    pick = iota((rows, HEADS), 1) == (iota((rows, HEADS), 0) & (GROUP - 1))
    lane = iota((rows, 256), 1)
    for base, x in ((4 * HD, lse_ref[...]), (4 * HD + 3, delta[:, :HEADS])):
        own = jnp.sum(jnp.where(pick, x, 0.0), axis=1, keepdims=True)
        for n in range(3):
            piece = own.astype(BF).astype(F32)
            pay += jnp.where(lane == base + n, piece, 0.0)
            own = own - piece
    pay = pay.astype(BF)
    perm = (iota((rows, rows), 1) == packed_token(iota((rows, rows), 0))).astype(BF)
    pay_ref[...] = dot(perm, pay, 1, 0).astype(BF)
    at, token = iota((8 * HEADS, rows), 0), iota((8 * HEADS, rows), 1)
    here = token == 64 * (at & 3) + (at >> 3)
    first = (here & ((at & 4) == 0)).astype(BF)
    second = (here & ((at & 4) == 4)).astype(BF)
    top = (dot(first, pay[:, :128], 1, 0) + dot(second, pay[:, 128:], 1, 0)).astype(BF)
    for g in range(top_ref.shape[0]):
        top_ref[g] = top


def weight_kernel(o_ref, dy_ref, gw_ref):
    parts, blocks, block_rows, cols = gw_ref.shape
    o_t = jnp.transpose(o_ref[...])
    for d in range(parts):
        piece = dot(o_t, dy_ref[:, cols * d : cols * (d + 1)], 1, 0).astype(BF)
        for x in range(blocks):
            gw_ref[d, x] = piece[block_rows * x : block_rows * (x + 1)]


def weight_mid_kernel(in_ref, out_ref):
    total = jnp.sum(in_ref[...].astype(F32), axis=0).astype(BF)
    rows, cols = total.shape
    total = jnp.concatenate([total, jnp.zeros((rows, 128 - cols), BF)], axis=1)
    at, row = iota((out_ref.shape[1], rows), 0), iota((out_ref.shape[1], rows), 1)
    each = 8 * rows // out_ref.shape[1]
    sel = (((at & 7) < each) & (row == each * (at >> 3) + (at & 7))).astype(BF)
    spaced = dot(sel, total, 1, 0).astype(BF)
    for d in range(out_ref.shape[0]):
        out_ref[d] = spaced


def weight_end_kernel(in_ref, out_ref):
    each, cols = out_ref.shape
    parts = in_ref.shape[0]
    total = jnp.sum(in_ref[...].astype(F32), axis=1)
    out_ref[...] = jnp.concatenate([total[d, :each, : cols // parts] for d in range(parts)], axis=1)


def window(h):
    lo = HD * h // 128 * 128
    hi = -(-HD * (h + 1) // 128) * 128
    return lo, hi


def padded(x_t, before, total):
    parts = []
    if before:
        parts.append(jnp.zeros((before, x_t.shape[1]), x_t.dtype))
    parts.append(x_t)
    after = total - before - x_t.shape[0]
    if after:
        parts.append(jnp.zeros((after, x_t.shape[1]), x_t.dtype))
    return jnp.concatenate(parts, axis=0)


def set_grads(q_win, do_win, k_pad, v_pad, q_t, k_t, do_t, lse, delta):
    scale = float(HD) ** -0.5
    probs = jnp.exp(dot(q_win, k_pad, 1, 0) * scale - lse)
    d_scores = (probs * (dot(do_win, v_pad, 1, 0) - delta)).astype(BF)
    return (
        dot(k_t, d_scores, 1, 1) * scale,
        dot(q_t, d_scores, 1, 0) * scale,
        dot(do_t, probs.astype(BF), 1, 0),
    )


def local_kernel(q_ref, k_ref, v_ref, do_ref, delta_ref, lse_ref, dq_ref, dk_ref, dv_ref, t_ref):
    q_t, k_t, v_t, do_t = (jnp.transpose(r[...]) for r in (q_ref, k_ref, v_ref, do_ref))
    for h in range(HEADS):
        own = slice(HD * h, HD * (h + 1))
        lo, hi = window(h)
        grads = set_grads(
            q_ref[:, lo:hi],
            do_ref[:, lo:hi],
            padded(k_t[own], HD * h - lo, hi - lo),
            padded(v_t[own], HD * h - lo, hi - lo),
            q_t[own],
            k_t[own],
            do_t[own],
            lse_ref[:, h : h + 1],
            delta_ref[:, h : h + 1],
        )
        for n, g in enumerate(grads):
            t_ref[n, own, :] = g
    for n, out in enumerate((dq_ref, dk_ref, dv_ref)):
        out[...] = jnp.transpose(t_ref[n])


def packed_grads(x):
    x_t = dot(eye(256), x, 1, 1).astype(BF)
    tail = x[:, 128:].astype(F32)

    def column(n):
        at = 4 * HD + 3 * n - 128
        return tail[:, at : at + 1] + tail[:, at + 1 : at + 2] + tail[:, at + 2 : at + 3]

    q_t, k_t, v_t, do_t = (x_t[HD * n : HD * (n + 1)] for n in range(4))
    grads = set_grads(
        x[:, :128], x[:, 128:], padded(k_t, 0, 128), padded(v_t, 3 * HD - 128, 128), q_t, k_t, do_t, column(0), column(1)
    )
    return jnp.concatenate(grads, axis=0)


def group_kernel(x_ref, g_ref):
    g_ref[...] = packed_grads(x_ref[...])


def far_kernel(where_ref, y_ref, g_ref, back_ref):
    at, row = iota((256, 512), 0), iota((256, 512), 1)
    first = (row == 8 * (at >> 2) + (at & 3)).astype(BF)
    second = (row == 8 * (at >> 2) + 4 + (at & 3)).astype(BF)
    y = jnp.concatenate([dot(first, y_ref[...], 1, 0), dot(second, y_ref[...], 1, 0)], axis=1)
    far = packed_grads(y.astype(BF))
    row, col = iota((256, 256), 0), iota((256, 256), 1)
    here = (row >> 5) == where_ref[0]
    sel = (here & (col == 32 * ((row >> 2) & 7) + (row & 3))).astype(BF)
    hi, lo = split(far)
    total = (g_ref[...] + dot(hi, sel, 1, 0) + dot(lo, sel, 1, 0)).astype(BF)
    total = jnp.concatenate([total, jnp.zeros((256 - total.shape[0], 256), BF)], axis=0)
    back_ref[...] = dot(eye(256), total, 1, 1).astype(BF)


def final_kernel(z_ref, dq_ref, dk_ref, dv_ref, oq_ref, ok_ref, ov_ref):
    rows, width = dq_ref.shape
    perm_t = (iota((rows, rows), 0) == packed_token(iota((rows, rows), 1))).astype(BF)
    y = dot(perm_t, z_ref[...], 1, 0).astype(BF)
    mine = own_head(rows, width)
    for n, (near, out) in enumerate(((dq_ref, oq_ref), (dk_ref, ok_ref), (dv_ref, ov_ref))):
        far = dot(y, spread(n, (256, width), 0, 1), 1, 0)
        out[...] = (near[...] + jnp.where(mine, far, 0.0)).astype(BF)


def call(kernel, outs, *args, scratch=(), smem=0, flops=0):
    vmem = pl.BlockSpec(memory_space=pltpu.VMEM)
    return pl.pallas_call(
        kernel,
        out_shape=outs,
        in_specs=[pl.BlockSpec(memory_space=pltpu.SMEM)] * smem + [vmem] * (len(args) - smem),
        out_specs=jax.tree.map(lambda _: vmem, outs),
        scratch_shapes=list(scratch),
        compiler_params=pltpu.CompilerParams(vmem_limit_bytes=32 * 1024 * 1024),
        cost_estimate=pl.CostEstimate(flops=flops, bytes_accessed=2_000_000, transcendentals=0),
    )(*args)


def on_device(queries, keys, values, outputs, d_final, stats, w_out):
    q, k, v, o, dy, lse = (x[0] for x in (queries, keys, values, outputs, d_final, stats))
    rows, width = q.shape
    cols = dy.shape[1]
    dp, blocks, ring = lax.axis_size("dp"), lax.axis_size("x"), lax.axis_size(("zh", "zl"))
    groups = lax.axis_size(("x", "zh"))
    shape = jax.ShapeDtypeStruct

    def exchange(x, axes):
        return lax.all_to_all(x, axes, 0, 0, tiled=True)

    gw = call(
        weight_kernel,
        shape((dp, blocks, width // blocks, cols // dp), BF),
        o, dy,
        flops=150_000_000,
    )
    gw = exchange(gw.reshape(dp * blocks, width // blocks, cols // dp), ("dp", "x"))
    pay, top, d_out, delta = call(
        pre_kernel,
        (
            shape((rows, 256), BF),
            shape((groups, 8 * HEADS, 128), BF),
            shape((rows, width), BF),
            shape((rows, HEADS), F32),
        ),
        q, k, v, o, dy, lse, w_out,
        flops=1_000_000_000,
    )
    tops = exchange(top.reshape(groups * GROUP, 8, 128), ("x", "zh", "zl")).reshape(-1, 128)
    mine = exchange(pay.reshape(GROUP, rows // GROUP, 256), "zl").reshape(256, 256)
    dq0, dk0, dv0 = call(
        local_kernel,
        (shape((rows, width), F32),) * 3,
        q, k, v, d_out, delta, lse,
        scratch=[pltpu.VMEM((3, width, rows), F32)],
        flops=1_000_000_000,
    )
    gw = call(weight_mid_kernel, shape((dp, 8 * ring, 128), BF), gw, flops=10_000_000)
    gw = exchange(gw.reshape(dp * ring, 8, 128), ("dp", "zh", "zl"))
    group = call(group_kernel, shape((3 * HD, 256), F32), mine, flops=100_000_000)
    where = lax.axis_index(("x", "zh")).astype(jnp.int32).reshape(1)
    back = call(far_kernel, shape((256, 256), BF), where, tops, group, smem=1, flops=100_000_000)
    z = exchange(back.reshape(GROUP, rows // GROUP, 256), "zl").reshape(256, 256)
    d_q, d_k, d_v = call(final_kernel, (shape((rows, width), BF),) * 3, z, dq0, dk0, dv0, flops=300_000_000)
    grad_weight = call(
        weight_end_kernel,
        shape((width // (blocks * ring), cols), F32),
        gw.reshape(dp, ring, 8, 128),
        flops=1_000_000,
    )
    return d_q[None], d_k[None], d_v[None], grad_weight


def solution(mesh):
    dp, seq = mesh.devices.shape
    fine = jax.sharding.Mesh(
        mesh.devices.reshape(dp, seq // 16, 16 // GROUP, GROUP), ("dp", "x", "zh", "zl")
    )
    seq_axes = ("x", "zh", "zl")
    placed = P("dp", seq_axes, None)
    return jax.shard_map(
        on_device,
        mesh=fine,
        in_specs=(placed,) * 6 + (P(),),
        out_specs=(placed,) * 3 + (P(seq_axes, None),),
        check_vma=False,
    )
```

time: 636 us -> 133 us (0.21); the launches traced: 624 us -> 132 us
  blocking collectives: 282 us -> 23.3 us
  local copies, waits for them, and re-layouts: 96.5 us -> 6.6 us
  waiting for transfers between devices: 111 us -> 52.3 us
  starting transfers between devices: 91 us -> 37.9 us
  matrix products: 17.9 us -> 0 us
  between operations: 16.9 us -> 0.75 us
  Pallas kernels: 0 us -> 11.3 us
  other arithmetic: 8.04 us -> 0 us
    unnamed x1 -> x0, blocking collectives: 131 us -> none
    unnamed x18 -> x0, waiting for transfers between devices: 85.8 us -> none
    psum x1 -> x0, blocking collectives: 77.5 us -> none  [on_device(): summed = lax.psum(full, 'dp')]
    all_gather x1 -> x0, blocking collectives: 73.2 us -> none  [on_device(): far_remote = lax.all_gather(far_pair, 'seq', axis=1, tiled=True)]
    unnamed x17 -> x0, starting transfers between devices: 72.1 us -> none
    all_to_all x0 -> x4, waiting for transfers between devices: none -> 52.3 us  [exchange(): return lax.all_to_all(x, axes, 0, 0, tiled=True)]
    all_to_all x0 -> x4, starting transfers between devices: none -> 37.9 us  [exchange(): return lax.all_to_all(x, axes, 0, 0, tiled=True)]
    unnamed x208 -> x23, local copies, waits for them, and re-layouts: 38 us -> 6.6 us
  transfers between devices with their start and end apart: 23 -> 4, of which waited for: 2 -> 4; matrix products, arithmetic and copies ran while one was open for 16% -> 0% of each run, Pallas kernels for 0% -> 7%
where the time goes in v1:
time: 133 us; the launch traced here: 132 us
  waiting for transfers between devices  52.3 us (39%)
  starting transfers between devices  37.9 us (28%)
  blocking collectives  23.3 us (18%)
  Pallas kernels  11.3 us (8%)
  local copies, waits for them, and re-layouts  6.6 us (5%)
    all_to_all x4, waiting for transfers between devices, exchange(): return lax.all_to_all(x, axes, 0, 0, tiled=True)  52.3 us
    all_to_all x4, starting transfers between devices, exchange(): return lax.all_to_all(x, axes, 0, 0, tiled=True)  37.9 us
    all_to_all x1, blocking collectives, exchange(): return lax.all_to_all(x, axes, 0, 0, tiled=True)  23.3 us
    pallas_call x8, Pallas kernels, call(): pl.pallas_call(kernel, out_shape=outs, in_specs=[pl.BlockSpec(memory_spac...  11.3 us
    unnamed x23, local copies, waits for them, and re-layouts  6.6 us
  transfers between devices with their start and end apart: 4, of which 4 were waited for; matrix products, arithmetic and copies ran while one was open for 0% of the time, Pallas kernels for 7%

profile of v1, /device:TPU:1, one launch (start us, length us, event | category | flops | bytes accessed | tf_op | source)
XLA Modules:
  0.0 132.2 jit_solution(6849304248767120569)
XLA Ops:
  0.6 0.8 copy.11
  1.5 0.0 copy-start
  1.5 1.0 copy-done
  2.5 0.0 copy-start.2
  2.5 0.9 copy-done.2
  3.4 1.1 copy-done.4
  4.5 0.9 copy-done.5
  5.4 0.9 copy-done.7
  6.3 0.9 copy-done.9
  7.2 2.0 %shard_map.102 = (bf16[256,256]{1,0:T(8,128)(2,1)S(1)}, bf16[8,64,128]{2,1,0:T(8,128)(2,1)}, bf16[256,384]{1,0:T(8,128)(2,1)S(1)}, f32[256,8]{1,0:T(8,128)S(1)}) custom-call(bf16[256,384]{1,0:T(8,128)(2,1)S(1)} %bitcast.30, bf16[256,384]{1,0:T(8,128)(2,1)S(1)} %bitcast.32, bf16[256,384]{1,0:T(8,128)(2,1)S(1)} %bitcast.34, bf16[256,384]{1,0:T(8,128)(2,1)S(1)} %bitcast.24, ...), custom_call_target="tpu_custom_call" | custom-call | flops 1000000000 | bytes 2000000 | tf_op jit(solution)/shard_map/pallas_call | solution.py:206
  9.2 23.3 %all_to_all.25 = bf16[8,32,256]{2,1,0:T(8,128)(2,1)S(1)} all-to-all(bf16[8,32,256]{2,1,0:T(8,128)(2,1)S(1)} %bitcast.29), channel_id=1, replica_groups=mesh['dp'=8,'x'=4,'zh'=2,'zl'=8] {'zl'}, dimensions={0} | all-to-all | bytes 262144 | tf_op jit(solution)/shard_map/all_to_all | solution.py:226
  32.6 10.8 %all-to-all-start = ((bf16[64,8,128]{2,1,0:T(8,128)(2,1)}), bf16[64,8,128]{2,1,0:T(8,128)(2,1)S(1)}, u32[]{:S(2)}, u32[]{:S(2)}) async-start(bf16[64,8,128]{2,1,0:T(8,128)(2,1)} %bitcast.7), calls=%async_computation | async-start | bytes 262144 | tf_op jit(solution)/shard_map/all_to_all | solution.py:226
  43.3 0.0 copy-done.3
  43.4 0.0 copy-done.1
  43.4 1.6 %shard_map.107 = bf16[8,4,96,96]{3,2,1,0:T(8,128)(2,1)} custom-call(bf16[256,384]{1,0:T(8,128)(2,1)S(1)} %bitcast.25, bf16[256,768]{1,0:T(8,128)(2,1)S(1)} %bitcast.23), custom_call_target="tpu_custom_call" | custom-call | flops 150000000 | bytes 2000000 | tf_op jit(solution)/shard_map/pallas_call | solution.py:206
  44.9 12.4 %all-to-all-done = bf16[64,8,128]{2,1,0:T(8,128)(2,1)S(1)} async-done(((bf16[64,8,128]{2,1,0:T(8,128)(2,1)}), bf16[64,8,128]{2,1,0:T(8,128)(2,1)S(1)}, u32[]{:S(2)}, u32[]{:S(2)}) %all-to-all-start) | async-done | bytes 131104 | tf_op jit(solution)/shard_map/all_to_all | solution.py:226
  57.3 10.2 %all-to-all-start.3 = ((bf16[32,96,96]{2,1,0:T(8,128)(2,1)}), bf16[32,96,96]{2,1,0:T(8,128)(2,1)S(1)}, u32[]{:S(2)}, u32[]{:S(2)}) async-start(bf16[32,96,96]{2,1,0:T(8,128)(2,1)} %bitcast.16), calls=%async_computation.3 | async-start | bytes 1572864 | tf_op jit(solution)/shard_map/all_to_all | solution.py:226
  67.5 0.6 shard_map.103.g_ref
  68.1 1.9 %shard_map.104 = bf16[256,256]{1,0:T(8,128)(2,1)} custom-call(s32[1]{0:T(128)} %bitcast.where_ref, bf16[512,128]{1,0:T(8,128)(2,1)S(1)} %bitcast.21, f32[144,256]{1,0:T(8,128)S(1)} %shard_map.103.g_ref), custom_call_target="tpu_custom_call" | custom-call | flops 100000000 | bytes 2000000 | tf_op jit(solution)/shard_map/pallas_call | solution.py:206
  70.0 11.1 %all-to-all-done.3.in_ref = bf16[32,96,96]{2,1,0:T(8,128)(2,1)S(1)} async-done(((bf16[32,96,96]{2,1,0:T(8,128)(2,1)}), bf16[32,96,96]{2,1,0:T(8,128)(2,1)S(1)}, u32[]{:S(2)}, u32[]{:S(2)}) %all-to-all-start.3) | async-done | bytes 589856 | tf_op jit(solution)/shard_map/all_to_all | solution.py:226
  81.1 3.4 %all-to-all-start.2 = ((bf16[8,32,256]{2,1,0:T(8,128)(2,1)}), bf16[8,32,256]{2,1,0:T(8,128)(2,1)S(1)}, u32[]{:S(2)}, u32[]{:S(2)}) async-start(bf16[8,32,256]{2,1,0:T(8,128)(2,1)} %bitcast.11), calls=%async_computation.2 | async-start | bytes 262144 | tf_op jit(solution)/shard_map/all_to_all | solution.py:226
  84.5 0.0 copy-start.10
  84.5 1.0 shard_map.108
  85.6 9.2 %all-to-all-done.2 = bf16[8,32,256]{2,1,0:T(8,128)(2,1)S(1)} async-done(((bf16[8,32,256]{2,1,0:T(8,128)(2,1)}), bf16[8,32,256]{2,1,0:T(8,128)(2,1)S(1)}, u32[]{:S(2)}, u32[]{:S(2)}) %all-to-all-start.2) | async-done | bytes 131104 | tf_op jit(solution)/shard_map/all_to_all | solution.py:226
  94.8 13.6 %all-to-all-start.4 = ((bf16[128,8,128]{2,1,0:T(8,128)(2,1)}), bf16[128,8,128]{2,1,0:T(8,128)(2,1)S(1)}, u32[]{:S(2)}, u32[]{:S(2)}) async-start(bf16[128,8,128]{2,1,0:T(8,128)(2,1)} %bitcast.17), calls=%async_computation.4 | async-start | bytes 524288 | tf_op jit(solution)/shard_map/all_to_all | solution.py:226
  108.4 0.0 copy-done.10
  108.4 0.0 copy-done.6
  108.4 0.0 copy-done.8
  108.4 2.3 %shard_map.105 = (f32[256,384]{1,0:T(8,128)S(1)}, f32[256,384]{1,0:T(8,128)S(1)}, f32[256,384]{1,0:T(8,128)S(1)}) custom-call(bf16[256,384]{1,0:T(8,128)(2,1)S(1)} %bitcast.31, bf16[256,384]{1,0:T(8,128)(2,1)S(1)} %bitcast.33, bf16[256,384]{1,0:T(8,128)(2,1)S(1)} %bitcast.35, bf16[256,384]{1,0:T(8,128)(2,1)S(1)} %get-tuple-element.16.do_ref, ...), custom_call_target="tpu_custom_call" | custom-call | flops 1000000000 | bytes 2000000 | tf_op jit(solution)/shard_map/pallas_call | solution.py:206
  110.7 1.2 shard_map.106
  111.9 19.6 %all-to-all-done.4 = bf16[128,8,128]{2,1,0:T(8,128)(2,1)S(1)} async-done(((bf16[128,8,128]{2,1,0:T(8,128)(2,1)}), bf16[128,8,128]{2,1,0:T(8,128)(2,1)S(1)}, u32[]{:S(2)}, u32[]{:S(2)}) %all-to-all-start.4) | async-done | bytes 262176 | tf_op jit(solution)/shard_map/all_to_all | solution.py:226
  131.5 0.7 shard_map.109
  (8 shorter events, 0.0 us)
Async XLA Ops:
  1.5 1.0 copy-start
  2.5 0.9 copy-start.2
  3.4 1.1 copy-start.4
  4.5 0.9 copy-start.5
  5.4 0.9 copy-start.7
  6.3 0.9 copy-start.9
  7.2 36.1 %copy-start.3 = (bf16[1,256,384]{2,1,0:T(8,128)(2,1)S(1)}, bf16[1,256,384]{2,1,0:T(8,128)(2,1)}, u32[]{:S(2)}) copy-start(bf16[1,256,384]{2,1,0:T(8,128)(2,1)} %param.10) | copy-start | bytes 589828
  9.2 34.1 %copy-start.1 = (bf16[1,256,768]{2,1,0:T(8,128)(2,1)S(1)}, bf16[1,256,768]{2,1,0:T(8,128)(2,1)}, u32[]{:S(2)}) copy-start(bf16[1,256,768]{2,1,0:T(8,128)(2,1)} %param.11) | copy-start | bytes 1179652
  32.6 24.7 %all-to-all-start = ((bf16[64,8,128]{2,1,0:T(8,128)(2,1)}), bf16[64,8,128]{2,1,0:T(8,128)(2,1)S(1)}, u32[]{:S(2)}, u32[]{:S(2)}) async-start(bf16[64,8,128]{2,1,0:T(8,128)(2,1)} %bitcast.7), calls=%async_computation | async-start | bytes 262144 | tf_op jit(solution)/shard_map/all_to_all | solution.py:226
  57.3 23.8 %all-to-all-start.3 = ((bf16[32,96,96]{2,1,0:T(8,128)(2,1)}), bf16[32,96,96]{2,1,0:T(8,128)(2,1)S(1)}, u32[]{:S(2)}, u32[]{:S(2)}) async-start(bf16[32,96,96]{2,1,0:T(8,128)(2,1)} %bitcast.16), calls=%async_computation.3 | async-start | bytes 1572864 | tf_op jit(solution)/shard_map/all_to_all | solution.py:226
  81.1 13.7 %all-to-all-start.2 = ((bf16[8,32,256]{2,1,0:T(8,128)(2,1)}), bf16[8,32,256]{2,1,0:T(8,128)(2,1)S(1)}, u32[]{:S(2)}, u32[]{:S(2)}) async-start(bf16[8,32,256]{2,1,0:T(8,128)(2,1)} %bitcast.11), calls=%async_computation.2 | async-start | bytes 262144 | tf_op jit(solution)/shard_map/all_to_all | solution.py:226
  84.5 23.9 %copy-start.10 = (bf16[1,256,384]{2,1,0:T(8,128)(2,1)S(1)}, bf16[1,256,384]{2,1,0:T(8,128)(2,1)}, u32[]{:S(2)}) copy-start(bf16[1,256,384]{2,1,0:T(8,128)(2,1)} %param.9) | copy-start | bytes 589828
  94.8 13.6 %copy-start.6 = (bf16[1,256,384]{2,1,0:T(8,128)(2,1)S(1)}, bf16[1,256,384]{2,1,0:T(8,128)(2,1)}, u32[]{:S(2)}) copy-start(bf16[1,256,384]{2,1,0:T(8,128)(2,1)} %param.7) | copy-start | bytes 589828
  94.8 13.6 %copy-start.8 = (bf16[1,256,384]{2,1,0:T(8,128)(2,1)S(1)}, bf16[1,256,384]{2,1,0:T(8,128)(2,1)}, u32[]{:S(2)}) copy-start(bf16[1,256,384]{2,1,0:T(8,128)(2,1)} %param.8) | copy-start | bytes 589828
  94.8 36.7 %all-to-all-start.4 = ((bf16[128,8,128]{2,1,0:T(8,128)(2,1)}), bf16[128,8,128]{2,1,0:T(8,128)(2,1)S(1)}, u32[]{:S(2)}, u32[]{:S(2)}) async-start(bf16[128,8,128]{2,1,0:T(8,128)(2,1)} %bitcast.17), calls=%async_computation.4 | async-start | bytes 524288 | tf_op jit(solution)/shard_map/all_to_all | solution.py:226

commit v2 on v1

v2 whole, which is shorter than its diff:
```python
import functools

import jax
import jax.numpy as jnp
from jax import lax
from jax.experimental import pallas as pl
from jax.experimental.pallas import tpu as pltpu
from jax.sharding import PartitionSpec as P

HEADS = 8
HD = 48
GROUP = 8
BF = jnp.bfloat16
F32 = jnp.float32


def iota(shape, dim):
    return lax.broadcasted_iota(jnp.int32, shape, dim)


def dot(a, b, ca, cb):
    return lax.dot_general(a, b, (((ca,), (cb,)), ((), ())), preferred_element_type=F32)


def split(x):
    hi = x.astype(BF)
    return hi, (x - hi.astype(F32)).astype(BF)


def eye(n):
    return (iota((n, n), 0) == iota((n, n), 1)).astype(BF)


def packed_token(p):
    return 64 * (p & 3) + 8 * ((p >> 2) & 7) + (p >> 5)


def spread(part, shape, lane_dim, channel_dim):
    return (iota(shape, lane_dim) == HD * part + lax.rem(iota(shape, channel_dim), HD)).astype(BF)


def own_head(rows, width):
    return lax.div(iota((rows, width), 1), HD) == (iota((rows, width), 0) & (GROUP - 1))


def one_hot(rows, cols, row_of):
    return (iota((rows, cols), 0) == row_of(iota((rows, cols), 1))).astype(BF)


def front_kernel(*refs):
    hbm, (pay_ref, out_ref, do_ref, stat_ref), vmem, sems = refs[:7], refs[7:11], refs[11:18], refs[18]
    copies = [pltpu.make_async_copy(a, b, sems.at[n]) for n, (a, b) in enumerate(zip(hbm, vmem))]
    for copy in copies:
        copy.start()
    dy_ref, w_ref, o_ref, lse_ref, q_ref, k_ref, v_ref = vmem
    for copy in copies[:4]:
        copy.wait()
    rows, width = o_ref.shape
    cols = dy_ref.shape[1]
    out, dy = o_ref[...], dy_ref[...]
    d_out = dot(dy, w_ref[...], 1, 1).astype(BF)
    do_ref[...] = d_out
    hi, lo = split(d_out.astype(F32) * out.astype(F32))
    heads = (lax.div(iota((width, 128), 0), HD) == iota((width, 128), 1)).astype(BF)
    delta = (dot(hi, heads, 1, 0) + dot(lo, heads, 1, 0))[:, :HEADS]
    lse = jnp.transpose(lse_ref[...])
    stat_ref[...] = jnp.concatenate([delta, lse], axis=1)
    parts = out_ref.shape[0]
    each = width // parts
    grad = dot(out, dy, 0, 0)
    for x in range(parts):
        for t in range(cols // 128):
            out_ref[x, each * t : each * (t + 1)] = grad[each * x : each * (x + 1), 128 * t : 128 * (t + 1)].astype(BF)
    for copy in copies[4:]:
        copy.wait()
    mine = own_head(rows, width)
    pay = jnp.zeros((rows, 256), F32)
    for part, x in enumerate((q_ref[...], k_ref[...], v_ref[...], d_out)):
        pay += dot(jnp.where(mine, x, jnp.zeros_like(x)), spread(part, (width, 256), 1, 0), 1, 0)
    pick = iota((rows, HEADS), 1) == (iota((rows, HEADS), 0) & (GROUP - 1))
    lane = iota((rows, 256), 1)
    for base, x in ((4 * HD, lse), (4 * HD + 3, delta)):
        own = jnp.sum(jnp.where(pick, x, 0.0), axis=1, keepdims=True)
        for n in range(3):
            piece = own.astype(BF).astype(F32)
            pay += jnp.where(lane == base + n, piece, 0.0)
            own = own - piece
    pay = pay.astype(BF)
    perm = (iota((rows, rows), 1) == packed_token(iota((rows, rows), 0))).astype(BF)
    pay_ref[...] = dot(perm, pay, 1, 0).astype(BF)
    at, token = iota((8 * HEADS, rows), 0), iota((8 * HEADS, rows), 1)
    here = token == 64 * (at & 3) + ((at >> 2) & 7)
    first = (here & (at < 4 * HEADS)).astype(BF)
    second = (here & (at >= 4 * HEADS)).astype(BF)
    top = (dot(first, pay[:, :128], 1, 0) + dot(second, pay[:, 128:], 1, 0)).astype(BF)
    for x in range(parts):
        out_ref[x, width * cols // parts // 128 :] = top


def mid_kernel(in_ref, pay_ref, out_ref):
    parts = in_ref.shape[0]
    ring = out_ref.shape[0]
    count = in_ref.shape[1] - 8 * HEADS
    grad = jnp.sum(in_ref[:, :count].astype(F32), axis=0).astype(BF)
    room = out_ref.shape[1] - 96
    tiles = 6
    each = count // tiles
    few = each // ring
    top = jnp.concatenate([in_ref[x, count:] for x in range(parts)], axis=0)
    n = top.shape[0]
    to, frm = iota((n, n), 0), iota((n, n), 1)
    source = 64 * ((to >> 2) & 3) + 32 * ((to >> 4) & 1) + 4 * (to >> 5) + (to & 3)
    top = dot((frm == source).astype(BF), top, 1, 0).astype(BF)
    big, row = iota((room * ring, count), 0), iota((room * ring, count), 1)
    z, at = lax.div(big[:, :1], room), lax.rem(big[:, :1], room)
    source = jnp.where(at < tiles * few, each * lax.div(at, few) + few * z + lax.rem(at, few), -1)
    grad = dot((row == source).astype(BF), grad, 1, 0).astype(BF)
    for z in range(ring):
        r = z & (GROUP - 1)
        out_ref[z, :32] = pay_ref[32 * r : 32 * (r + 1), :128]
        out_ref[z, 32:64] = pay_ref[32 * r : 32 * (r + 1), 128:]
        out_ref[z, 64:96] = top[32 * r : 32 * (r + 1)]
        out_ref[z, 96:] = grad[room * z : room * (z + 1)]


def weight_kernel(in_ref, _, out_ref):
    each, cols = out_ref.shape
    total = jnp.sum(in_ref[:, 96:].astype(F32), axis=0)
    out_ref[...] = jnp.concatenate([total[each * t : each * (t + 1)] for t in range(cols // 128)], axis=1)


def window(h):
    lo = HD * h // 128 * 128
    hi = -(-HD * (h + 1) // 128) * 128
    return lo, hi


def padded(x_t, before, total):
    parts = []
    if before:
        parts.append(jnp.zeros((before, x_t.shape[1]), x_t.dtype))
    parts.append(x_t)
    after = total - before - x_t.shape[0]
    if after:
        parts.append(jnp.zeros((after, x_t.shape[1]), x_t.dtype))
    return jnp.concatenate(parts, axis=0)


def set_grads(q_win, do_win, k_pad, v_pad, q_t, k_t, do_t, lse, delta):
    scale = float(HD) ** -0.5
    probs = jnp.exp(dot(q_win, k_pad, 1, 0) * scale - lse)
    d_scores = (probs * (dot(do_win, v_pad, 1, 0) - delta)).astype(BF)
    return (
        dot(k_t, d_scores, 1, 1) * scale,
        dot(q_t, d_scores, 1, 0) * scale,
        dot(do_t, probs.astype(BF), 1, 0),
    )


def local_kernel(q_ref, k_ref, v_ref, do_ref, stat_ref, dq_ref, dk_ref, dv_ref, t_ref):
    q_t, k_t, v_t, do_t = (jnp.transpose(r[...]) for r in (q_ref, k_ref, v_ref, do_ref))
    for h in range(HEADS):
        own = slice(HD * h, HD * (h + 1))
        lo, hi = window(h)
        grads = set_grads(
            q_ref[:, lo:hi],
            do_ref[:, lo:hi],
            padded(k_t[own], HD * h - lo, hi - lo),
            padded(v_t[own], HD * h - lo, hi - lo),
            q_t[own],
            k_t[own],
            do_t[own],
            stat_ref[:, HEADS + h : HEADS + h + 1],
            stat_ref[:, h : h + 1],
        )
        for n, g in enumerate(grads):
            t_ref[n, own, :] = g
    for n, out in enumerate((dq_ref, dk_ref, dv_ref)):
        out[...] = jnp.transpose(t_ref[n])


def packed_grads(x):
    x_t = dot(eye(256), x, 1, 1).astype(BF)
    tail = x[:, 128:].astype(F32)

    def column(n):
        at = 4 * HD + 3 * n - 128
        return tail[:, at : at + 1] + tail[:, at + 1 : at + 2] + tail[:, at + 2 : at + 3]

    q_t, k_t, v_t, do_t = (x_t[HD * n : HD * (n + 1)] for n in range(4))
    grads = set_grads(
        x[:, :128], x[:, 128:], padded(k_t, 0, 128), padded(v_t, 3 * HD - 128, 128), q_t, k_t, do_t, column(0), column(1)
    )
    return jnp.concatenate(grads, axis=0)


def joined(in_ref, where, first, count):
    lo = in_ref[where, first : first + count].reshape(256, 128)
    hi = in_ref[where, first + count : first + 2 * count].reshape(256, 128)
    return jnp.concatenate([lo, hi], axis=1)


def group_kernel(where_ref, in_ref, _, g_ref):
    g_ref[...] = packed_grads(joined(in_ref, pl.ds(GROUP * where_ref[1], GROUP), 0, 32))


def far_kernel(where_ref, in_ref, g_ref, back_ref):
    far = packed_grads(joined(in_ref, slice(None), 64, 16))
    row, col = iota((256, 256), 0), iota((256, 256), 1)
    here = ((row >> 7) == where_ref[1]) & (((row >> 2) & 3) == where_ref[0])
    sel = (here & (col == 32 * ((row >> 4) & 7) + (row & 3))).astype(BF)
    hi, lo = split(far)
    total = (g_ref[...] + dot(hi, sel, 1, 0) + dot(lo, sel, 1, 0)).astype(BF)
    total = jnp.concatenate([total, jnp.zeros((256 - total.shape[0], 256), BF)], axis=0)
    back_ref[...] = dot(eye(256), total, 1, 1).astype(BF)


def final_kernel(z_ref, dq_ref, dk_ref, dv_ref, oq_ref, ok_ref, ov_ref):
    rows, width = dq_ref.shape
    perm_t = (iota((rows, rows), 0) == packed_token(iota((rows, rows), 1))).astype(BF)
    y = dot(perm_t, z_ref[...], 1, 0).astype(BF)
    mine = own_head(rows, width)
    for n, (near, out) in enumerate(((dq_ref, oq_ref), (dk_ref, ok_ref), (dv_ref, ov_ref))):
        far = dot(y, spread(n, (256, width), 0, 1), 1, 0)
        out[...] = (near[...] + jnp.where(mine, far, 0.0)).astype(BF)


def call(kernel, outs, *args, scratch=(), smem=0, hbm=False, flops=0):
    vmem = pl.BlockSpec(memory_space=pltpu.VMEM)
    held = pl.BlockSpec(memory_space=pltpu.HBM) if hbm else vmem
    return pl.pallas_call(
        kernel,
        out_shape=outs,
        in_specs=[pl.BlockSpec(memory_space=pltpu.SMEM)] * smem + [held] * (len(args) - smem),
        out_specs=jax.tree.map(lambda _: vmem, outs),
        scratch_shapes=list(scratch),
        compiler_params=pltpu.CompilerParams(vmem_limit_bytes=32 * 1024 * 1024),
        cost_estimate=pl.CostEstimate(flops=flops, bytes_accessed=2_000_000, transcendentals=0),
    )(*args)


def on_device(queries, keys, values, outputs, d_final, stats, w_out):
    q, k, v, o, dy, lse = (x[0] for x in (queries, keys, values, outputs, d_final, stats))
    rows, width = q.shape
    cols = dy.shape[1]
    blocks, ring = lax.axis_size("x"), lax.axis_size(("zh", "zl"))
    shape = jax.ShapeDtypeStruct

    def exchange(x, axes):
        return lax.all_to_all(x, axes, 0, 0, tiled=True)

    ins = (dy, w_out, o, lse.T, q, k, v)
    pay, out, d_out, stat = call(
        front_kernel,
        (
            shape((rows, 256), BF),
            shape((blocks, width * cols // blocks // 128 + 8 * HEADS, 128), BF),
            shape((rows, width), BF),
            shape((rows, 2 * HEADS), F32),
        ),
        *ins,
        hbm=True,
        scratch=[pltpu.VMEM(x.shape, x.dtype) for x in ins] + [pltpu.SemaphoreType.DMA((len(ins),))],
        flops=1_000_000_000,
    )
    over_x = exchange(out, "x")
    out = call(mid_kernel, shape((ring, 144, 128), BF), over_x, pay, flops=100_000_000)
    over_z = exchange(out, ("zh", "zl"))
    near = call(
        local_kernel,
        (shape((rows, width), F32),) * 3,
        q, k, v, d_out, stat,
        scratch=[pltpu.VMEM((3, width, rows), F32)],
        flops=1_000_000_000,
    )
    where = jnp.stack([lax.axis_index("x"), lax.axis_index("zh")]).astype(jnp.int32)
    group = call(group_kernel, shape((3 * HD, 256), F32), where, over_z, near[0], smem=1, flops=100_000_000)
    back = call(far_kernel, shape((256, 256), BF), where, over_z, group, smem=1, flops=100_000_000)
    z = exchange(back.reshape(GROUP, rows // GROUP, 256), "zl").reshape(256, 256)
    grad = call(weight_kernel, shape((width // (blocks * ring), cols), F32), over_z, near[0], flops=1_000_000)
    members = lax.axis_size("dp")
    for bit in range(members.bit_length() - 1):
        grad = grad + lax.ppermute(grad, "dp", [(i, i ^ (1 << bit)) for i in range(members)])
    d_q, d_k, d_v = call(final_kernel, (shape((rows, width), BF),) * 3, z, *near, flops=300_000_000)
    return d_q[None], d_k[None], d_v[None], grad


def solution(mesh):
    dp, seq = mesh.devices.shape
    fine = jax.sharding.Mesh(
        mesh.devices.reshape(dp, seq // 16, 16 // GROUP, GROUP), ("dp", "x", "zh", "zl")
    )
    seq_axes = ("x", "zh", "zl")
    placed = P("dp", seq_axes, None)
    return jax.shard_map(
        on_device,
        mesh=fine,
        in_specs=(placed,) * 6 + (P(),),
        out_specs=(placed,) * 3 + (P(seq_axes, None),),
        check_vma=False,
    )
```

time: 133 us -> 101 us (0.76)
  waiting for transfers between devices: 52.3 us -> 25.7 us
  blocking collectives: 23.3 us -> 12.3 us
  starting transfers between devices: 37.9 us -> 42 us
    all_to_all x4 -> x2, waiting for transfers between devices: 52.3 us -> 21.9 us  [exchange(): return lax.all_to_all(x, axes, 0, 0, tiled=True)]
    ppermute x0 -> x3, starting transfers between devices: none -> 12 us  [on_device(): lax.ppermute(grad, 'dp', [(i, i ^ 1 << bit) for i in range(members)])]
    all_to_all x1, blocking collectives: 23.3 us -> 12.3 us  [exchange(): return lax.all_to_all(x, axes, 0, 0, tiled=True)]
    all_to_all x4 -> x2, starting transfers between devices: 37.9 us -> 30 us  [exchange(): return lax.all_to_all(x, axes, 0, 0, tiled=True)]
    ppermute x0 -> x3, waiting for transfers between devices: none -> 3.74 us  [on_device(): lax.ppermute(grad, 'dp', [(i, i ^ 1 << bit) for i in range(members)])]
    pallas_call x8 -> x7, Pallas kernels: 11.3 us -> 11.7 us  [call(): pl.pallas_call(kernel, out_shape=outs, in_specs=[pl.BlockSpec(memory_spac...]
    unnamed x23 -> x20, local copies, waits for them, and re-layouts: 6.6 us -> 6.47 us
  transfers between devices with their start and end apart: 4 -> 5, of which waited for: 4 -> 4; matrix products, arithmetic and copies ran while one was open for 0% -> 1% of each run, Pallas kernels for 7% -> 2%
where the time goes in v2:
time: 101 us; the launch traced here: 99.5 us
  starting transfers between devices  42 us (42%)
  waiting for transfers between devices  25.7 us (25%)
  blocking collectives  12.3 us (12%)
  Pallas kernels  11.7 us (12%)
  local copies, waits for them, and re-layouts  6.47 us (6%)
    all_to_all x2, starting transfers between devices, exchange(): return lax.all_to_all(x, axes, 0, 0, tiled=True)  30 us
    all_to_all x2, waiting for transfers between devices, exchange(): return lax.all_to_all(x, axes, 0, 0, tiled=True)  21.9 us
    all_to_all x1, blocking collectives, exchange(): return lax.all_to_all(x, axes, 0, 0, tiled=True)  12.3 us
    ppermute x3, starting transfers between devices, on_device(): lax.ppermute(grad, 'dp', [(i, i ^ 1 << bit) for i in range(members)])  12 us
    pallas_call x7, Pallas kernels, call(): pl.pallas_call(kernel, out_shape=outs, in_specs=[pl.BlockSpec(memory_spac...  11.7 us
    unnamed x20, local copies, waits for them, and re-layouts  6.47 us
    ppermute x3, waiting for transfers between devices, on_device(): lax.ppermute(grad, 'dp', [(i, i ^ 1 << bit) for i in range(members)])  3.74 us
  transfers between devices with their start and end apart: 5, of which 4 were waited for; matrix products, arithmetic and copies ran while one was open for 1% of the time, Pallas kernels for 2%

profile of v2, /device:TPU:1, one launch (start us, length us, event | category | flops | bytes accessed | tf_op | source)
XLA Modules:
  0.0 99.5 jit_solution(3454962337683141845)
XLA Ops:
  0.6 0.0 copy-start.9
  0.6 0.7 copy-done.9
  1.3 0.0 copy-start
  1.3 1.1 %copy-done = bf16[384,768]{1,0:T(8,128)(2,1)S(1)} copy-done((bf16[384,768]{1,0:T(8,128)(2,1)S(1)}, bf16[384,768]{1,0:T(8,128)(2,1)}, u32[]{:S(2)}) %copy-start) | copy-done | bytes 589848
  2.4 1.0 copy-done.1
  3.4 0.0 copy-start.2
  3.4 0.9 copy-done.2
  4.3 0.9 copy-done.3
  5.2 0.9 copy-done.5
  6.2 0.9 copy-done.7
  7.1 3.2 %shard_map.102 = (bf16[256,256]{1,0:T(8,128)(2,1)S(1)}, bf16[4,640,128]{2,1,0:T(8,128)(2,1)S(1)}, bf16[256,384]{1,0:T(8,128)(2,1)S(1)}, f32[256,16]{1,0:T(8,128)S(1)}) custom-call(bf16[256,768]{1,0:T(8,128)(2,1)S(1)} %bitcast.16, bf16[384,768]{1,0:T(8,128)(2,1)S(1)} %copy-done, bf16[256,384]{1,0:T(8,128)(2,1)S(1)} %bitcast.17, f32[8,256]{1,0:T(8,128)S(1)} %bitcast.24, ...), custom_call_target="tpu_custom_call" | custom-call | flops 1000000000 | bytes 2000000 | tf_op jit(solution)/shard_map/pallas_call | solution.py:231
  10.3 12.3 %all_to_all.15.in_ref = bf16[4,640,128]{2,1,0:T(8,128)(2,1)S(1)} all-to-all(bf16[4,640,128]{2,1,0:T(8,128)(2,1)S(1)} %get-tuple-element.14), channel_id=1, replica_groups=mesh['dp'=8,'x'=4,'zh'=2,'zl'=8] {'x'}, dimensions={0} | all-to-all | bytes 1310720 | tf_op jit(solution)/shard_map/all_to_all | solution.py:250
  22.6 1.6 %shard_map.103 = bf16[16,144,128]{2,1,0:T(8,128)(2,1)} custom-call(bf16[4,640,128]{2,1,0:T(8,128)(2,1)S(1)} %all_to_all.15.in_ref, bf16[256,256]{1,0:T(8,128)(2,1)S(1)} %get-tuple-element.15.pay_ref), custom_call_target="tpu_custom_call" | custom-call | flops 100000000 | bytes 2000000 | tf_op jit(solution)/shard_map/pallas_call | solution.py:231
  24.2 17.4 %all-to-all-start.1 = ((bf16[16,144,128]{2,1,0:T(8,128)(2,1)}), bf16[16,144,128]{2,1,0:T(8,128)(2,1)S(1)}, u32[]{:S(2)}, u32[]{:S(2)}) async-start(bf16[16,144,128]{2,1,0:T(8,128)(2,1)} %shard_map.103), calls=%async_computation.1 | async-start | bytes 1179648 | tf_op jit(solution)/shard_map/all_to_all | solution.py:250
  41.6 0.0 copy-done.4
  41.6 0.0 copy-done.6
  41.6 0.0 copy-done.8
  41.6 2.3 %shard_map.104 = (f32[256,384]{1,0:T(8,128)S(1)}, f32[256,384]{1,0:T(8,128)S(1)}, f32[256,384]{1,0:T(8,128)S(1)}) custom-call(bf16[256,384]{1,0:T(8,128)(2,1)S(1)} %bitcast.19, bf16[256,384]{1,0:T(8,128)(2,1)S(1)} %bitcast.21, bf16[256,384]{1,0:T(8,128)(2,1)S(1)} %bitcast.23, bf16[256,384]{1,0:T(8,128)(2,1)S(1)} %get-tuple-element.16.do_ref, ...), custom_call_target="tpu_custom_call" | custom-call | flops 1000000000 | bytes 2000000 | tf_op jit(solution)/shard_map/pallas_call | solution.py:231
  43.9 0.1 pad_add_fusion.where_ref
  44.0 21.9 %all-to-all-done.1.in_ref = bf16[16,144,128]{2,1,0:T(8,128)(2,1)S(1)} async-done(((bf16[16,144,128]{2,1,0:T(8,128)(2,1)}), bf16[16,144,128]{2,1,0:T(8,128)(2,1)S(1)}, u32[]{:S(2)}, u32[]{:S(2)}) %all-to-all-start.1) | async-done | bytes 589856 | tf_op jit(solution)/shard_map/all_to_all | solution.py:250
  65.9 1.2 %shard_map.105.g_ref = f32[144,256]{1,0:T(8,128)S(1)} custom-call(s32[2]{0:T(128)S(1)} %pad_add_fusion.where_ref, bf16[16,144,128]{2,1,0:T(8,128)(2,1)S(1)} %all-to-all-done.1.in_ref, f32[256,384]{1,0:T(8,128)S(1)} %get-tuple-element.18._.dq_ref), custom_call_target="tpu_custom_call" | custom-call | flops 100000000 | bytes 2000000 | tf_op jit(solution)/shard_map/pallas_call | solution.py:231
  67.1 2.2 %shard_map.106 = bf16[256,256]{1,0:T(8,128)(2,1)} custom-call(s32[2]{0:T(128)S(1)} %pad_add_fusion.where_ref, bf16[16,144,128]{2,1,0:T(8,128)(2,1)S(1)} %all-to-all-done.1.in_ref, f32[144,256]{1,0:T(8,128)S(1)} %shard_map.105.g_ref), custom_call_target="tpu_custom_call" | custom-call | flops 100000000 | bytes 2000000 | tf_op jit(solution)/shard_map/pallas_call | solution.py:231
  69.3 12.6 %all-to-all-start.2 = ((bf16[8,32,256]{2,1,0:T(8,128)(2,1)}), bf16[8,32,256]{2,1,0:T(8,128)(2,1)S(1)}, u32[]{:S(2)}, u32[]{:S(2)}) async-start(bf16[8,32,256]{2,1,0:T(8,128)(2,1)} %bitcast.9), calls=%async_computation.2 | async-start | bytes 262144 | tf_op jit(solution)/shard_map/all_to_all | solution.py:250
  81.9 4.0 %collective-permute-start = (f32[6,768]{1,0:T(8,128)S(1)}, f32[6,768]{1,0:T(8,128)S(1)}, u32[]{:S(2)}, u32[]{:S(2)}) collective-permute-start(f32[6,768]{1,0:T(8,128)S(1)} %shard_map.108), channel_id=1, source_target_pairs={{0,64},{64,0},{128,192},{192,128},{256,320},{320,256},{384,448},{4... | collective-permute-start | bytes 55304 | tf_op jit(solution)/shard_map/ppermute | solution.py:283
  85.9 0.8 collective-permute-done
  86.8 3.2 %collective-permute-start.1 = (f32[6,768]{1,0:T(8,128)S(1)}, f32[6,768]{1,0:T(8,128)S(1)}, u32[]{:S(2)}, u32[]{:S(2)}) collective-permute-start(f32[6,768]{1,0:T(8,128)S(1)} %add.9), channel_id=1, source_target_pairs={{0,128},{64,192},{128,0},{192,64},{256,384},{320,448},{384,256},{4... | collective-permute-start | bytes 55304 | tf_op jit(solution)/shard_map/ppermute | solution.py:283
  89.9 1.7 %collective-permute-done.1 = f32[6,768]{1,0:T(8,128)S(1)} collective-permute-done((f32[6,768]{1,0:T(8,128)S(1)}, f32[6,768]{1,0:T(8,128)S(1)}, u32[]{:S(2)}, u32[]{:S(2)}) %collective-permute-start.1) | collective-permute-done | bytes 18464 | tf_op jit(solution)/shard_map/ppermute | solution.py:283
  91.6 4.8 %collective-permute-start.2 = (f32[6,768]{1,0:T(8,128)S(1)}, f32[6,768]{1,0:T(8,128)S(1)}, u32[]{:S(2)}, u32[]{:S(2)}) collective-permute-start(f32[6,768]{1,0:T(8,128)S(1)} %add.10), channel_id=1, source_target_pairs={{0,256},{64,320},{128,384},{192,448},{256,0},{320,64},{384,128},{4... | collective-permute-start | bytes 55304 | tf_op jit(solution)/shard_map/ppermute | solution.py:283
  96.4 1.3 %collective-permute-done.2 = f32[6,768]{1,0:T(8,128)S(1)} collective-permute-done((f32[6,768]{1,0:T(8,128)S(1)}, f32[6,768]{1,0:T(8,128)S(1)}, u32[]{:S(2)}, u32[]{:S(2)}) %collective-permute-start.2) | collective-permute-done | bytes 18464 | tf_op jit(solution)/shard_map/ppermute | solution.py:283
  97.7 0.6 add.11
  98.3 0.0 all-to-all-done.2
  98.3 1.2 %shard_map.107 = (bf16[256,384]{1,0:T(8,128)(2,1)}, bf16[256,384]{1,0:T(8,128)(2,1)}, bf16[256,384]{1,0:T(8,128)(2,1)}) custom-call(bf16[256,256]{1,0:T(8,128)(2,1)S(1)} %bitcast.15, f32[256,384]{1,0:T(8,128)S(1)} %get-tuple-element.18._.dq_ref, f32[256,384]{1,0:T(8,128)S(1)} %get-tuple-element.19.dk_ref, f32[256,384]{1,0:T(8,128)S(1)} %get-tuple-element.20.dv_ref), custom_call_target="tpu_custom_call" | custom-call | flops 300000000 | bytes 2000000 | tf_op jit(solution)/shard_map/pallas_call | solution.py:231
  (10 shorter events, 0.1 us)
Async XLA Ops:
  0.6 0.7 copy-start.9
  1.3 1.1 %copy-start = (bf16[384,768]{1,0:T(8,128)(2,1)S(1)}, bf16[384,768]{1,0:T(8,128)(2,1)}, u32[]{:S(2)}) copy-start(bf16[384,768]{1,0:T(8,128)(2,1)} %refs_1_.1) | copy-start | bytes 1769476
  2.4 1.0 %copy-start.1 = (bf16[1,256,768]{2,1,0:T(8,128)(2,1)S(1)}, bf16[1,256,768]{2,1,0:T(8,128)(2,1)}, u32[]{:S(2)}) copy-start(bf16[1,256,768]{2,1,0:T(8,128)(2,1)} %param.11) | copy-start | bytes 1179652
  3.4 0.9 copy-start.2
  4.3 0.9 copy-start.3
  5.2 0.9 copy-start.5
  6.2 0.9 copy-start.7
  24.2 17.4 %copy-start.4 = (bf16[1,256,384]{2,1,0:T(8,128)(2,1)S(1)}, bf16[1,256,384]{2,1,0:T(8,128)(2,1)}, u32[]{:S(2)}) copy-start(bf16[1,256,384]{2,1,0:T(8,128)(2,1)} %param.7) | copy-start | bytes 589828
  24.2 17.4 %copy-start.6 = (bf16[1,256,384]{2,1,0:T(8,128)(2,1)S(1)}, bf16[1,256,384]{2,1,0:T(8,128)(2,1)}, u32[]{:S(2)}) copy-start(bf16[1,256,384]{2,1,0:T(8,128)(2,1)} %param.8) | copy-start | bytes 589828
  24.2 17.4 %copy-start.8 = (bf16[1,256,384]{2,1,0:T(8,128)(2,1)S(1)}, bf16[1,256,384]{2,1,0:T(8,128)(2,1)}, u32[]{:S(2)}) copy-start(bf16[1,256,384]{2,1,0:T(8,128)(2,1)} %param.9) | copy-start | bytes 589828
  24.2 41.8 %all-to-all-start.1 = ((bf16[16,144,128]{2,1,0:T(8,128)(2,1)}), bf16[16,144,128]{2,1,0:T(8,128)(2,1)S(1)}, u32[]{:S(2)}, u32[]{:S(2)}) async-start(bf16[16,144,128]{2,1,0:T(8,128)(2,1)} %shard_map.103), calls=%async_computation.1 | async-start | bytes 1179648 | tf_op jit(solution)/shard_map/all_to_all | solution.py:250
  69.3 29.0 %all-to-all-start.2 = ((bf16[8,32,256]{2,1,0:T(8,128)(2,1)}), bf16[8,32,256]{2,1,0:T(8,128)(2,1)S(1)}, u32[]{:S(2)}, u32[]{:S(2)}) async-start(bf16[8,32,256]{2,1,0:T(8,128)(2,1)} %bitcast.9), calls=%async_computation.2 | async-start | bytes 262144 | tf_op jit(solution)/shard_map/all_to_all | solution.py:250
  81.9 4.8 %collective-permute-start = (f32[6,768]{1,0:T(8,128)S(1)}, f32[6,768]{1,0:T(8,128)S(1)}, u32[]{:S(2)}, u32[]{:S(2)}) collective-permute-start(f32[6,768]{1,0:T(8,128)S(1)} %shard_map.108), channel_id=1, source_target_pairs={{0,64},{64,0},{128,192},{192,128},{256,320},{320,256},{384,448},{4... | collective-permute-start | bytes 55304 | tf_op jit(solution)/shard_map/ppermute | solution.py:283
  86.8 4.9 %collective-permute-start.1 = (f32[6,768]{1,0:T(8,128)S(1)}, f32[6,768]{1,0:T(8,128)S(1)}, u32[]{:S(2)}, u32[]{:S(2)}) collective-permute-start(f32[6,768]{1,0:T(8,128)S(1)} %add.9), channel_id=1, source_target_pairs={{0,128},{64,192},{128,0},{192,64},{256,384},{320,448},{384,256},{4... | collective-permute-start | bytes 55304 | tf_op jit(solution)/shard_map/ppermute | solution.py:283
  91.6 6.1 %collective-permute-start.2 = (f32[6,768]{1,0:T(8,128)S(1)}, f32[6,768]{1,0:T(8,128)S(1)}, u32[]{:S(2)}, u32[]{:S(2)}) collective-permute-start(f32[6,768]{1,0:T(8,128)S(1)} %add.10), channel_id=1, source_target_pairs={{0,256},{64,320},{128,384},{192,448},{256,0},{320,64},{384,128},{4... | collective-permute-start | bytes 55304 | tf_op jit(solution)/shard_map/ppermute | solution.py:283

commit v3 on v2

--- a/solution.py
+++ b/solution.py
@@ -10,6 +10,8 @@
 HEADS = 8
 HD = 48
 GROUP = 8
+CORES = 2
+ROOM = 60
 BF = jnp.bfloat16
 F32 = jnp.float32
 
@@ -66,11 +68,13 @@
     lse = jnp.transpose(lse_ref[...])
     stat_ref[...] = jnp.concatenate([delta, lse], axis=1)
     parts = out_ref.shape[0]
-    each = width // parts
+    each, half = width * CORES // parts, cols // CORES
     grad = dot(out, dy, 0, 0)
-    for x in range(parts):
-        for t in range(cols // 128):
-            out_ref[x, each * t : each * (t + 1)] = grad[each * x : each * (x + 1), 128 * t : 128 * (t + 1)].astype(BF)
+    for n in range(parts):
+        x, c = divmod(n, CORES)
+        for t in range(half // 128):
+            tile = grad[each * x : each * (x + 1), half * c + 128 * t : half * c + 128 * (t + 1)]
+            out_ref[n, each * t : each * (t + 1)] = tile.astype(BF)
     for copy in copies[4:]:
         copy.wait()
     mine = own_head(rows, width)
@@ -93,40 +97,64 @@
     first = (here & (at < 4 * HEADS)).astype(BF)
     second = (here & (at >= 4 * HEADS)).astype(BF)
     top = (dot(first, pay[:, :128], 1, 0) + dot(second, pay[:, 128:], 1, 0)).astype(BF)
-    for x in range(parts):
-        out_ref[x, width * cols // parts // 128 :] = top
-
-
-def mid_kernel(in_ref, pay_ref, out_ref):
-    parts = in_ref.shape[0]
+    for n in range(parts):
+        out_ref[n, width * cols // parts // 128 :] = top
+
+
+def mid_kernel(where_ref, in_ref, pay_ref, out_ref):
     ring = out_ref.shape[0]
     count = in_ref.shape[1] - 8 * HEADS
-    grad = jnp.sum(in_ref[:, :count].astype(F32), axis=0).astype(BF)
-    room = out_ref.shape[1] - 96
-    tiles = 6
-    each = count // tiles
+    sums = jnp.sum(in_ref[:, :count].astype(F32), axis=0)
+    each = count // 3
     few = each // ring
-    top = jnp.concatenate([in_ref[x, count:] for x in range(parts)], axis=0)
+    wide = jnp.concatenate([sums[each * t : each * (t + 1)] for t in range(3)], axis=1)
+    chunks = jnp.concatenate([wide[:, HD * u : HD * (u + 1)] for u in range(8)], axis=0).astype(BF)
+    n = chunks.shape[0]
+    to = iota((n, 1), 0)
+    third, z, p = to >> 8, (to >> 4) & 15, to & 15
+    q = 16 * third + p
+    source = each * (q & 7) + few * z + (q >> 3)
+    grad = dot((iota((n, n), 1) == source).astype(BF), chunks, 1, 0)
+    grad = jnp.concatenate([grad[256 * t : 256 * (t + 1)] for t in range(3)], axis=1)
+    top = jnp.concatenate([in_ref[CORES * x + where_ref[2], count:] for x in range(4)], axis=0)
     n = top.shape[0]
-    to, frm = iota((n, n), 0), iota((n, n), 1)
+    to = iota((n, 1), 0)
     source = 64 * ((to >> 2) & 3) + 32 * ((to >> 4) & 1) + 4 * (to >> 5) + (to & 3)
-    top = dot((frm == source).astype(BF), top, 1, 0).astype(BF)
-    big, row = iota((room * ring, count), 0), iota((room * ring, count), 1)
-    z, at = lax.div(big[:, :1], room), lax.rem(big[:, :1], room)
-    source = jnp.where(at < tiles * few, each * lax.div(at, few) + few * z + lax.rem(at, few), -1)
-    grad = dot((row == source).astype(BF), grad, 1, 0).astype(BF)
+    top = dot((iota((n, n), 1) == source).astype(BF), top, 1, 0)
     for z in range(ring):
         r = z & (GROUP - 1)
         out_ref[z, :32] = pay_ref[32 * r : 32 * (r + 1), :128]
-        out_ref[z, 32:64] = pay_ref[32 * r : 32 * (r + 1), 128:]
-        out_ref[z, 64:96] = top[32 * r : 32 * (r + 1)]
-        out_ref[z, 96:] = grad[room * z : room * (z + 1)]
+        rest = pay_ref[32 * r : 32 * (r + 1), 128:].astype(F32)
+        out_ref[z, 32:48] = jnp.concatenate([rest[:16, :64], rest[16:, :64]], axis=1).astype(BF)
+        out_ref[z, 48:64] = top[32 * r : 32 * r + 16].astype(BF)
+        mixed = [
+            top[32 * r + 16 : 32 * (r + 1), :72],
+            rest[:16, 64:72],
+            rest[16:, 64:72],
+            jnp.zeros((16, 24), F32),
+            grad[16 * z : 16 * (z + 1), 128:],
+        ]
+        out_ref[z, 64:80] = jnp.concatenate(mixed, axis=1).astype(BF)
+        out_ref[z, 80:] = grad[16 * z : 16 * (z + 1), :128].astype(BF)
 
 
 def weight_kernel(in_ref, _, out_ref):
-    each, cols = out_ref.shape
-    total = jnp.sum(in_ref[:, 96:].astype(F32), axis=0)
-    out_ref[...] = jnp.concatenate([total[each * t : each * (t + 1)] for t in range(cols // 128)], axis=1)
+    main = jnp.sum(in_ref[:, 80:].astype(F32), axis=0)
+    tail = jnp.sum(in_ref[:, 64:80].astype(F32), axis=0)
+    out_ref[...] = jnp.concatenate([main, tail], axis=1)
+
+
+def weight_end_kernel(in_ref, out_ref):
+    each = out_ref.shape[0]
+    parts = []
+    for c in range(CORES):
+        total = in_ref[c]
+        for y in range(1, in_ref.shape[0] // CORES):
+            total = total + in_ref[CORES * y + c]
+        total = jnp.concatenate([total[:, :128], total[:, 240:]], axis=1)
+        chunks = jnp.concatenate([total[:, HD * t : HD * (t + 1)] for t in range(3)], axis=0).reshape(each, 8, HD)
+        parts += [chunks[:, u, :] for u in range(8)]
+    out_ref[...] = jnp.concatenate(parts, axis=1)
 
 
 def window(h):
@@ -179,53 +207,57 @@
         out[...] = jnp.transpose(t_ref[n])
 
 
-def packed_grads(x):
+def packed_grads(lo, hi, stat):
+    x = jnp.concatenate([lo.astype(F32), hi, jnp.zeros_like(hi)], axis=1).astype(BF)
     x_t = dot(eye(256), x, 1, 1).astype(BF)
-    tail = x[:, 128:].astype(F32)
-
-    def column(n):
-        at = 4 * HD + 3 * n - 128
-        return tail[:, at : at + 1] + tail[:, at + 1 : at + 2] + tail[:, at + 2 : at + 3]
-
     q_t, k_t, v_t, do_t = (x_t[HD * n : HD * (n + 1)] for n in range(4))
+    lse, delta = (stat[:, n : n + 1] + stat[:, n + 1 : n + 2] + stat[:, n + 2 : n + 3] for n in (0, 3))
     grads = set_grads(
-        x[:, :128], x[:, 128:], padded(k_t, 0, 128), padded(v_t, 3 * HD - 128, 128), q_t, k_t, do_t, column(0), column(1)
+        x[:, :128], x[:, 128:], padded(k_t, 0, 128), padded(v_t, 3 * HD - 128, 128), q_t, k_t, do_t, lse, delta
     )
     return jnp.concatenate(grads, axis=0)
 
 
-def joined(in_ref, where, first, count):
-    lo = in_ref[where, first : first + count].reshape(256, 128)
-    hi = in_ref[where, first + count : first + 2 * count].reshape(256, 128)
-    return jnp.concatenate([lo, hi], axis=1)
-
-
-def group_kernel(where_ref, in_ref, _, g_ref):
-    g_ref[...] = packed_grads(joined(in_ref, pl.ds(GROUP * where_ref[1], GROUP), 0, 32))
-
-
-def far_kernel(where_ref, in_ref, g_ref, back_ref):
-    far = packed_grads(joined(in_ref, slice(None), 64, 16))
+def sets_kernel(where_ref, in_ref, _, back_ref):
+    own = pl.ds(GROUP * where_ref[1], GROUP)
+    pairs = in_ref[own, 32:48].astype(F32)
+    mixed = in_ref[:, 64:80].astype(F32)
+    mine = in_ref[own, 64:80].astype(F32)
+    group = packed_grads(
+        in_ref[own, :32].reshape(256, 128),
+        jnp.concatenate([pairs[:, :, :64], pairs[:, :, 64:]], axis=1).reshape(256, 64),
+        jnp.concatenate([mine[:, :, 72:80], mine[:, :, 80:88]], axis=1).reshape(256, 8),
+    )
+    mixed = mixed.reshape(256, 128)
+    far = packed_grads(in_ref[:, 48:64].reshape(256, 128), mixed[:, :64], mixed[:, 64:72])
     row, col = iota((256, 256), 0), iota((256, 256), 1)
     here = ((row >> 7) == where_ref[1]) & (((row >> 2) & 3) == where_ref[0])
     sel = (here & (col == 32 * ((row >> 4) & 7) + (row & 3))).astype(BF)
     hi, lo = split(far)
-    total = (g_ref[...] + dot(hi, sel, 1, 0) + dot(lo, sel, 1, 0)).astype(BF)
+    total = (group + dot(hi, sel, 1, 0) + dot(lo, sel, 1, 0)).astype(BF)
     total = jnp.concatenate([total, jnp.zeros((256 - total.shape[0], 256), BF)], axis=0)
-    back_ref[...] = dot(eye(256), total, 1, 1).astype(BF)
+    total = dot(eye(256), total, 1, 1)
+    for src in range(GROUP):
+        rows = total[32 * src : 32 * (src + 1)]
+        back_ref[src, :32] = rows[:, :128].astype(BF)
+        tail = [rows[:16, 128:144], rows[16:, 128:144], jnp.zeros((16, 96), F32)]
+        back_ref[src, 32:] = jnp.concatenate(tail, axis=1).astype(BF)
 
 
 def final_kernel(z_ref, dq_ref, dk_ref, dv_ref, oq_ref, ok_ref, ov_ref):
     rows, width = dq_ref.shape
     perm_t = (iota((rows, rows), 0) == packed_token(iota((rows, rows), 1))).astype(BF)
-    y = dot(perm_t, z_ref[...], 1, 0).astype(BF)
+    tail = z_ref[:, 32:].astype(F32)
+    tail = jnp.concatenate([tail[:, :, :16], tail[:, :, 16:32]], axis=1).reshape(rows, 16)
+    lanes = [z_ref[:, :32].reshape(rows, 128).astype(F32), tail, jnp.zeros((rows, 112), F32)]
+    y = dot(perm_t, jnp.concatenate(lanes, axis=1).astype(BF), 1, 0).astype(BF)
     mine = own_head(rows, width)
     for n, (near, out) in enumerate(((dq_ref, oq_ref), (dk_ref, ok_ref), (dv_ref, ov_ref))):
         far = dot(y, spread(n, (256, width), 0, 1), 1, 0)
         out[...] = (near[...] + jnp.where(mine, far, 0.0)).astype(BF)
 
 
-def call(kernel, outs, *args, scratch=(), smem=0, hbm=False, flops=0):
+def call(kernel, outs, *args, scratch=(), smem=0, hbm=False, flops=0, room=32):
     vmem = pl.BlockSpec(memory_space=pltpu.VMEM)
     held = pl.BlockSpec(memory_space=pltpu.HBM) if hbm else vmem
     return pl.pallas_call(
@@ -234,7 +266,7 @@
         in_specs=[pl.BlockSpec(memory_space=pltpu.SMEM)] * smem + [held] * (len(args) - smem),
         out_specs=jax.tree.map(lambda _: vmem, outs),
         scratch_shapes=list(scratch),
-        compiler_params=pltpu.CompilerParams(vmem_limit_bytes=32 * 1024 * 1024),
+        compiler_params=pltpu.CompilerParams(vmem_limit_bytes=room * 1024 * 1024),
         cost_estimate=pl.CostEstimate(flops=flops, bytes_accessed=2_000_000, transcendentals=0),
     )(*args)
 
@@ -250,21 +282,24 @@
         return lax.all_to_all(x, axes, 0, 0, tiled=True)
 
     ins = (dy, w_out, o, lse.T, q, k, v)
+    parts = blocks * CORES
     pay, out, d_out, stat = call(
         front_kernel,
         (
             shape((rows, 256), BF),
-            shape((blocks, width * cols // blocks // 128 + 8 * HEADS, 128), BF),
+            shape((parts, width * cols // parts // 128 + 8 * HEADS, 128), BF),
             shape((rows, width), BF),
             shape((rows, 2 * HEADS), F32),
         ),
         *ins,
         hbm=True,
+        room=ROOM,
         scratch=[pltpu.VMEM(x.shape, x.dtype) for x in ins] + [pltpu.SemaphoreType.DMA((len(ins),))],
         flops=1_000_000_000,
     )
-    over_x = exchange(out, "x")
-    out = call(mid_kernel, shape((ring, 144, 128), BF), over_x, pay, flops=100_000_000)
+    where = jnp.stack([lax.axis_index(a) for a in ("x", "zh", "c")]).astype(jnp.int32)
+    over_x = exchange(out, ("x", "c"))
+    out = call(mid_kernel, shape((ring, 96, 128), BF), where, over_x, pay, smem=1, flops=100_000_000)
     over_z = exchange(out, ("zh", "zl"))
     near = call(
         local_kernel,
@@ -273,14 +308,11 @@
         scratch=[pltpu.VMEM((3, width, rows), F32)],
         flops=1_000_000_000,
     )
-    where = jnp.stack([lax.axis_index("x"), lax.axis_index("zh")]).astype(jnp.int32)
-    group = call(group_kernel, shape((3 * HD, 256), F32), where, over_z, near[0], smem=1, flops=100_000_000)
-    back = call(far_kernel, shape((256, 256), BF), where, over_z, group, smem=1, flops=100_000_000)
-    z = exchange(back.reshape(GROUP, rows // GROUP, 256), "zl").reshape(256, 256)
-    grad = call(weight_kernel, shape((width // (blocks * ring), cols), F32), over_z, near[0], flops=1_000_000)
-    members = lax.axis_size("dp")
-    for bit in range(members.bit_length() - 1):
-        grad = grad + lax.ppermute(grad, "dp", [(i, i ^ (1 << bit)) for i in range(members)])
+    back = call(sets_kernel, shape((GROUP, 48, 128), BF), where, over_z, near[0], smem=1, flops=200_000_000)
+    z = exchange(back, "zl")
+    grad = call(weight_kernel, shape((16, 256), F32), over_z, near[0], flops=1_000_000)
+    grad = lax.all_gather(grad, ("y", "c"), axis=0)
+    grad = call(weight_end_kernel, shape((width // (blocks * ring), cols), F32), grad, flops=1_000_000)
     d_q, d_k, d_v = call(final_kernel, (shape((rows, width), BF),) * 3, z, *near, flops=300_000_000)
     return d_q[None], d_k[None], d_v[None], grad
 
@@ -288,10 +320,10 @@
 def solution(mesh):
     dp, seq = mesh.devices.shape
     fine = jax.sharding.Mesh(
-        mesh.devices.reshape(dp, seq // 16, 16 // GROUP, GROUP), ("dp", "x", "zh", "zl")
-    )
-    seq_axes = ("x", "zh", "zl")
-    placed = P("dp", seq_axes, None)
+        mesh.devices.reshape(dp // CORES, CORES, seq // 16, 16 // GROUP, GROUP), ("y", "c", "x", "zh", "zl")
+    )
+    dp_axes, seq_axes = ("y", "c"), ("x", "zh", "zl")
+    placed = P(dp_axes, seq_axes, None)
     return jax.shard_map(
         on_device,
         mesh=fine,

time: 101 us -> 88.4 us (0.88); the launches traced: 99.5 us -> 88 us
  starting transfers between devices: 42 us -> 32.4 us
  local copies, waits for them, and re-layouts: 6.47 us -> 0.02 us
  blocking collectives: 12.3 us -> 14.2 us
  Pallas kernels: 11.7 us -> 13.4 us
  waiting for transfers between devices: 25.7 us -> 27.2 us
    all_gather x0 -> x1, blocking collectives: none -> 14.2 us  [on_device(): grad = lax.all_gather(grad, ('y', 'c'), axis=0)]
    all_to_all x1 -> x0, blocking collectives: 12.3 us -> none  [exchange(): return lax.all_to_all(x, axes, 0, 0, tiled=True)]
    ppermute x3 -> x0, starting transfers between devices: 12 us -> none  [on_device(): lax.ppermute(grad, 'dp', [(i, i ^ 1 << bit) for i in range(members)])]
    unnamed x20 -> x12, local copies, waits for them, and re-layouts: 6.47 us -> 0.02 us
    all_to_all x2 -> x3, waiting for transfers between devices: 21.9 us -> 27.2 us  [exchange(): return lax.all_to_all(x, axes, 0, 0, tiled=True)]
    ppermute x3 -> x0, waiting for transfers between devices: 3.74 us -> none  [on_device(): lax.ppermute(grad, 'dp', [(i, i ^ 1 << bit) for i in range(members)])]
    all_to_all x2 -> x3, starting transfers between devices: 30 us -> 32.4 us  [exchange(): return lax.all_to_all(x, axes, 0, 0, tiled=True)]
    pallas_call x7, Pallas kernels: 11.7 us -> 13.4 us  [call(): pl.pallas_call(kernel, out_shape=outs, in_specs=[pl.BlockSpec(memory_spac...]
  transfers between devices with their start and end apart: 5 -> 3, of which waited for: 4 -> 2; matrix products, arithmetic and copies ran while one was open for 1% -> 0% of each run, Pallas kernels for 2% -> 4%
where the time goes in v3:
time: 88.4 us; the launch traced here: 88 us
  starting transfers between devices  32.4 us (37%)
  waiting for transfers between devices  27.2 us (31%)
  blocking collectives  14.2 us (16%)
  Pallas kernels  13.4 us (15%)
    all_to_all x3, starting transfers between devices, exchange(): return lax.all_to_all(x, axes, 0, 0, tiled=True)  32.4 us
    all_to_all x3, waiting for transfers between devices, exchange(): return lax.all_to_all(x, axes, 0, 0, tiled=True)  27.2 us
    all_gather x1, blocking collectives, on_device(): grad = lax.all_gather(grad, ('y', 'c'), axis=0)  14.2 us
    pallas_call x7, Pallas kernels, call(): pl.pallas_call(kernel, out_shape=outs, in_specs=[pl.BlockSpec(memory_spac...  13.4 us
  transfers between devices with their start and end apart: 3, of which 2 were waited for; matrix products, arithmetic and copies ran while one was open for 0% of the time, Pallas kernels for 4%

profile of v3, /device:TPU:1, one launch (start us, length us, event | category | flops | bytes accessed | tf_op | source)
XLA Modules:
  0.0 88.0 jit_solution(5694092667228150377)
XLA Ops:
  0.6 4.0 %shard_map.102 = (bf16[256,256]{1,0:T(8,128)(2,1)}, bf16[8,352,128]{2,1,0:T(8,128)(2,1)}, bf16[256,384]{1,0:T(8,128)(2,1)}, f32[256,16]{1,0:T(8,128)}) custom-call(bf16[256,768]{1,0:T(8,128)(2,1)} %bitcast.22, bf16[384,768]{1,0:T(8,128)(2,1)} %refs_1_.1, bf16[256,384]{1,0:T(8,128)(2,1)} %bitcast.23, f32[8,256]{1,0:T(8,128)} %bitcast.27, ...), custom_call_target="tpu_custom_call" | custom-call | flops 1000000000 | bytes 2000000 | tf_op jit(solution)/shard_map/pallas_call | solution.py:263
  4.7 0.0 copy-start
  4.7 10.5 %all-to-all-start = ((bf16[8,352,128]{2,1,0:T(8,128)(2,1)}), bf16[8,352,128]{2,1,0:T(8,128)(2,1)S(1)}, u32[]{:S(2)}, u32[]{:S(2)}) async-start(bf16[8,352,128]{2,1,0:T(8,128)(2,1)} %get-tuple-element.14), calls=%async_computation | async-start | bytes 1441792 | tf_op jit(solution)/shard_map/all_to_all | solution.py:282
  15.1 0.1 pad_add_fusion.where_ref
  15.2 11.5 %all-to-all-done.in_ref = bf16[8,352,128]{2,1,0:T(8,128)(2,1)S(1)} async-done(((bf16[8,352,128]{2,1,0:T(8,128)(2,1)}), bf16[8,352,128]{2,1,0:T(8,128)(2,1)S(1)}, u32[]{:S(2)}, u32[]{:S(2)}) %all-to-all-start) | async-done | bytes 720928 | tf_op jit(solution)/shard_map/all_to_all | solution.py:282
  26.8 0.0 copy-done
  26.8 0.0 copy-start.5
  26.8 2.1 %shard_map.103 = bf16[16,96,128]{2,1,0:T(8,128)(2,1)} custom-call(s32[3]{0:T(128)S(1)} %pad_add_fusion.where_ref, bf16[8,352,128]{2,1,0:T(8,128)(2,1)S(1)} %all-to-all-done.in_ref, bf16[256,256]{1,0:T(8,128)(2,1)S(1)} %copy-done), custom_call_target="tpu_custom_call" | custom-call | flops 100000000 | bytes 2000000 | tf_op jit(solution)/shard_map/pallas_call | solution.py:263
  28.8 0.0 copy-start.1
  28.8 0.0 copy-start.2
  28.8 0.0 copy-start.3
  28.8 0.0 copy-start.4
  28.8 10.5 %all-to-all-start.1 = ((bf16[16,96,128]{2,1,0:T(8,128)(2,1)}), bf16[16,96,128]{2,1,0:T(8,128)(2,1)S(1)}, u32[]{:S(2)}, u32[]{:S(2)}) async-start(bf16[16,96,128]{2,1,0:T(8,128)(2,1)} %shard_map.103), calls=%async_computation.1 | async-start | bytes 786432 | tf_op jit(solution)/shard_map/all_to_all | solution.py:282
  39.4 0.0 copy-done.5
  39.4 0.0 copy-done.1
  39.4 0.0 copy-done.2
  39.4 0.0 copy-done.3
  39.4 0.0 copy-done.4
  39.4 2.3 %shard_map.104 = (f32[256,384]{1,0:T(8,128)S(1)}, f32[256,384]{1,0:T(8,128)S(1)}, f32[256,384]{1,0:T(8,128)S(1)}) custom-call(bf16[256,384]{1,0:T(8,128)(2,1)S(1)} %bitcast.17, bf16[256,384]{1,0:T(8,128)(2,1)S(1)} %bitcast.19, bf16[256,384]{1,0:T(8,128)(2,1)S(1)} %bitcast.21, bf16[256,384]{1,0:T(8,128)(2,1)S(1)} %copy-done.4, f32[256,16]{1,0:T(8,128)S(1)} %copy-done.5), custom_call_target="tpu_custom_call" | custom-call | flops 1000000000 | bytes 2000000 | tf_op jit(solution)/shard_map/pallas_call | solution.py:263
  41.8 15.7 %all-to-all-done.1.in_ref = bf16[16,96,128]{2,1,0:T(8,128)(2,1)S(1)} async-done(((bf16[16,96,128]{2,1,0:T(8,128)(2,1)}), bf16[16,96,128]{2,1,0:T(8,128)(2,1)S(1)}, u32[]{:S(2)}, u32[]{:S(2)}) %all-to-all-start.1) | async-done | bytes 393248 | tf_op jit(solution)/shard_map/all_to_all | solution.py:282
  57.4 2.8 %shard_map.105 = bf16[8,48,128]{2,1,0:T(8,128)(2,1)} custom-call(s32[3]{0:T(128)S(1)} %pad_add_fusion.where_ref, bf16[16,96,128]{2,1,0:T(8,128)(2,1)S(1)} %all-to-all-done.1.in_ref, f32[256,384]{1,0:T(8,128)S(1)} %get-tuple-element.18._.dq_ref), custom_call_target="tpu_custom_call" | custom-call | flops 200000000 | bytes 2000000 | tf_op jit(solution)/shard_map/pallas_call | solution.py:263
  60.2 11.4 %all-to-all-start.2 = ((bf16[8,48,128]{2,1,0:T(8,128)(2,1)}), bf16[8,48,128]{2,1,0:T(8,128)(2,1)S(1)}, u32[]{:S(2)}, u32[]{:S(2)}) async-start(bf16[8,48,128]{2,1,0:T(8,128)(2,1)} %shard_map.105), calls=%async_computation.2 | async-start | bytes 196608 | tf_op jit(solution)/shard_map/all_to_all | solution.py:282
  71.7 14.2 %all-gather = f32[128,256]{1,0:T(8,128)S(1)} all-gather(f32[16,256]{1,0:T(8,128)S(1)} %shard_map.107), channel_id=2, replica_groups=mesh['y'=4,'c'=2,'x'=4,'zh'=2,'zl'=8] {'y','c'}, dimensions={0}, use_global_device_ids=true | all-gather | bytes 147456 | tf_op jit(solution)/shard_map/all_gather | solution.py:314
  85.9 0.8 shard_map.108
  86.7 0.0 all-to-all-done.2.z_ref
  86.8 1.3 %shard_map.106 = (bf16[256,384]{1,0:T(8,128)(2,1)}, bf16[256,384]{1,0:T(8,128)(2,1)}, bf16[256,384]{1,0:T(8,128)(2,1)}) custom-call(bf16[8,48,128]{2,1,0:T(8,128)(2,1)S(1)} %all-to-all-done.2.z_ref, f32[256,384]{1,0:T(8,128)S(1)} %get-tuple-element.18._.dq_ref, f32[256,384]{1,0:T(8,128)S(1)} %get-tuple-element.19.dk_ref, f32[256,384]{1,0:T(8,128)S(1)} %get-tuple-element.20.dv_ref), custom_call_target="tpu_custom_call" | custom-call | flops 300000000 | bytes 2000000 | tf_op jit(solution)/shard_map/pallas_call | solution.py:263
  (1 shorter events, 0.0 us)
Async XLA Ops:
  4.7 22.1 %copy-start = (bf16[256,256]{1,0:T(8,128)(2,1)S(1)}, bf16[256,256]{1,0:T(8,128)(2,1)}, u32[]{:S(2)}) copy-start(bf16[256,256]{1,0:T(8,128)(2,1)} %get-tuple-element.15.pay_ref) | copy-start | bytes 393220
  4.7 22.1 %all-to-all-start = ((bf16[8,352,128]{2,1,0:T(8,128)(2,1)}), bf16[8,352,128]{2,1,0:T(8,128)(2,1)S(1)}, u32[]{:S(2)}, u32[]{:S(2)}) async-start(bf16[8,352,128]{2,1,0:T(8,128)(2,1)} %get-tuple-element.14), calls=%async_computation | async-start | bytes 1441792 | tf_op jit(solution)/shard_map/all_to_all | solution.py:282
  26.8 12.6 %copy-start.5 = (f32[256,16]{1,0:T(8,128)S(1)}, f32[256,16]{1,0:T(8,128)}, u32[]{:S(2)}) copy-start(f32[256,16]{1,0:T(8,128)} %get-tuple-element.17.stat_ref) | copy-start | bytes 49156
  28.8 10.5 %copy-start.1 = (bf16[1,256,384]{2,1,0:T(8,128)(2,1)S(1)}, bf16[1,256,384]{2,1,0:T(8,128)(2,1)}, u32[]{:S(2)}) copy-start(bf16[1,256,384]{2,1,0:T(8,128)(2,1)} %param.7) | copy-start | bytes 589828
  28.8 10.6 %copy-start.2 = (bf16[1,256,384]{2,1,0:T(8,128)(2,1)S(1)}, bf16[1,256,384]{2,1,0:T(8,128)(2,1)}, u32[]{:S(2)}) copy-start(bf16[1,256,384]{2,1,0:T(8,128)(2,1)} %param.8) | copy-start | bytes 589828
  28.8 10.6 %copy-start.3 = (bf16[1,256,384]{2,1,0:T(8,128)(2,1)S(1)}, bf16[1,256,384]{2,1,0:T(8,128)(2,1)}, u32[]{:S(2)}) copy-start(bf16[1,256,384]{2,1,0:T(8,128)(2,1)} %param.9) | copy-start | bytes 589828
  28.8 10.6 %copy-start.4 = (bf16[256,384]{1,0:T(8,128)(2,1)S(1)}, bf16[256,384]{1,0:T(8,128)(2,1)}, u32[]{:S(2)}) copy-start(bf16[256,384]{1,0:T(8,128)(2,1)} %get-tuple-element.16.do_ref) | copy-start | bytes 589828
  28.8 28.6 %all-to-all-start.1 = ((bf16[16,96,128]{2,1,0:T(8,128)(2,1)}), bf16[16,96,128]{2,1,0:T(8,128)(2,1)S(1)}, u32[]{:S(2)}, u32[]{:S(2)}) async-start(bf16[16,96,128]{2,1,0:T(8,128)(2,1)} %shard_map.103), calls=%async_computation.1 | async-start | bytes 786432 | tf_op jit(solution)/shard_map/all_to_all | solution.py:282
  60.2 26.5 %all-to-all-start.2 = ((bf16[8,48,128]{2,1,0:T(8,128)(2,1)}), bf16[8,48,128]{2,1,0:T(8,128)(2,1)S(1)}, u32[]{:S(2)}, u32[]{:S(2)}) async-start(bf16[8,48,128]{2,1,0:T(8,128)(2,1)} %shard_map.105), calls=%async_computation.2 | async-start | bytes 196608 | tf_op jit(solution)/shard_map/all_to_all | solution.py:282

commit v4 on v3

v4 whole, which is shorter than its diff:
```python
import functools

import jax
import jax.numpy as jnp
from jax import lax
from jax.experimental import pallas as pl
from jax.experimental.pallas import tpu as pltpu
from jax.sharding import PartitionSpec as P

HEADS = 8
HD = 48
GROUP = 8
CORES = 2
ROOM = 60
BF = jnp.bfloat16
F32 = jnp.float32


def iota(shape, dim):
    return lax.broadcasted_iota(jnp.int32, shape, dim)


def dot(a, b, ca, cb):
    return lax.dot_general(a, b, (((ca,), (cb,)), ((), ())), preferred_element_type=F32)


def split(x):
    hi = x.astype(BF)
    return hi, (x - hi.astype(F32)).astype(BF)


def eye(n):
    return (iota((n, n), 0) == iota((n, n), 1)).astype(BF)


def packed_token(p):
    return 64 * (p & 3) + 8 * ((p >> 2) & 7) + (p >> 5)


def spread(part, lanes, width):
    return (iota((1, lanes), 1) - HD * part == lax.rem(iota((width, 1), 0), HD)).astype(BF)


def own_head(rows, width):
    return lax.div(iota((1, width), 1), HD) == (iota((rows, 1), 0) & (GROUP - 1))


def selector(source, count):
    return (iota((source.shape[0], count), 1) == source).astype(BF)


def front_kernel(*refs):
    hbm, outs, vmem, held, (stat_ref, sems) = refs[:7], refs[7:10], refs[11:18], refs[18:21], (refs[10], refs[21])
    copies = [pltpu.make_async_copy(a, b, sems.at[n]) for n, (a, b) in enumerate(zip(hbm, vmem))]
    for copy in copies:
        copy.start()
    dy_ref, o_ref, w_ref, lse_ref, q_ref, k_ref, v_ref = vmem
    out_ref, do_ref, pay_ref = held
    rows, width = o_ref.shape
    cols = dy_ref.shape[1]
    parts = out_ref.shape[0]
    count = width * cols // parts // 128
    leave = [
        pltpu.make_async_copy(held[0].at[:, :count], outs[0].at[:, :count], sems.at[7]),
        pltpu.make_async_copy(held[1], outs[1], sems.at[8]),
        pltpu.make_async_copy(held[2], outs[2], sems.at[9]),
        pltpu.make_async_copy(held[0].at[:, count:], outs[0].at[:, count:], sems.at[10]),
    ]
    copies[0].wait()
    copies[1].wait()
    out, dy = o_ref[...], dy_ref[...]
    each, half = width * CORES // parts, cols // CORES
    grad = dot(out, dy, 0, 0)
    for n in range(parts):
        x, c = divmod(n, CORES)
        for t in range(half // 128):
            tile = grad[each * x : each * (x + 1), half * c + 128 * t : half * c + 128 * (t + 1)]
            out_ref[n, each * t : each * (t + 1)] = tile.astype(BF)
    leave[0].start()
    copies[2].wait()
    copies[3].wait()
    d_out = dot(dy, w_ref[...], 1, 1).astype(BF)
    do_ref[...] = d_out
    leave[1].start()
    hi, lo = split(d_out.astype(F32) * out.astype(F32))
    heads = (lax.div(iota((width, 1), 0), HD) == iota((width, 128), 1)).astype(BF)
    delta = (dot(hi, heads, 1, 0) + dot(lo, heads, 1, 0))[:, :HEADS]
    lse = jnp.transpose(lse_ref[...])
    stat_ref[...] = jnp.concatenate([delta, lse], axis=1)
    for copy in copies[4:]:
        copy.wait()
    mine = own_head(rows, width)
    pay = jnp.zeros((rows, 256), F32)
    for part, x in enumerate((q_ref[...], k_ref[...], v_ref[...], d_out)):
        pay += dot(jnp.where(mine, x, jnp.zeros_like(x)), spread(part, 256, width), 1, 0)
    pick = iota((1, HEADS), 1) == (iota((rows, 1), 0) & (GROUP - 1))
    lane = iota((rows, 128), 1)
    tail = pay[:, 128:]
    for base, x in ((64, lse), (67, delta)):
        own = jnp.sum(jnp.where(pick, x, 0.0), axis=1, keepdims=True)
        for n in range(3):
            piece = own.astype(BF).astype(F32)
            tail += jnp.where(lane == base + n, piece, 0.0)
            own = own - piece
    pay = jnp.concatenate([pay[:, :128], tail], axis=1).astype(BF)
    pay_ref[...] = dot(selector(packed_token(iota((rows, 1), 0)), rows), pay, 1, 0).astype(BF)
    leave[2].start()
    at = iota((8 * HEADS, 1), 0)
    token = 64 * (at & 3) + ((at >> 2) & 7)
    first = selector(jnp.where(at < 4 * HEADS, token, -1), rows)
    second = selector(jnp.where(at < 4 * HEADS, -1, token), rows)
    top = (dot(first, pay[:, :128], 1, 0) + dot(second, pay[:, 128:], 1, 0)).astype(BF)
    for n in range(parts):
        out_ref[n, count:] = top
    leave[3].start()
    for copy in leave:
        copy.wait()


def mid_kernel(where_ref, in_ref, pay_ref, out_ref):
    ring = out_ref.shape[0]
    count = in_ref.shape[1] - 8 * HEADS
    sums = jnp.sum(in_ref[:, :count].astype(F32), axis=0).astype(BF)
    each = count // 3
    few = each // ring
    to = iota((16 * ring, 1), 0)
    z, q = to >> 4, to & 15
    t = (q * 43) >> 8
    main = dot(selector(each * t + few * z + q - few * t, count), sums, 1, 0).astype(BF)
    last = selector(jnp.where(q < 8, 2 * each + few * z + 4 + (q & 1), -1), count)
    last = dot(last, sums, 1, 0)
    lane = iota((1, 128), 1)
    last = jnp.where((lane >> 5) == (q >> 1), last, 0.0).astype(BF)
    last = dot(last, selector(96 + (iota((128, 1), 0) & 31), 128), 1, 0)
    top = jnp.concatenate([in_ref[CORES * x + where_ref[2], count:] for x in range(4)], axis=0)
    to = iota((top.shape[0], 1), 0)
    source = 64 * ((to >> 2) & 3) + 32 * ((to >> 4) & 1) + 4 * (to >> 5) + (to & 3)
    top = dot(selector(source, top.shape[0]), top, 1, 0)
    for r in range(GROUP):
        low = pay_ref[32 * r : 32 * (r + 1), :128]
        rest = pay_ref[32 * r : 32 * (r + 1), 128:].astype(F32)
        pairs = jnp.concatenate([rest[:16, :64], rest[16:, :64]], axis=1).astype(BF)
        near = top[32 * r : 32 * r + 16].astype(BF)
        mixed = [top[32 * r + 16 : 32 * (r + 1), :72], rest[:16, 64:72], rest[16:, 64:72], jnp.zeros((16, 40), F32)]
        mixed = jnp.concatenate(mixed, axis=1)
        for z in range(r, ring, GROUP):
            out_ref[z, :32] = low
            out_ref[z, 32:48] = pairs
            out_ref[z, 48:64] = near
            out_ref[z, 64:80] = (mixed + last[16 * z : 16 * (z + 1)]).astype(BF)
            out_ref[z, 80:] = main[16 * z : 16 * (z + 1)]


def weight_kernel(in_ref, _, out_ref):
    out_ref[:16] = jnp.sum(in_ref[:, 80:].astype(F32), axis=0)
    out_ref[16:] = jnp.sum(in_ref[:, 64:80].astype(F32), axis=0)[:8]


def weight_end_kernel(in_ref, out_ref):
    each = out_ref.shape[0]
    parts = []
    for c in range(CORES):
        total = in_ref[c]
        for y in range(1, in_ref.shape[0] // CORES):
            total = total + in_ref[CORES * y + c]
        last = jnp.concatenate([total[16 + 2 * k : 18 + 2 * k, 96:] for k in range(4)], axis=1)
        total = jnp.concatenate([total[:16], last], axis=0)
        parts += [total[each * t : each * (t + 1)] for t in range(3)]
    out_ref[...] = jnp.concatenate(parts, axis=1)


def window(h):
    lo = HD * h // 128 * 128
    hi = -(-HD * (h + 1) // 128) * 128
    return lo, hi


def padded(x_t, before, total):
    parts = []
    if before:
        parts.append(jnp.zeros((before, x_t.shape[1]), x_t.dtype))
    parts.append(x_t)
    after = total - before - x_t.shape[0]
    if after:
        parts.append(jnp.zeros((after, x_t.shape[1]), x_t.dtype))
    return jnp.concatenate(parts, axis=0)


def set_grads(q_win, do_win, k_pad, v_pad, q_t, k_t, do_t, lse, delta):
    scale = float(HD) ** -0.5
    probs = jnp.exp(dot(q_win, k_pad, 1, 0) * scale - lse)
    d_scores = (probs * (dot(do_win, v_pad, 1, 0) - delta)).astype(BF)
    return (
        dot(k_t, d_scores, 1, 1) * scale,
        dot(q_t, d_scores, 1, 0) * scale,
        dot(do_t, probs.astype(BF), 1, 0),
    )


def local_kernel(q_ref, k_ref, v_ref, do_ref, stat_ref, dq_ref, dk_ref, dv_ref, t_ref):
    q_t, k_t, v_t, do_t = (jnp.transpose(r[...]) for r in (q_ref, k_ref, v_ref, do_ref))
    for h in range(HEADS):
        own = slice(HD * h, HD * (h + 1))
        lo, hi = window(h)
        grads = set_grads(
            q_ref[:, lo:hi],
            do_ref[:, lo:hi],
            padded(k_t[own], HD * h - lo, hi - lo),
            padded(v_t[own], HD * h - lo, hi - lo),
            q_t[own],
            k_t[own],
            do_t[own],
            stat_ref[:, HEADS + h : HEADS + h + 1],
            stat_ref[:, h : h + 1],
        )
        for n, g in enumerate(grads):
            t_ref[n, own, :] = g
    for n, out in enumerate((dq_ref, dk_ref, dv_ref)):
        out[...] = jnp.transpose(t_ref[n])


def packed_grads(lo, hi):
    scale = float(HD) ** -0.5
    one = eye(128)
    x_t = jnp.concatenate([dot(one, lo, 1, 1), dot(one, hi, 1, 1)], axis=0).astype(BF)
    q_t, k_t, v_t, do_t = (x_t[HD * n : HD * (n + 1)] for n in range(4))
    row = iota((64, 256), 0)
    lse = dot(hi, jnp.concatenate([jnp.zeros((64, 256), BF), (row < 3).astype(BF)], axis=0), 1, 0)
    minus = jnp.where((row >= 3) & (row < 6), -1.0, 0.0).astype(BF)
    probs = jnp.exp(dot(lo, padded(k_t, 0, 128), 1, 0) * scale - lse)
    d_probs = dot(hi, jnp.concatenate([jnp.zeros((16, 256), BF), v_t, minus], axis=0), 1, 0)
    d_scores = (probs * d_probs).astype(BF)
    return jnp.concatenate(
        [
            dot(k_t, d_scores, 1, 1) * scale,
            dot(q_t, d_scores, 1, 0) * scale,
            dot(do_t, probs.astype(BF), 1, 0),
        ],
        axis=0,
    )


def sets_kernel(where_ref, in_ref, _, back_ref):
    own = pl.ds(GROUP * where_ref[1], GROUP)
    pairs = in_ref[own, 32:48].astype(F32)
    mine = in_ref[own, 64:80].astype(F32)
    blank = jnp.zeros((GROUP, 16, 56), F32)
    hi = jnp.concatenate(
        [
            jnp.concatenate([pairs[:, :, :64], mine[:, :, 72:80], blank], axis=2),
            jnp.concatenate([pairs[:, :, 64:], mine[:, :, 80:88], blank], axis=2),
        ],
        axis=1,
    )
    group = packed_grads(in_ref[own, :32].reshape(256, 128), hi.reshape(256, 128).astype(BF))
    hi = in_ref[:, 64:80].reshape(256, 128)
    hi = jnp.where(iota((1, 128), 1) < 72, hi, jnp.zeros_like(hi))
    far = packed_grads(in_ref[:, 48:64].reshape(256, 128), hi)
    row = iota((256, 1), 0)
    here = ((row >> 7) == where_ref[1]) & (((row >> 2) & 3) == where_ref[0])
    sel = selector(jnp.where(here, 32 * ((row >> 4) & 7) + (row & 3), -1), 256)
    hi, lo = split(far)
    total = (group + dot(hi, sel, 1, 0) + dot(lo, sel, 1, 0)).astype(BF)
    total = dot(eye(256), total, 1, 1)
    for src in range(GROUP):
        rows = total[32 * src : 32 * (src + 1)]
        back_ref[src, :32] = rows[:, :128].astype(BF)
        tail = [rows[:16, 128:144], rows[16:, 128:144], jnp.zeros((16, 96), F32)]
        back_ref[src, 32:] = jnp.concatenate(tail, axis=1).astype(BF)


def final_kernel(z_ref, dq_ref, dk_ref, dv_ref, oq_ref, ok_ref, ov_ref):
    rows, width = dq_ref.shape
    token = iota((rows, 1), 0)
    perm_t = selector(32 * (token & 7) + 4 * ((token >> 3) & 7) + (token >> 6), rows)
    tail = z_ref[:, 32:].astype(F32)
    tail = jnp.concatenate([tail[:, :, :16], tail[:, :, 16:32]], axis=1).reshape(rows, 16)
    lanes = [z_ref[:, :32].reshape(rows, 128).astype(F32), tail, jnp.zeros((rows, 112), F32)]
    y = dot(perm_t, jnp.concatenate(lanes, axis=1).astype(BF), 1, 0).astype(BF)
    mine = own_head(rows, width)
    for n, (near, out) in enumerate(((dq_ref, oq_ref), (dk_ref, ok_ref), (dv_ref, ov_ref))):
        far = dot(y, (iota((256, 1), 0) - HD * n == lax.rem(iota((1, width), 1), HD)).astype(BF), 1, 0)
        out[...] = (near[...] + jnp.where(mine, far, 0.0)).astype(BF)


def call(kernel, outs, *args, scratch=(), smem=0, hbm=(), flops=0, room=32):
    vmem = pl.BlockSpec(memory_space=pltpu.VMEM)
    far = pl.BlockSpec(memory_space=pltpu.HBM)
    held = far if hbm else vmem
    return pl.pallas_call(
        kernel,
        out_shape=outs,
        in_specs=[pl.BlockSpec(memory_space=pltpu.SMEM)] * smem + [held] * (len(args) - smem),
        out_specs=tuple(far if n in hbm else vmem for n in range(len(outs))) if isinstance(outs, tuple) else vmem,
        scratch_shapes=list(scratch),
        compiler_params=pltpu.CompilerParams(vmem_limit_bytes=room * 1024 * 1024),
        cost_estimate=pl.CostEstimate(flops=flops, bytes_accessed=2_000_000, transcendentals=0),
    )(*args)


def on_device(queries, keys, values, outputs, d_final, stats, w_out):
    q, k, v, o, dy, lse = (x[0] for x in (queries, keys, values, outputs, d_final, stats))
    rows, width = q.shape
    cols = dy.shape[1]
    blocks, ring = lax.axis_size("x"), lax.axis_size(("zh", "zl"))
    shape = jax.ShapeDtypeStruct

    def exchange(x, axes):
        return lax.all_to_all(x, axes, 0, 0, tiled=True)

    ins = (dy, o, w_out, lse.T, q, k, v)
    parts = blocks * CORES
    outs = (
        shape((parts, width * cols // parts // 128 + 8 * HEADS, 128), BF),
        shape((rows, width), BF),
        shape((rows, 256), BF),
        shape((rows, 2 * HEADS), F32),
    )
    out, d_out, pay, stat = call(
        front_kernel,
        outs,
        *ins,
        hbm=(0, 1, 2),
        room=ROOM,
        scratch=[pltpu.VMEM(x.shape, x.dtype) for x in ins + outs[:3]] + [pltpu.SemaphoreType.DMA((11,))],
        flops=1_000_000_000,
    )
    where = jnp.stack([lax.axis_index(a) for a in ("x", "zh", "c")]).astype(jnp.int32)
    over_x = exchange(out, ("x", "c"))
    out = call(mid_kernel, shape((ring, 96, 128), BF), where, over_x, pay, smem=1, flops=100_000_000)
    over_z = exchange(out, ("zh", "zl"))
    near = call(
        local_kernel,
        (shape((rows, width), F32),) * 3,
        q, k, v, d_out, stat,
        scratch=[pltpu.VMEM((3, width, rows), F32)],
        flops=1_000_000_000,
    )
    back = call(sets_kernel, shape((GROUP, 48, 128), BF), where, over_z, near[0], smem=1, flops=200_000_000)
    z = exchange(back, "zl")
    grad = call(weight_kernel, shape((24, 128), F32), over_z, near[0], flops=1_000_000)
    grad = lax.all_gather(grad, ("y", "c"), axis=0)
    grad = call(weight_end_kernel, shape((width // (blocks * ring), cols), F32), grad, flops=1_000_000)
    d_q, d_k, d_v = call(final_kernel, (shape((rows, width), BF),) * 3, z, *near, flops=300_000_000)
    return d_q[None], d_k[None], d_v[None], grad


def solution(mesh):
    dp, seq = mesh.devices.shape
    fine = jax.sharding.Mesh(
        mesh.devices.reshape(dp // CORES, CORES, seq // 16, 16 // GROUP, GROUP), ("y", "c", "x", "zh", "zl")
    )
    dp_axes, seq_axes = ("y", "c"), ("x", "zh", "zl")
    placed = P(dp_axes, seq_axes, None)
    return jax.shard_map(
        on_device,
        mesh=fine,
        in_specs=(placed,) * 6 + (P(),),
        out_specs=(placed,) * 3 + (P(seq_axes, None),),
        check_vma=False,
    )
```

time: 88.4 us -> 88.3 us (level)
  transfers between devices with their start and end apart: 3 -> 3, of which waited for: 2 -> 2; matrix products, arithmetic and copies ran while one was open for 0% -> 0% of each run, Pallas kernels for 4% -> 3%
where the time goes in v4:
time: 88.3 us; the launch traced here: 87.9 us
  starting transfers between devices  32.4 us (37%)
  waiting for transfers between devices  27.2 us (31%)
  blocking collectives  14.2 us (16%)
  Pallas kernels  13.3 us (15%)
    all_to_all x3, starting transfers between devices, exchange(): return lax.all_to_all(x, axes, 0, 0, tiled=True)  32.4 us
    all_to_all x3, waiting for transfers between devices, exchange(): return lax.all_to_all(x, axes, 0, 0, tiled=True)  27.2 us
    all_gather x1, blocking collectives, on_device(): grad = lax.all_gather(grad, ('y', 'c'), axis=0)  14.2 us
    pallas_call x7, Pallas kernels, call(): pl.pallas_call(kernel, out_shape=outs, in_specs=[pl.BlockSpec(memory_spac...  13.3 us
  transfers between devices with their start and end apart: 3, of which 2 were waited for; matrix products, arithmetic and copies ran while one was open for 0% of the time, Pallas kernels for 3%

profile of v4, /device:TPU:1, one launch (start us, length us, event | category | flops | bytes accessed | tf_op | source)
XLA Modules:
  0.0 87.9 jit_solution(9759725513373373796)
XLA Ops:
  0.6 4.6 %shard_map.102 = (bf16[8,352,128]{2,1,0:T(8,128)(2,1)}, bf16[256,384]{1,0:T(8,128)(2,1)}, bf16[256,256]{1,0:T(8,128)(2,1)}, f32[256,16]{1,0:T(8,128)}) custom-call(bf16[256,768]{1,0:T(8,128)(2,1)} %bitcast.22, bf16[256,384]{1,0:T(8,128)(2,1)} %bitcast.23, bf16[384,768]{1,0:T(8,128)(2,1)} %refs_2_.1, f32[8,256]{1,0:T(8,128)} %bitcast.27, ...), custom_call_target="tpu_custom_call" | custom-call | flops 1000000000 | bytes 2000000 | tf_op jit(solution)/shard_map/pallas_call | solution.py:290
  5.2 0.0 copy-start
  5.2 10.5 %all-to-all-start = ((bf16[8,352,128]{2,1,0:T(8,128)(2,1)}), bf16[8,352,128]{2,1,0:T(8,128)(2,1)S(1)}, u32[]{:S(2)}, u32[]{:S(2)}) async-start(bf16[8,352,128]{2,1,0:T(8,128)(2,1)} %get-tuple-element.14), calls=%async_computation | async-start | bytes 1441792 | tf_op jit(solution)/shard_map/all_to_all | solution.py:309
  15.7 0.1 pad_add_fusion.where_ref
  15.8 11.5 %all-to-all-done.in_ref = bf16[8,352,128]{2,1,0:T(8,128)(2,1)S(1)} async-done(((bf16[8,352,128]{2,1,0:T(8,128)(2,1)}), bf16[8,352,128]{2,1,0:T(8,128)(2,1)S(1)}, u32[]{:S(2)}, u32[]{:S(2)}) %all-to-all-start) | async-done | bytes 720928 | tf_op jit(solution)/shard_map/all_to_all | solution.py:309
  27.3 0.0 copy-done
  27.3 0.0 copy-start.5
  27.3 1.8 %shard_map.103 = bf16[16,96,128]{2,1,0:T(8,128)(2,1)} custom-call(s32[3]{0:T(128)S(1)} %pad_add_fusion.where_ref, bf16[8,352,128]{2,1,0:T(8,128)(2,1)S(1)} %all-to-all-done.in_ref, bf16[256,256]{1,0:T(8,128)(2,1)S(1)} %copy-done), custom_call_target="tpu_custom_call" | custom-call | flops 100000000 | bytes 2000000 | tf_op jit(solution)/shard_map/pallas_call | solution.py:290
  29.1 0.0 copy-start.1
  29.1 0.0 copy-start.2
  29.1 0.0 copy-start.3
  29.1 0.0 copy-start.4
  29.1 10.5 %all-to-all-start.1 = ((bf16[16,96,128]{2,1,0:T(8,128)(2,1)}), bf16[16,96,128]{2,1,0:T(8,128)(2,1)S(1)}, u32[]{:S(2)}, u32[]{:S(2)}) async-start(bf16[16,96,128]{2,1,0:T(8,128)(2,1)} %shard_map.103), calls=%async_computation.1 | async-start | bytes 786432 | tf_op jit(solution)/shard_map/all_to_all | solution.py:309
  39.6 0.0 copy-done.5
  39.6 0.0 copy-done.1
  39.6 0.0 copy-done.2
  39.6 0.0 copy-done.3
  39.6 0.0 copy-done.4
  39.7 2.3 %shard_map.104 = (f32[256,384]{1,0:T(8,128)S(1)}, f32[256,384]{1,0:T(8,128)S(1)}, f32[256,384]{1,0:T(8,128)S(1)}) custom-call(bf16[256,384]{1,0:T(8,128)(2,1)S(1)} %bitcast.17, bf16[256,384]{1,0:T(8,128)(2,1)S(1)} %bitcast.19, bf16[256,384]{1,0:T(8,128)(2,1)S(1)} %bitcast.21, bf16[256,384]{1,0:T(8,128)(2,1)S(1)} %copy-done.4, f32[256,16]{1,0:T(8,128)S(1)} %copy-done.5), custom_call_target="tpu_custom_call" | custom-call | flops 1000000000 | bytes 2000000 | tf_op jit(solution)/shard_map/pallas_call | solution.py:290
  42.0 15.7 %all-to-all-done.1.in_ref = bf16[16,96,128]{2,1,0:T(8,128)(2,1)S(1)} async-done(((bf16[16,96,128]{2,1,0:T(8,128)(2,1)}), bf16[16,96,128]{2,1,0:T(8,128)(2,1)S(1)}, u32[]{:S(2)}, u32[]{:S(2)}) %all-to-all-start.1) | async-done | bytes 393248 | tf_op jit(solution)/shard_map/all_to_all | solution.py:309
  57.7 2.6 %shard_map.105 = bf16[8,48,128]{2,1,0:T(8,128)(2,1)} custom-call(s32[3]{0:T(128)S(1)} %pad_add_fusion.where_ref, bf16[16,96,128]{2,1,0:T(8,128)(2,1)S(1)} %all-to-all-done.1.in_ref, f32[256,384]{1,0:T(8,128)S(1)} %get-tuple-element.18._.dq_ref), custom_call_target="tpu_custom_call" | custom-call | flops 200000000 | bytes 2000000 | tf_op jit(solution)/shard_map/pallas_call | solution.py:290
  60.3 11.4 %all-to-all-start.2 = ((bf16[8,48,128]{2,1,0:T(8,128)(2,1)}), bf16[8,48,128]{2,1,0:T(8,128)(2,1)S(1)}, u32[]{:S(2)}, u32[]{:S(2)}) async-start(bf16[8,48,128]{2,1,0:T(8,128)(2,1)} %shard_map.105), calls=%async_computation.2 | async-start | bytes 196608 | tf_op jit(solution)/shard_map/all_to_all | solution.py:309
  71.7 14.2 %all-gather = f32[192,128]{1,0:T(8,128)S(1)} all-gather(f32[24,128]{1,0:T(8,128)S(1)} %shard_map.107), channel_id=2, replica_groups=mesh['y'=4,'c'=2,'x'=4,'zh'=2,'zl'=8] {'y','c'}, dimensions={0}, use_global_device_ids=true | all-gather | bytes 110592 | tf_op jit(solution)/shard_map/all_gather | solution.py:342
  86.0 0.7 shard_map.108
  86.6 0.0 all-to-all-done.2.z_ref
  86.6 1.3 %shard_map.106 = (bf16[256,384]{1,0:T(8,128)(2,1)}, bf16[256,384]{1,0:T(8,128)(2,1)}, bf16[256,384]{1,0:T(8,128)(2,1)}) custom-call(bf16[8,48,128]{2,1,0:T(8,128)(2,1)S(1)} %all-to-all-done.2.z_ref, f32[256,384]{1,0:T(8,128)S(1)} %get-tuple-element.18._.dq_ref, f32[256,384]{1,0:T(8,128)S(1)} %get-tuple-element.19.dk_ref, f32[256,384]{1,0:T(8,128)S(1)} %get-tuple-element.20.dv_ref), custom_call_target="tpu_custom_call" | custom-call | flops 300000000 | bytes 2000000 | tf_op jit(solution)/shard_map/pallas_call | solution.py:290
  (1 shorter events, 0.0 us)
Async XLA Ops:
  5.2 22.1 %copy-start = (bf16[256,256]{1,0:T(8,128)(2,1)S(1)}, bf16[256,256]{1,0:T(8,128)(2,1)}, u32[]{:S(2)}) copy-start(bf16[256,256]{1,0:T(8,128)(2,1)} %get-tuple-element.15.pay_ref) | copy-start | bytes 393220
  5.2 22.1 %all-to-all-start = ((bf16[8,352,128]{2,1,0:T(8,128)(2,1)}), bf16[8,352,128]{2,1,0:T(8,128)(2,1)S(1)}, u32[]{:S(2)}, u32[]{:S(2)}) async-start(bf16[8,352,128]{2,1,0:T(8,128)(2,1)} %get-tuple-element.14), calls=%async_computation | async-start | bytes 1441792 | tf_op jit(solution)/shard_map/all_to_all | solution.py:309
  27.3 12.3 %copy-start.5 = (f32[256,16]{1,0:T(8,128)S(1)}, f32[256,16]{1,0:T(8,128)}, u32[]{:S(2)}) copy-start(f32[256,16]{1,0:T(8,128)} %get-tuple-element.17.stat_ref) | copy-start | bytes 49156
  29.1 10.6 %copy-start.1 = (bf16[1,256,384]{2,1,0:T(8,128)(2,1)S(1)}, bf16[1,256,384]{2,1,0:T(8,128)(2,1)}, u32[]{:S(2)}) copy-start(bf16[1,256,384]{2,1,0:T(8,128)(2,1)} %param.7) | copy-start | bytes 589828
  29.1 10.6 %copy-start.2 = (bf16[1,256,384]{2,1,0:T(8,128)(2,1)S(1)}, bf16[1,256,384]{2,1,0:T(8,128)(2,1)}, u32[]{:S(2)}) copy-start(bf16[1,256,384]{2,1,0:T(8,128)(2,1)} %param.8) | copy-start | bytes 589828
  29.1 10.6 %copy-start.3 = (bf16[1,256,384]{2,1,0:T(8,128)(2,1)S(1)}, bf16[1,256,384]{2,1,0:T(8,128)(2,1)}, u32[]{:S(2)}) copy-start(bf16[1,256,384]{2,1,0:T(8,128)(2,1)} %param.9) | copy-start | bytes 589828
  29.1 10.6 %copy-start.4 = (bf16[256,384]{1,0:T(8,128)(2,1)S(1)}, bf16[256,384]{1,0:T(8,128)(2,1)}, u32[]{:S(2)}) copy-start(bf16[256,384]{1,0:T(8,128)(2,1)} %get-tuple-element.16.do_ref) | copy-start | bytes 589828
  29.1 28.6 %all-to-all-start.1 = ((bf16[16,96,128]{2,1,0:T(8,128)(2,1)}), bf16[16,96,128]{2,1,0:T(8,128)(2,1)S(1)}, u32[]{:S(2)}, u32[]{:S(2)}) async-start(bf16[16,96,128]{2,1,0:T(8,128)(2,1)} %shard_map.103), calls=%async_computation.1 | async-start | bytes 786432 | tf_op jit(solution)/shard_map/all_to_all | solution.py:309
  60.3 26.3 %all-to-all-start.2 = ((bf16[8,48,128]{2,1,0:T(8,128)(2,1)}), bf16[8,48,128]{2,1,0:T(8,128)(2,1)S(1)}, u32[]{:S(2)}, u32[]{:S(2)}) async-start(bf16[8,48,128]{2,1,0:T(8,128)(2,1)} %shard_map.105), calls=%async_computation.2 | async-start | bytes 196608 | tf_op jit(solution)/shard_map/all_to_all | solution.py:309

commit v5 on v4

--- a/solution.py
+++ b/solution.py
@@ -50,45 +50,25 @@
 
 
 def front_kernel(*refs):
-    hbm, outs, vmem, held, (stat_ref, sems) = refs[:7], refs[7:10], refs[11:18], refs[18:21], (refs[10], refs[21])
+    hbm, (out_ref, do_ref, pay_ref, stat_ref), vmem, sems = refs[:7], refs[7:11], refs[11:18], refs[18]
     copies = [pltpu.make_async_copy(a, b, sems.at[n]) for n, (a, b) in enumerate(zip(hbm, vmem))]
     for copy in copies:
         copy.start()
     dy_ref, o_ref, w_ref, lse_ref, q_ref, k_ref, v_ref = vmem
-    out_ref, do_ref, pay_ref = held
     rows, width = o_ref.shape
     cols = dy_ref.shape[1]
     parts = out_ref.shape[0]
     count = width * cols // parts // 128
-    leave = [
-        pltpu.make_async_copy(held[0].at[:, :count], outs[0].at[:, :count], sems.at[7]),
-        pltpu.make_async_copy(held[1], outs[1], sems.at[8]),
-        pltpu.make_async_copy(held[2], outs[2], sems.at[9]),
-        pltpu.make_async_copy(held[0].at[:, count:], outs[0].at[:, count:], sems.at[10]),
-    ]
-    copies[0].wait()
-    copies[1].wait()
+    for copy in copies:
+        copy.wait()
     out, dy = o_ref[...], dy_ref[...]
-    each, half = width * CORES // parts, cols // CORES
-    grad = dot(out, dy, 0, 0)
-    for n in range(parts):
-        x, c = divmod(n, CORES)
-        for t in range(half // 128):
-            tile = grad[each * x : each * (x + 1), half * c + 128 * t : half * c + 128 * (t + 1)]
-            out_ref[n, each * t : each * (t + 1)] = tile.astype(BF)
-    leave[0].start()
-    copies[2].wait()
-    copies[3].wait()
     d_out = dot(dy, w_ref[...], 1, 1).astype(BF)
     do_ref[...] = d_out
-    leave[1].start()
     hi, lo = split(d_out.astype(F32) * out.astype(F32))
     heads = (lax.div(iota((width, 1), 0), HD) == iota((width, 128), 1)).astype(BF)
     delta = (dot(hi, heads, 1, 0) + dot(lo, heads, 1, 0))[:, :HEADS]
     lse = jnp.transpose(lse_ref[...])
     stat_ref[...] = jnp.concatenate([delta, lse], axis=1)
-    for copy in copies[4:]:
-        copy.wait()
     mine = own_head(rows, width)
     pay = jnp.zeros((rows, 256), F32)
     for part, x in enumerate((q_ref[...], k_ref[...], v_ref[...], d_out)):
@@ -104,7 +84,6 @@
             own = own - piece
     pay = jnp.concatenate([pay[:, :128], tail], axis=1).astype(BF)
     pay_ref[...] = dot(selector(packed_token(iota((rows, 1), 0)), rows), pay, 1, 0).astype(BF)
-    leave[2].start()
     at = iota((8 * HEADS, 1), 0)
     token = 64 * (at & 3) + ((at >> 2) & 7)
     first = selector(jnp.where(at < 4 * HEADS, token, -1), rows)
@@ -112,12 +91,16 @@
     top = (dot(first, pay[:, :128], 1, 0) + dot(second, pay[:, 128:], 1, 0)).astype(BF)
     for n in range(parts):
         out_ref[n, count:] = top
-    leave[3].start()
-    for copy in leave:
-        copy.wait()
-
-
-def mid_kernel(where_ref, in_ref, pay_ref, out_ref):
+    each, half = width * CORES // parts, cols // CORES
+    grad = dot(out, dy, 0, 0)
+    for n in range(parts):
+        x, c = divmod(n, CORES)
+        for t in range(half // 128):
+            tile = grad[each * x : each * (x + 1), half * c + 128 * t : half * c + 128 * (t + 1)]
+            out_ref[n, each * t : each * (t + 1)] = tile.astype(BF)
+
+
+def mid_kernel(where_ref, in_ref, pay_ref, _, out_ref):
     ring = out_ref.shape[0]
     count = in_ref.shape[1] - 8 * HEADS
     sums = jnp.sum(in_ref[:, :count].astype(F32), axis=0).astype(BF)
@@ -151,7 +134,7 @@
             out_ref[z, 80:] = main[16 * z : 16 * (z + 1)]
 
 
-def weight_kernel(in_ref, _, out_ref):
+def weight_kernel(in_ref, out_ref):
     out_ref[:16] = jnp.sum(in_ref[:, 80:].astype(F32), axis=0)
     out_ref[16:] = jnp.sum(in_ref[:, 64:80].astype(F32), axis=0)[:8]
 
@@ -240,7 +223,7 @@
     )
 
 
-def sets_kernel(where_ref, in_ref, _, back_ref):
+def sets_kernel(where_ref, in_ref, back_ref):
     own = pl.ds(GROUP * where_ref[1], GROUP)
     pairs = in_ref[own, 32:48].astype(F32)
     mine = in_ref[own, 64:80].astype(F32)
@@ -283,15 +266,14 @@
         out[...] = (near[...] + jnp.where(mine, far, 0.0)).astype(BF)
 
 
-def call(kernel, outs, *args, scratch=(), smem=0, hbm=(), flops=0, room=32):
+def call(kernel, outs, *args, scratch=(), smem=0, hbm=False, flops=0, room=32):
     vmem = pl.BlockSpec(memory_space=pltpu.VMEM)
-    far = pl.BlockSpec(memory_space=pltpu.HBM)
-    held = far if hbm else vmem
+    held = pl.BlockSpec(memory_space=pltpu.HBM) if hbm else vmem
     return pl.pallas_call(
         kernel,
         out_shape=outs,
         in_specs=[pl.BlockSpec(memory_space=pltpu.SMEM)] * smem + [held] * (len(args) - smem),
-        out_specs=tuple(far if n in hbm else vmem for n in range(len(outs))) if isinstance(outs, tuple) else vmem,
+        out_specs=jax.tree.map(lambda _: vmem, outs),
         scratch_shapes=list(scratch),
         compiler_params=pltpu.CompilerParams(vmem_limit_bytes=room * 1024 * 1024),
         cost_estimate=pl.CostEstimate(flops=flops, bytes_accessed=2_000_000, transcendentals=0),
@@ -320,15 +302,13 @@
         front_kernel,
         outs,
         *ins,
-        hbm=(0, 1, 2),
+        hbm=True,
         room=ROOM,
-        scratch=[pltpu.VMEM(x.shape, x.dtype) for x in ins + outs[:3]] + [pltpu.SemaphoreType.DMA((11,))],
+        scratch=[pltpu.VMEM(x.shape, x.dtype) for x in ins] + [pltpu.SemaphoreType.DMA((len(ins),))],
         flops=1_000_000_000,
     )
     where = jnp.stack([lax.axis_index(a) for a in ("x", "zh", "c")]).astype(jnp.int32)
     over_x = exchange(out, ("x", "c"))
-    out = call(mid_kernel, shape((ring, 96, 128), BF), where, over_x, pay, smem=1, flops=100_000_000)
-    over_z = exchange(out, ("zh", "zl"))
     near = call(
         local_kernel,
         (shape((rows, width), F32),) * 3,
@@ -336,9 +316,11 @@
         scratch=[pltpu.VMEM((3, width, rows), F32)],
         flops=1_000_000_000,
     )
-    back = call(sets_kernel, shape((GROUP, 48, 128), BF), where, over_z, near[0], smem=1, flops=200_000_000)
+    out = call(mid_kernel, shape((ring, 96, 128), BF), where, over_x, pay, near[0], smem=1, flops=100_000_000)
+    over_z = exchange(out, ("zh", "zl"))
+    back = call(sets_kernel, shape((GROUP, 48, 128), BF), where, over_z, smem=1, flops=200_000_000)
     z = exchange(back, "zl")
-    grad = call(weight_kernel, shape((24, 128), F32), over_z, near[0], flops=1_000_000)
+    grad = call(weight_kernel, shape((24, 128), F32), over_z, flops=1_000_000)
     grad = lax.all_gather(grad, ("y", "c"), axis=0)
     grad = call(weight_end_kernel, shape((width // (blocks * ring), cols), F32), grad, flops=1_000_000)
     d_q, d_k, d_v = call(final_kernel, (shape((rows, width), BF),) * 3, z, *near, flops=300_000_000)

time: 88.3 us -> 86.7 us (0.982)
  blocking collectives: 14.2 us -> 42.5 us
  waiting for transfers between devices: 27.2 us -> 9.16 us
  starting transfers between devices: 32.4 us -> 21.9 us
  Pallas kernels: 13.3 us -> 12 us
    all_to_all x0 -> x1, blocking collectives: none -> 28.2 us  [exchange(): return lax.all_to_all(x, axes, 0, 0, tiled=True)]
    all_to_all x3 -> x2, waiting for transfers between devices: 27.2 us -> 9.16 us  [exchange(): return lax.all_to_all(x, axes, 0, 0, tiled=True)]
    all_to_all x3 -> x2, starting transfers between devices: 32.4 us -> 21.9 us  [exchange(): return lax.all_to_all(x, axes, 0, 0, tiled=True)]
    pallas_call x7, Pallas kernels: 13.3 us -> 12 us  [call(): pl.pallas_call(kernel, out_shape=outs, in_specs=[pl.BlockSpec(memory_spac...]
  transfers between devices with their start and end apart: 3 -> 2, of which waited for: 2 -> 1; matrix products, arithmetic and copies ran while one was open for 0% -> 0% of each run, Pallas kernels for 3% -> 4%
where the time goes in v5:
time: 86.7 us; the launch traced here: 86.3 us
  blocking collectives  42.5 us (49%)
  starting transfers between devices  21.9 us (25%)
  Pallas kernels  12 us (14%)
  waiting for transfers between devices  9.16 us (11%)
    all_to_all x1, blocking collectives, exchange(): return lax.all_to_all(x, axes, 0, 0, tiled=True)  28.2 us
    all_to_all x2, starting transfers between devices, exchange(): return lax.all_to_all(x, axes, 0, 0, tiled=True)  21.9 us
    all_gather x1, blocking collectives, on_device(): grad = lax.all_gather(grad, ('y', 'c'), axis=0)  14.2 us
    pallas_call x7, Pallas kernels, call(): pl.pallas_call(kernel, out_shape=outs, in_specs=[pl.BlockSpec(memory_spac...  12 us
    all_to_all x2, waiting for transfers between devices, exchange(): return lax.all_to_all(x, axes, 0, 0, tiled=True)  9.16 us
  transfers between devices with their start and end apart: 2, of which 1 were waited for; matrix products, arithmetic and copies ran while one was open for 0% of the time, Pallas kernels for 4%

profile of v5, /device:TPU:1, one launch (start us, length us, event | category | flops | bytes accessed | tf_op | source)
XLA Modules:
  0.0 86.3 jit_solution(5524964528704942445)
XLA Ops:
  0.6 4.0 %shard_map.102 = (bf16[8,352,128]{2,1,0:T(8,128)(2,1)}, bf16[256,384]{1,0:T(8,128)(2,1)}, bf16[256,256]{1,0:T(8,128)(2,1)}, f32[256,16]{1,0:T(8,128)}) custom-call(bf16[256,768]{1,0:T(8,128)(2,1)} %bitcast.22, bf16[256,384]{1,0:T(8,128)(2,1)} %bitcast.23, bf16[384,768]{1,0:T(8,128)(2,1)} %refs_2_.1, f32[8,256]{1,0:T(8,128)} %bitcast.27, ...), custom_call_target="tpu_custom_call" | custom-call | flops 1000000000 | bytes 2000000 | tf_op jit(solution)/shard_map/pallas_call | solution.py:272
  4.7 0.0 copy-start.1
  4.7 0.0 copy-start.2
  4.7 0.0 copy-start.3
  4.7 0.0 copy-start.4
  4.7 0.0 copy-start.5
  4.7 10.5 %all-to-all-start = ((bf16[8,352,128]{2,1,0:T(8,128)(2,1)}), bf16[8,352,128]{2,1,0:T(8,128)(2,1)S(1)}, u32[]{:S(2)}, u32[]{:S(2)}) async-start(bf16[8,352,128]{2,1,0:T(8,128)(2,1)} %get-tuple-element.14), calls=%async_computation | async-start | bytes 1441792 | tf_op jit(solution)/shard_map/all_to_all | solution.py:291
  15.2 0.0 copy-done.1
  15.2 0.0 copy-done.2
  15.2 0.0 copy-done.3
  15.2 0.0 copy-done.4
  15.2 0.0 copy-done.5
  15.3 0.0 copy-start
  15.3 2.3 %shard_map.103 = (f32[256,384]{1,0:T(8,128)S(1)}, f32[256,384]{1,0:T(8,128)S(1)}, f32[256,384]{1,0:T(8,128)S(1)}) custom-call(bf16[256,384]{1,0:T(8,128)(2,1)S(1)} %bitcast.17, bf16[256,384]{1,0:T(8,128)(2,1)S(1)} %bitcast.19, bf16[256,384]{1,0:T(8,128)(2,1)S(1)} %bitcast.21, bf16[256,384]{1,0:T(8,128)(2,1)S(1)} %copy-done.4, f32[256,16]{1,0:T(8,128)S(1)} %copy-done.5), custom_call_target="tpu_custom_call" | custom-call | flops 1000000000 | bytes 2000000 | tf_op jit(solution)/shard_map/pallas_call | solution.py:272
  17.6 0.1 pad_add_fusion.where_ref
  17.7 9.2 %all-to-all-done.in_ref = bf16[8,352,128]{2,1,0:T(8,128)(2,1)S(1)} async-done(((bf16[8,352,128]{2,1,0:T(8,128)(2,1)}), bf16[8,352,128]{2,1,0:T(8,128)(2,1)S(1)}, u32[]{:S(2)}, u32[]{:S(2)}) %all-to-all-start) | async-done | bytes 720928 | tf_op jit(solution)/shard_map/all_to_all | solution.py:291
  26.8 0.0 copy-done
  26.8 1.0 %shard_map.104 = bf16[16,96,128]{2,1,0:T(8,128)(2,1)S(1)} custom-call(s32[3]{0:T(128)S(1)} %pad_add_fusion.where_ref, bf16[8,352,128]{2,1,0:T(8,128)(2,1)S(1)} %all-to-all-done.in_ref, bf16[256,256]{1,0:T(8,128)(2,1)S(1)} %copy-done, f32[256,384]{1,0:T(8,128)S(1)} %get-tuple-element.18._.dq_ref), custom_call_target="tpu_custom_call" | custom-call | flops 100000000 | bytes 2000000 | tf_op jit(solution)/shard_map/pallas_call | solution.py:272
  27.9 28.2 %all_to_all.15.in_ref = bf16[16,96,128]{2,1,0:T(8,128)(2,1)S(1)} all-to-all(bf16[16,96,128]{2,1,0:T(8,128)(2,1)S(1)} %shard_map.104), channel_id=1, replica_groups=mesh['y'=4,'c'=2,'x'=4,'zh'=2,'zl'=8] {'zh','zl'}, dimensions={0} | all-to-all | bytes 786432 | tf_op jit(solution)/shard_map/all_to_all | solution.py:291
  56.1 2.6 %shard_map.105 = bf16[8,48,128]{2,1,0:T(8,128)(2,1)} custom-call(s32[3]{0:T(128)S(1)} %pad_add_fusion.where_ref, bf16[16,96,128]{2,1,0:T(8,128)(2,1)S(1)} %all_to_all.15.in_ref), custom_call_target="tpu_custom_call" | custom-call | flops 200000000 | bytes 2000000 | tf_op jit(solution)/shard_map/pallas_call | solution.py:272
  58.7 11.4 %all-to-all-start.2 = ((bf16[8,48,128]{2,1,0:T(8,128)(2,1)}), bf16[8,48,128]{2,1,0:T(8,128)(2,1)S(1)}, u32[]{:S(2)}, u32[]{:S(2)}) async-start(bf16[8,48,128]{2,1,0:T(8,128)(2,1)} %shard_map.105), calls=%async_computation.2 | async-start | bytes 196608 | tf_op jit(solution)/shard_map/all_to_all | solution.py:291
  70.1 14.2 %all-gather = f32[192,128]{1,0:T(8,128)S(1)} all-gather(f32[24,128]{1,0:T(8,128)S(1)} %shard_map.107), channel_id=2, replica_groups=mesh['y'=4,'c'=2,'x'=4,'zh'=2,'zl'=8] {'y','c'}, dimensions={0}, use_global_device_ids=true | all-gather | bytes 110592 | tf_op jit(solution)/shard_map/all_gather | solution.py:324
  84.4 0.7 shard_map.108
  85.1 0.0 all-to-all-done.2.z_ref
  85.1 1.3 %shard_map.106 = (bf16[256,384]{1,0:T(8,128)(2,1)}, bf16[256,384]{1,0:T(8,128)(2,1)}, bf16[256,384]{1,0:T(8,128)(2,1)}) custom-call(bf16[8,48,128]{2,1,0:T(8,128)(2,1)S(1)} %all-to-all-done.2.z_ref, f32[256,384]{1,0:T(8,128)S(1)} %get-tuple-element.18._.dq_ref, f32[256,384]{1,0:T(8,128)S(1)} %get-tuple-element.19.dk_ref, f32[256,384]{1,0:T(8,128)S(1)} %get-tuple-element.20.dv_ref), custom_call_target="tpu_custom_call" | custom-call | flops 300000000 | bytes 2000000 | tf_op jit(solution)/shard_map/pallas_call | solution.py:272
  (1 shorter events, 0.0 us)
Async XLA Ops:
  4.7 10.5 %copy-start.1 = (bf16[1,256,384]{2,1,0:T(8,128)(2,1)S(1)}, bf16[1,256,384]{2,1,0:T(8,128)(2,1)}, u32[]{:S(2)}) copy-start(bf16[1,256,384]{2,1,0:T(8,128)(2,1)} %param.7) | copy-start | bytes 589828
  4.7 10.5 %copy-start.2 = (bf16[1,256,384]{2,1,0:T(8,128)(2,1)S(1)}, bf16[1,256,384]{2,1,0:T(8,128)(2,1)}, u32[]{:S(2)}) copy-start(bf16[1,256,384]{2,1,0:T(8,128)(2,1)} %param.8) | copy-start | bytes 589828
  4.7 10.5 %copy-start.3 = (bf16[1,256,384]{2,1,0:T(8,128)(2,1)S(1)}, bf16[1,256,384]{2,1,0:T(8,128)(2,1)}, u32[]{:S(2)}) copy-start(bf16[1,256,384]{2,1,0:T(8,128)(2,1)} %param.9) | copy-start | bytes 589828
  4.7 10.5 %copy-start.4 = (bf16[256,384]{1,0:T(8,128)(2,1)S(1)}, bf16[256,384]{1,0:T(8,128)(2,1)}, u32[]{:S(2)}) copy-start(bf16[256,384]{1,0:T(8,128)(2,1)} %get-tuple-element.16.do_ref) | copy-start | bytes 589828
  4.7 10.5 %copy-start.5 = (f32[256,16]{1,0:T(8,128)S(1)}, f32[256,16]{1,0:T(8,128)}, u32[]{:S(2)}) copy-start(f32[256,16]{1,0:T(8,128)} %get-tuple-element.17.stat_ref) | copy-start | bytes 49156
  4.7 22.1 %all-to-all-start = ((bf16[8,352,128]{2,1,0:T(8,128)(2,1)}), bf16[8,352,128]{2,1,0:T(8,128)(2,1)S(1)}, u32[]{:S(2)}, u32[]{:S(2)}) async-start(bf16[8,352,128]{2,1,0:T(8,128)(2,1)} %get-tuple-element.14), calls=%async_computation | async-start | bytes 1441792 | tf_op jit(solution)/shard_map/all_to_all | solution.py:291
  15.3 11.6 %copy-start = (bf16[256,256]{1,0:T(8,128)(2,1)S(1)}, bf16[256,256]{1,0:T(8,128)(2,1)}, u32[]{:S(2)}) copy-start(bf16[256,256]{1,0:T(8,128)(2,1)} %get-tuple-element.15.pay_ref) | copy-start | bytes 393220
  58.7 26.3 %all-to-all-start.2 = ((bf16[8,48,128]{2,1,0:T(8,128)(2,1)}), bf16[8,48,128]{2,1,0:T(8,128)(2,1)S(1)}, u32[]{:S(2)}, u32[]{:S(2)}) async-start(bf16[8,48,128]{2,1,0:T(8,128)(2,1)} %shard_map.105), calls=%async_computation.2 | async-start | bytes 196608 | tf_op jit(solution)/shard_map/all_to_all | solution.py:291

commit v6 on v5

--- a/solution.py
+++ b/solution.py
@@ -83,7 +83,7 @@
             tail += jnp.where(lane == base + n, piece, 0.0)
             own = own - piece
     pay = jnp.concatenate([pay[:, :128], tail], axis=1).astype(BF)
-    pay_ref[...] = dot(selector(packed_token(iota((rows, 1), 0)), rows), pay, 1, 0).astype(BF)
+    pay_ref[...] = pay
     at = iota((8 * HEADS, 1), 0)
     token = 64 * (at & 3) + ((at >> 2) & 7)
     first = selector(jnp.where(at < 4 * HEADS, token, -1), rows)
@@ -98,6 +98,18 @@
         for t in range(half // 128):
             tile = grad[each * x : each * (x + 1), half * c + 128 * t : half * c + 128 * (t + 1)]
             out_ref[n, each * t : each * (t + 1)] = tile.astype(BF)
+
+
+def pack_kernel(pay_ref, out_ref):
+    rows = pay_ref.shape[0]
+    pay = dot(selector(packed_token(iota((rows, 1), 0)), rows), pay_ref[...], 1, 0)
+    for r in range(GROUP):
+        low = pay[32 * r : 32 * (r + 1), :128]
+        rest = pay[32 * r : 32 * (r + 1), 128:]
+        out_ref[r, :32] = low.astype(BF)
+        out_ref[r, 32:48] = jnp.concatenate([rest[:16, :64], rest[16:, :64]], axis=1).astype(BF)
+        stats = [jnp.zeros((16, 72), F32), rest[:16, 64:72], rest[16:, 64:72], jnp.zeros((16, 40), F32)]
+        out_ref[r, 48:] = jnp.concatenate(stats, axis=1).astype(BF)
 
 
 def mid_kernel(where_ref, in_ref, pay_ref, _, out_ref):
@@ -119,27 +131,18 @@
     to = iota((top.shape[0], 1), 0)
     source = 64 * ((to >> 2) & 3) + 32 * ((to >> 4) & 1) + 4 * (to >> 5) + (to & 3)
     top = dot(selector(source, top.shape[0]), top, 1, 0)
+    lane = iota((1, 128), 1)
     for r in range(GROUP):
-        low = pay_ref[32 * r : 32 * (r + 1), :128]
-        rest = pay_ref[32 * r : 32 * (r + 1), 128:].astype(F32)
-        pairs = jnp.concatenate([rest[:16, :64], rest[16:, :64]], axis=1).astype(BF)
         near = top[32 * r : 32 * r + 16].astype(BF)
-        mixed = [top[32 * r + 16 : 32 * (r + 1), :72], rest[:16, 64:72], rest[16:, 64:72], jnp.zeros((16, 40), F32)]
-        mixed = jnp.concatenate(mixed, axis=1)
+        mixed = jnp.where(lane < 72, top[32 * r + 16 : 32 * (r + 1)], 0.0) + pay_ref[r, 48:].astype(F32)
         for z in range(r, ring, GROUP):
-            out_ref[z, :32] = low
-            out_ref[z, 32:48] = pairs
+            out_ref[z, :48] = pay_ref[r, :48]
             out_ref[z, 48:64] = near
             out_ref[z, 64:80] = (mixed + last[16 * z : 16 * (z + 1)]).astype(BF)
             out_ref[z, 80:] = main[16 * z : 16 * (z + 1)]
 
 
-def weight_kernel(in_ref, out_ref):
-    out_ref[:16] = jnp.sum(in_ref[:, 80:].astype(F32), axis=0)
-    out_ref[16:] = jnp.sum(in_ref[:, 64:80].astype(F32), axis=0)[:8]
-
-
-def weight_end_kernel(in_ref, out_ref):
+def weight_end(in_ref, out_ref):
     each = out_ref.shape[0]
     parts = []
     for c in range(CORES):
@@ -223,7 +226,9 @@
     )
 
 
-def sets_kernel(where_ref, in_ref, back_ref):
+def sets_kernel(where_ref, in_ref, back_ref, grad_ref):
+    grad_ref[:16] = jnp.sum(in_ref[:, 80:].astype(F32), axis=0)
+    grad_ref[16:] = jnp.sum(in_ref[:, 64:80].astype(F32), axis=0)[:8]
     own = pl.ds(GROUP * where_ref[1], GROUP)
     pairs = in_ref[own, 32:48].astype(F32)
     mine = in_ref[own, 64:80].astype(F32)
@@ -239,12 +244,12 @@
     hi = in_ref[:, 64:80].reshape(256, 128)
     hi = jnp.where(iota((1, 128), 1) < 72, hi, jnp.zeros_like(hi))
     far = packed_grads(in_ref[:, 48:64].reshape(256, 128), hi)
-    row = iota((256, 1), 0)
-    here = ((row >> 7) == where_ref[1]) & (((row >> 2) & 3) == where_ref[0])
-    sel = selector(jnp.where(here, 32 * ((row >> 4) & 7) + (row & 3), -1), 256)
-    hi, lo = split(far)
-    total = (group + dot(hi, sel, 1, 0) + dot(lo, sel, 1, 0)).astype(BF)
-    total = dot(eye(256), total, 1, 1)
+    token, far_token = iota((256, 1), 0), iota((1, 256), 1)
+    match = 128 * where_ref[1] + 16 * (token >> 5) + 4 * where_ref[0] + (token & 3)
+    sel = ((far_token == match) & ((token & 31) < 4)).astype(BF)
+    turn = jnp.concatenate([eye(256), sel], axis=1)
+    hi, lo = split(jnp.concatenate([group, far], axis=1))
+    total = dot(turn, hi, 1, 1) + dot(turn, lo, 1, 1)
     for src in range(GROUP):
         rows = total[32 * src : 32 * (src + 1)]
         back_ref[src, :32] = rows[:, :128].astype(BF)
@@ -252,7 +257,8 @@
         back_ref[src, 32:] = jnp.concatenate(tail, axis=1).astype(BF)
 
 
-def final_kernel(z_ref, dq_ref, dk_ref, dv_ref, oq_ref, ok_ref, ov_ref):
+def final_kernel(z_ref, dq_ref, dk_ref, dv_ref, grad_ref, oq_ref, ok_ref, ov_ref, ow_ref):
+    weight_end(grad_ref, ow_ref)
     rows, width = dq_ref.shape
     token = iota((rows, 1), 0)
     perm_t = selector(32 * (token & 7) + 4 * ((token >> 3) & 7) + (token >> 6), rows)
@@ -309,6 +315,7 @@
     )
     where = jnp.stack([lax.axis_index(a) for a in ("x", "zh", "c")]).astype(jnp.int32)
     over_x = exchange(out, ("x", "c"))
+    pay = call(pack_kernel, shape((GROUP, 64, 128), BF), pay, flops=100_000_000)
     near = call(
         local_kernel,
         (shape((rows, width), F32),) * 3,
@@ -318,12 +325,17 @@
     )
     out = call(mid_kernel, shape((ring, 96, 128), BF), where, over_x, pay, near[0], smem=1, flops=100_000_000)
     over_z = exchange(out, ("zh", "zl"))
-    back = call(sets_kernel, shape((GROUP, 48, 128), BF), where, over_z, smem=1, flops=200_000_000)
+    back, grad = call(
+        sets_kernel, (shape((GROUP, 48, 128), BF), shape((24, 128), F32)), where, over_z, smem=1, flops=200_000_000
+    )
     z = exchange(back, "zl")
-    grad = call(weight_kernel, shape((24, 128), F32), over_z, flops=1_000_000)
     grad = lax.all_gather(grad, ("y", "c"), axis=0)
-    grad = call(weight_end_kernel, shape((width // (blocks * ring), cols), F32), grad, flops=1_000_000)
-    d_q, d_k, d_v = call(final_kernel, (shape((rows, width), BF),) * 3, z, *near, flops=300_000_000)
+    d_q, d_k, d_v, grad = call(
+        final_kernel,
+        (shape((rows, width), BF),) * 3 + (shape((width // (blocks * ring), cols), F32),),
+        z, *near, grad,
+        flops=300_000_000,
+    )
     return d_q[None], d_k[None], d_v[None], grad
 
 

time: 86.7 us -> 85.9 us (level)
  waiting for transfers between devices: 9.16 us -> 8.19 us
    all_to_all x2, waiting for transfers between devices: 9.16 us -> 8.19 us  [exchange(): return lax.all_to_all(x, axes, 0, 0, tiled=True)]
    pallas_call x7 -> x6, Pallas kernels: 12 us -> 11.5 us  [call(): pl.pallas_call(kernel, out_shape=outs, in_specs=[pl.BlockSpec(memory_spac...]
  transfers between devices with their start and end apart: 2 -> 2, of which waited for: 1 -> 1; matrix products, arithmetic and copies ran while one was open for 0% -> 0% of each run, Pallas kernels for 4% -> 3%
where the time goes in v6:
time: 85.9 us; the launch traced here: 85.6 us
  blocking collectives  42.5 us (49%)
  starting transfers between devices  21.9 us (25%)
  Pallas kernels  11.5 us (13%)
  waiting for transfers between devices  8.19 us (10%)
    all_to_all x1, blocking collectives, exchange(): return lax.all_to_all(x, axes, 0, 0, tiled=True)  28.2 us
    all_to_all x2, starting transfers between devices, exchange(): return lax.all_to_all(x, axes, 0, 0, tiled=True)  21.9 us
    all_gather x1, blocking collectives, on_device(): grad = lax.all_gather(grad, ('y', 'c'), axis=0)  14.2 us
    pallas_call x6, Pallas kernels, call(): pl.pallas_call(kernel, out_shape=outs, in_specs=[pl.BlockSpec(memory_spac...  11.5 us
    all_to_all x2, waiting for transfers between devices, exchange(): return lax.all_to_all(x, axes, 0, 0, tiled=True)  8.19 us
  transfers between devices with their start and end apart: 2, of which 1 were waited for; matrix products, arithmetic and copies ran while one was open for 0% of the time, Pallas kernels for 3%

profile of v6, /device:TPU:1, one launch (start us, length us, event | category | flops | bytes accessed | tf_op | source)
XLA Modules:
  0.0 85.6 jit_solution(10870901744147606499)
XLA Ops:
  0.6 4.0 %shard_map.102 = (bf16[8,352,128]{2,1,0:T(8,128)(2,1)}, bf16[256,384]{1,0:T(8,128)(2,1)}, bf16[256,256]{1,0:T(8,128)(2,1)}, f32[256,16]{1,0:T(8,128)}) custom-call(bf16[256,768]{1,0:T(8,128)(2,1)} %bitcast.22, bf16[256,384]{1,0:T(8,128)(2,1)} %bitcast.23, bf16[384,768]{1,0:T(8,128)(2,1)} %refs_2_.1, f32[8,256]{1,0:T(8,128)} %bitcast.27, ...), custom_call_target="tpu_custom_call" | custom-call | flops 1000000000 | bytes 2000000 | tf_op jit(solution)/shard_map/pallas_call | solution.py:278
  4.6 0.0 copy-start.3
  4.6 0.0 copy-start.2
  4.6 0.0 copy-start.4
  4.6 0.0 copy-start.5
  4.6 10.5 %all-to-all-start = ((bf16[8,352,128]{2,1,0:T(8,128)(2,1)}), bf16[8,352,128]{2,1,0:T(8,128)(2,1)S(1)}, u32[]{:S(2)}, u32[]{:S(2)}) async-start(bf16[8,352,128]{2,1,0:T(8,128)(2,1)} %get-tuple-element.17), calls=%async_computation | async-start | bytes 1441792 | tf_op jit(solution)/shard_map/all_to_all | solution.py:297
  15.1 0.0 copy-start
  15.1 0.0 copy-start.1
  15.1 0.0 copy-done.3
  15.1 0.3 shard_map.103.pay_ref
  15.4 0.0 copy-done.2
  15.4 0.0 copy-done.4
  15.4 0.0 copy-done.5
  15.4 0.6 copy-done
  16.0 0.1 copy-done.1
  16.1 2.3 %shard_map.104 = (f32[256,384]{1,0:T(8,128)S(1)}, f32[256,384]{1,0:T(8,128)S(1)}, f32[256,384]{1,0:T(8,128)S(1)}) custom-call(bf16[256,384]{1,0:T(8,128)(2,1)S(1)} %bitcast.17, bf16[256,384]{1,0:T(8,128)(2,1)S(1)} %bitcast.19, bf16[256,384]{1,0:T(8,128)(2,1)S(1)} %bitcast.21, bf16[256,384]{1,0:T(8,128)(2,1)S(1)} %copy-done.4, f32[256,16]{1,0:T(8,128)S(1)} %copy-done.5), custom_call_target="tpu_custom_call" | custom-call | flops 1000000000 | bytes 2000000 | tf_op jit(solution)/shard_map/pallas_call | solution.py:278
  18.5 0.1 pad_add_fusion.where_ref
  18.5 8.2 %all-to-all-done.in_ref = bf16[8,352,128]{2,1,0:T(8,128)(2,1)S(1)} async-done(((bf16[8,352,128]{2,1,0:T(8,128)(2,1)}), bf16[8,352,128]{2,1,0:T(8,128)(2,1)S(1)}, u32[]{:S(2)}, u32[]{:S(2)}) %all-to-all-start) | async-done | bytes 720928 | tf_op jit(solution)/shard_map/all_to_all | solution.py:297
  26.7 1.0 %shard_map.105 = bf16[16,96,128]{2,1,0:T(8,128)(2,1)S(1)} custom-call(s32[3]{0:T(128)S(1)} %pad_add_fusion.where_ref, bf16[8,352,128]{2,1,0:T(8,128)(2,1)S(1)} %all-to-all-done.in_ref, bf16[8,64,128]{2,1,0:T(8,128)(2,1)S(1)} %shard_map.103.pay_ref, f32[256,384]{1,0:T(8,128)S(1)} %get-tuple-element.21._.dq_ref), custom_call_target="tpu_custom_call" | custom-call | flops 100000000 | bytes 2000000 | tf_op jit(solution)/shard_map/pallas_call | solution.py:278
  27.7 28.2 %all_to_all.15.in_ref = bf16[16,96,128]{2,1,0:T(8,128)(2,1)S(1)} all-to-all(bf16[16,96,128]{2,1,0:T(8,128)(2,1)S(1)} %shard_map.105), channel_id=1, replica_groups=mesh['y'=4,'c'=2,'x'=4,'zh'=2,'zl'=8] {'zh','zl'}, dimensions={0} | all-to-all | bytes 786432 | tf_op jit(solution)/shard_map/all_to_all | solution.py:297
  56.0 2.7 %shard_map.106 = (bf16[8,48,128]{2,1,0:T(8,128)(2,1)}, f32[24,128]{1,0:T(8,128)S(1)}) custom-call(s32[3]{0:T(128)S(1)} %pad_add_fusion.where_ref, bf16[16,96,128]{2,1,0:T(8,128)(2,1)S(1)} %all_to_all.15.in_ref), custom_call_target="tpu_custom_call" | custom-call | flops 200000000 | bytes 2000000 | tf_op jit(solution)/shard_map/pallas_call | solution.py:278
  58.6 11.4 %all-to-all-start.2 = ((bf16[8,48,128]{2,1,0:T(8,128)(2,1)}), bf16[8,48,128]{2,1,0:T(8,128)(2,1)S(1)}, u32[]{:S(2)}, u32[]{:S(2)}) async-start(bf16[8,48,128]{2,1,0:T(8,128)(2,1)} %get-tuple-element.22), calls=%async_computation.2 | async-start | bytes 196608 | tf_op jit(solution)/shard_map/all_to_all | solution.py:297
  70.0 14.2 %all-gather = f32[192,128]{1,0:T(8,128)S(1)} all-gather(f32[24,128]{1,0:T(8,128)S(1)} %get-tuple-element.25), channel_id=2, replica_groups=mesh['y'=4,'c'=2,'x'=4,'zh'=2,'zl'=8] {'y','c'}, dimensions={0}, use_global_device_ids=true | all-gather | bytes 110592 | tf_op jit(solution)/shard_map/all_gather | solution.py:332
  84.3 0.0 all-to-all-done.2.z_ref
  84.3 1.3 %shard_map.107 = (bf16[256,384]{1,0:T(8,128)(2,1)}, bf16[256,384]{1,0:T(8,128)(2,1)}, bf16[256,384]{1,0:T(8,128)(2,1)}, f32[6,768]{1,0:T(8,128)}) custom-call(bf16[8,48,128]{2,1,0:T(8,128)(2,1)S(1)} %all-to-all-done.2.z_ref, f32[256,384]{1,0:T(8,128)S(1)} %get-tuple-element.21._.dq_ref, f32[256,384]{1,0:T(8,128)S(1)} %get-tuple-element.23.dk_ref, ...), custom_call_target="tpu_custom_call" | custom-call | flops 300000000 | bytes 2000000 | tf_op jit(solution)/shard_map/pallas_call | solution.py:278
Async XLA Ops:
  4.6 10.5 %copy-start.3 = (bf16[256,256]{1,0:T(8,128)(2,1)S(1)}, bf16[256,256]{1,0:T(8,128)(2,1)}, u32[]{:S(2)}) copy-start(bf16[256,256]{1,0:T(8,128)(2,1)} %get-tuple-element.18.pay_ref) | copy-start | bytes 393220
  4.6 10.8 %copy-start.2 = (bf16[1,256,384]{2,1,0:T(8,128)(2,1)S(1)}, bf16[1,256,384]{2,1,0:T(8,128)(2,1)}, u32[]{:S(2)}) copy-start(bf16[1,256,384]{2,1,0:T(8,128)(2,1)} %param.9) | copy-start | bytes 589828
  4.6 10.8 %copy-start.4 = (bf16[256,384]{1,0:T(8,128)(2,1)S(1)}, bf16[256,384]{1,0:T(8,128)(2,1)}, u32[]{:S(2)}) copy-start(bf16[256,384]{1,0:T(8,128)(2,1)} %get-tuple-element.19.do_ref) | copy-start | bytes 589828
  4.6 10.8 %copy-start.5 = (f32[256,16]{1,0:T(8,128)S(1)}, f32[256,16]{1,0:T(8,128)}, u32[]{:S(2)}) copy-start(f32[256,16]{1,0:T(8,128)} %get-tuple-element.20.stat_ref) | copy-start | bytes 49156
  4.6 22.1 %all-to-all-start = ((bf16[8,352,128]{2,1,0:T(8,128)(2,1)}), bf16[8,352,128]{2,1,0:T(8,128)(2,1)S(1)}, u32[]{:S(2)}, u32[]{:S(2)}) async-start(bf16[8,352,128]{2,1,0:T(8,128)(2,1)} %get-tuple-element.17), calls=%async_computation | async-start | bytes 1441792 | tf_op jit(solution)/shard_map/all_to_all | solution.py:297
  15.1 0.9 %copy-start = (bf16[1,256,384]{2,1,0:T(8,128)(2,1)S(1)}, bf16[1,256,384]{2,1,0:T(8,128)(2,1)}, u32[]{:S(2)}) copy-start(bf16[1,256,384]{2,1,0:T(8,128)(2,1)} %param.7) | copy-start | bytes 589828
  15.1 1.0 %copy-start.1 = (bf16[1,256,384]{2,1,0:T(8,128)(2,1)S(1)}, bf16[1,256,384]{2,1,0:T(8,128)(2,1)}, u32[]{:S(2)}) copy-start(bf16[1,256,384]{2,1,0:T(8,128)(2,1)} %param.8) | copy-start | bytes 589828
  58.6 25.6 %all-to-all-start.2 = ((bf16[8,48,128]{2,1,0:T(8,128)(2,1)}), bf16[8,48,128]{2,1,0:T(8,128)(2,1)S(1)}, u32[]{:S(2)}, u32[]{:S(2)}) async-start(bf16[8,48,128]{2,1,0:T(8,128)(2,1)} %get-tuple-element.22), calls=%async_computation.2 | async-start | bytes 196608 | tf_op jit(solution)/shard_map/all_to_all | solution.py:297

commit v7 on v6

--- a/solution.py
+++ b/solution.py
@@ -47,6 +47,16 @@
 
 def selector(source, count):
     return (iota((source.shape[0], count), 1) == source).astype(BF)
+
+
+def stat_lanes(x):
+    row, lane = iota((128, 1), 0), iota((1, 128), 1)
+    return dot(x, ((row >= 64) & (row < 72) & ((row & 7) == (lane & 7))).astype(BF), 1, 0)
+
+
+def stat_rows(rows_of, source, group):
+    x = dot(selector(source, rows_of.shape[0]), rows_of, 1, 0)
+    return jnp.where((iota((1, 128), 1) >> 3) == group, x, 0.0).astype(BF)
 
 
 def front_kernel(*refs):
@@ -76,19 +86,28 @@
     pick = iota((1, HEADS), 1) == (iota((rows, 1), 0) & (GROUP - 1))
     lane = iota((rows, 128), 1)
     tail = pay[:, 128:]
+    wide = jnp.zeros_like(tail)
     for base, x in ((64, lse), (67, delta)):
         own = jnp.sum(jnp.where(pick, x, 0.0), axis=1, keepdims=True)
         for n in range(3):
             piece = own.astype(BF).astype(F32)
             tail += jnp.where(lane == base + n, piece, 0.0)
+            wide += jnp.where((lane & 7) == base + n - 64, piece, 0.0)
             own = own - piece
     pay = jnp.concatenate([pay[:, :128], tail], axis=1).astype(BF)
     pay_ref[...] = pay
-    at = iota((8 * HEADS, 1), 0)
-    token = 64 * (at & 3) + ((at >> 2) & 7)
-    first = selector(jnp.where(at < 4 * HEADS, token, -1), rows)
-    second = selector(jnp.where(at < 4 * HEADS, -1, token), rows)
-    top = (dot(first, pay[:, :128], 1, 0) + dot(second, pay[:, 128:], 1, 0)).astype(BF)
+    lane = iota((1, 128), 1)
+    at = iota((4 * HEADS, 1), 0)
+    low = dot(selector(64 * (at & 3) + (at >> 2), rows), pay[:, :128], 1, 0)
+    at = iota((2 * HEADS, 1), 0)
+    token = 64 * (at & 1) + (at >> 1)
+    hi = jnp.where(lane < 64, tail, 0.0)
+    high = dot(selector(token, rows), hi.astype(BF), 1, 0)
+    hi = jnp.concatenate([hi[:, 64:], hi[:, :64]], axis=1)
+    high += dot(selector(token + 128, rows), hi.astype(BF), 1, 0)
+    wide = jnp.where(((lane >> 3) & 3) == (iota((rows, 1), 0) >> 6), wide, 0.0).astype(BF)
+    picked = ((iota((1, rows), 1) & 63) == iota((2 * HEADS, 1), 0)) & (iota((2 * HEADS, 1), 0) < HEADS)
+    top = jnp.concatenate([low, high, dot(picked.astype(BF), wide, 1, 0)], axis=0).astype(BF)
     for n in range(parts):
         out_ref[n, count:] = top
     each, half = width * CORES // parts, cols // CORES
@@ -103,13 +122,18 @@
 def pack_kernel(pay_ref, out_ref):
     rows = pay_ref.shape[0]
     pay = dot(selector(packed_token(iota((rows, 1), 0)), rows), pay_ref[...], 1, 0)
+    lane = iota((1, 128), 1)
+    token = iota((rows, 1), 0)
+    wide = stat_lanes(pay[:, 128:].astype(BF))
+    wide = jnp.where((lane >> 3) == (token & 15), wide, 0.0).astype(BF)
+    at, source = iota((40 * GROUP, 1), 0), iota((1, rows), 1)
+    r = lax.div(at, 40)
+    stats = dot(((at - 40 * r == 19 + ((source >> 4) & 1)) & (r == (source >> 5))).astype(BF), wide, 1, 0)
     for r in range(GROUP):
         low = pay[32 * r : 32 * (r + 1), :128]
         rest = pay[32 * r : 32 * (r + 1), 128:]
-        out_ref[r, :32] = low.astype(BF)
-        out_ref[r, 32:48] = jnp.concatenate([rest[:16, :64], rest[16:, :64]], axis=1).astype(BF)
-        stats = [jnp.zeros((16, 72), F32), rest[:16, 64:72], rest[16:, 64:72], jnp.zeros((16, 40), F32)]
-        out_ref[r, 48:] = jnp.concatenate(stats, axis=1).astype(BF)
+        pairs = jnp.concatenate([rest[:16, :64], rest[16:, :64]], axis=1)
+        out_ref[r] = jnp.concatenate([low, pairs, stats[40 * r : 40 * (r + 1)]], axis=0).astype(BF)
 
 
 def mid_kernel(where_ref, in_ref, pay_ref, _, out_ref):
@@ -118,28 +142,30 @@
     sums = jnp.sum(in_ref[:, :count].astype(F32), axis=0).astype(BF)
     each = count // 3
     few = each // ring
-    to = iota((16 * ring, 1), 0)
-    z, q = to >> 4, to & 15
+    at = iota((40 * ring, 1), 0)
+    z = lax.div(at, 40)
+    q = at - 40 * z - 22
     t = (q * 43) >> 8
-    main = dot(selector(each * t + few * z + q - few * t, count), sums, 1, 0).astype(BF)
-    last = selector(jnp.where(q < 8, 2 * each + few * z + 4 + (q & 1), -1), count)
-    last = dot(last, sums, 1, 0)
+    grad = dot(selector(jnp.where(q < 0, -1, each * t + few * z + q - few * t), count), sums, 1, 0)
     lane = iota((1, 128), 1)
-    last = jnp.where((lane >> 5) == (q >> 1), last, 0.0).astype(BF)
-    last = dot(last, selector(96 + (iota((128, 1), 0) & 31), 128), 1, 0)
-    top = jnp.concatenate([in_ref[CORES * x + where_ref[2], count:] for x in range(4)], axis=0)
-    to = iota((top.shape[0], 1), 0)
-    source = 64 * ((to >> 2) & 3) + 32 * ((to >> 4) & 1) + 4 * (to >> 5) + (to & 3)
-    top = dot(selector(source, top.shape[0]), top, 1, 0)
-    lane = iota((1, 128), 1)
+    tops = []
+    for k in range(3):
+        top = in_ref[CORES * ((where_ref[0] + 1 + k) & 3) + where_ref[2], count:]
+        tops += [top[:48], jnp.where((lane >> 5) == k, top[48:], jnp.zeros_like(top[48:]))]
+    at, source = iota((40 * GROUP, 1), 0), iota((1, 192), 1)
+    r = lax.div(at, 40)
+    at = at - 40 * r
+    h = (at >= 6).astype(jnp.int32)
+    low = 64 * ((at - 6 * h) >> 1) + 4 * r + (at & 1) + 2 * h
+    high = 64 * ((at - 12) >> 1) + 32 + 2 * r + (at & 1)
+    row = jnp.where(at < 12, low, jnp.where(at < 18, high, -1))
+    sel = (source == row) | ((at == 18) & ((source & 63) == 48 + r))
+    top = dot(sel.astype(BF), jnp.concatenate(tops, axis=0), 1, 0)
     for r in range(GROUP):
-        near = top[32 * r : 32 * r + 16].astype(BF)
-        mixed = jnp.where(lane < 72, top[32 * r + 16 : 32 * (r + 1)], 0.0) + pay_ref[r, 48:].astype(F32)
+        own = pay_ref[r].astype(F32)
         for z in range(r, ring, GROUP):
-            out_ref[z, :48] = pay_ref[r, :48]
-            out_ref[z, 48:64] = near
-            out_ref[z, 64:80] = (mixed + last[16 * z : 16 * (z + 1)]).astype(BF)
-            out_ref[z, 80:] = main[16 * z : 16 * (z + 1)]
+            rest = own[48:] + top[40 * r : 40 * (r + 1)] + grad[40 * z : 40 * (z + 1)]
+            out_ref[z] = jnp.concatenate([own[:48], rest], axis=0).astype(BF)
 
 
 def weight_end(in_ref, out_ref):
@@ -149,9 +175,7 @@
         total = in_ref[c]
         for y in range(1, in_ref.shape[0] // CORES):
             total = total + in_ref[CORES * y + c]
-        last = jnp.concatenate([total[16 + 2 * k : 18 + 2 * k, 96:] for k in range(4)], axis=1)
-        total = jnp.concatenate([total[:16], last], axis=0)
-        parts += [total[each * t : each * (t + 1)] for t in range(3)]
+        parts += [total[each * (t + 1) : each * (t + 2)] for t in range(3)]
     out_ref[...] = jnp.concatenate(parts, axis=1)
 
 
@@ -205,16 +229,16 @@
         out[...] = jnp.transpose(t_ref[n])
 
 
-def packed_grads(lo, hi):
+def packed_grads(lo, hi, stat):
     scale = float(HD) ** -0.5
     one = eye(128)
     x_t = jnp.concatenate([dot(one, lo, 1, 1), dot(one, hi, 1, 1)], axis=0).astype(BF)
     q_t, k_t, v_t, do_t = (x_t[HD * n : HD * (n + 1)] for n in range(4))
-    row = iota((64, 256), 0)
-    lse = dot(hi, jnp.concatenate([jnp.zeros((64, 256), BF), (row < 3).astype(BF)], axis=0), 1, 0)
-    minus = jnp.where((row >= 3) & (row < 6), -1.0, 0.0).astype(BF)
+    piece = iota((128, 256), 0) & 7
+    lse = dot(stat, (piece < 3).astype(BF), 1, 0)
+    minus = jnp.where((piece >= 3) & (piece < 6), -1.0, 0.0).astype(BF)
     probs = jnp.exp(dot(lo, padded(k_t, 0, 128), 1, 0) * scale - lse)
-    d_probs = dot(hi, jnp.concatenate([jnp.zeros((16, 256), BF), v_t, minus], axis=0), 1, 0)
+    d_probs = dot(jnp.concatenate([hi, stat], axis=1), jnp.concatenate([padded(v_t, 16, 128), minus], axis=0), 1, 0)
     d_scores = (probs * d_probs).astype(BF)
     return jnp.concatenate(
         [
@@ -227,25 +251,30 @@
 
 
 def sets_kernel(where_ref, in_ref, back_ref, grad_ref):
-    grad_ref[:16] = jnp.sum(in_ref[:, 80:].astype(F32), axis=0)
-    grad_ref[16:] = jnp.sum(in_ref[:, 64:80].astype(F32), axis=0)[:8]
     own = pl.ds(GROUP * where_ref[1], GROUP)
+    rest = in_ref[:, 48:].astype(F32)
+    grad_ref[...] = jnp.sum(rest[:, 16:], axis=0)
+    blank = jnp.zeros((256, 64), F32)
+    token = iota((256, 1), 0)
+    mine = in_ref[own, 48:].astype(F32)[:, 16:24].reshape(8 * GROUP, 128).astype(BF)
+    stat = stat_rows(mine, 8 * (token >> 5) + 3 + ((token >> 4) & 1), token & 15)
     pairs = in_ref[own, 32:48].astype(F32)
-    mine = in_ref[own, 64:80].astype(F32)
-    blank = jnp.zeros((GROUP, 16, 56), F32)
-    hi = jnp.concatenate(
-        [
-            jnp.concatenate([pairs[:, :, :64], mine[:, :, 72:80], blank], axis=2),
-            jnp.concatenate([pairs[:, :, 64:], mine[:, :, 80:88], blank], axis=2),
-        ],
-        axis=1,
-    )
-    group = packed_grads(in_ref[own, :32].reshape(256, 128), hi.reshape(256, 128).astype(BF))
-    hi = in_ref[:, 64:80].reshape(256, 128)
-    hi = jnp.where(iota((1, 128), 1) < 72, hi, jnp.zeros_like(hi))
-    far = packed_grads(in_ref[:, 48:64].reshape(256, 128), hi)
-    token, far_token = iota((256, 1), 0), iota((1, 256), 1)
-    match = 128 * where_ref[1] + 16 * (token >> 5) + 4 * where_ref[0] + (token & 3)
+    hi = jnp.concatenate([pairs[:, :, :64], pairs[:, :, 64:]], axis=1).reshape(256, 64)
+    hi = jnp.concatenate([hi, blank], axis=1)
+    group = packed_grads(in_ref[own, :32].reshape(256, 128), hi.astype(BF), stat)
+    n = token & 15
+    h = (n >= 6).astype(jnp.int32)
+    lanes = jnp.where(n < 12, 4 * ((n - 6 * h) >> 1) + (n & 1) + 2 * h, n - 12)
+    stat = stat_rows(
+        rest[:, 16:24].reshape(128, 128).astype(BF), 8 * (token >> 4) + 2 + (n >= 12).astype(jnp.int32), lanes
+    )
+    lo = jnp.concatenate([rest[:, :12], in_ref[:, :16].astype(F32)[:, :4]], axis=1).reshape(256, 128)
+    first = in_ref[:, 32:48].astype(F32)[:, :4, :64]
+    hi = jnp.concatenate([rest[:, 12:18, :64], rest[:, 12:18, 64:], first], axis=1).reshape(256, 64)
+    hi = jnp.concatenate([hi, blank], axis=1)
+    far = packed_grads(lo.astype(BF), hi.astype(BF), stat)
+    far_token = iota((1, 256), 1)
+    match = 128 * where_ref[1] + 16 * (token >> 5) + 12 + (token & 3)
     sel = ((far_token == match) & ((token & 31) < 4)).astype(BF)
     turn = jnp.concatenate([eye(256), sel], axis=1)
     hi, lo = split(jnp.concatenate([group, far], axis=1))
@@ -315,7 +344,7 @@
     )
     where = jnp.stack([lax.axis_index(a) for a in ("x", "zh", "c")]).astype(jnp.int32)
     over_x = exchange(out, ("x", "c"))
-    pay = call(pack_kernel, shape((GROUP, 64, 128), BF), pay, flops=100_000_000)
+    pay = call(pack_kernel, shape((GROUP, 88, 128), BF), pay, flops=100_000_000)
     near = call(
         local_kernel,
         (shape((rows, width), F32),) * 3,
@@ -323,7 +352,7 @@
         scratch=[pltpu.VMEM((3, width, rows), F32)],
         flops=1_000_000_000,
     )
-    out = call(mid_kernel, shape((ring, 96, 128), BF), where, over_x, pay, near[0], smem=1, flops=100_000_000)
+    out = call(mid_kernel, shape((ring, 88, 128), BF), where, over_x, pay, near[0], smem=1, flops=100_000_000)
     over_z = exchange(out, ("zh", "zl"))
     back, grad = call(
         sets_kernel, (shape((GROUP, 48, 128), BF), shape((24, 128), F32)), where, over_z, smem=1, flops=200_000_000

time: 85.9 us -> 84.8 us (0.987)
  blocking collectives: 42.5 us -> 40.6 us
    all_to_all x1, blocking collectives: 28.2 us -> 26.4 us  [exchange(): return lax.all_to_all(x, axes, 0, 0, tiled=True)]
where the time goes in v7:
time: 84.8 us; the launch traced here: 84.5 us
  blocking collectives  40.6 us (48%)
  starting transfers between devices  22.3 us (26%)
  Pallas kernels  12.1 us (14%)
  waiting for transfers between devices  8.18 us (10%)
    all_to_all x1, blocking collectives, exchange(): return lax.all_to_all(x, axes, 0, 0, tiled=True)  26.4 us
    all_to_all x2, starting transfers between devices, exchange(): return lax.all_to_all(x, axes, 0, 0, tiled=True)  22.3 us
    all_gather x1, blocking collectives, on_device(): grad = lax.all_gather(grad, ('y', 'c'), axis=0)  14.2 us
    pallas_call x6, Pallas kernels, call(): pl.pallas_call(kernel, out_shape=outs, in_specs=[pl.BlockSpec(memory_spac...  12.1 us
    all_to_all x2, waiting for transfers between devices, exchange(): return lax.all_to_all(x, axes, 0, 0, tiled=True)  8.18 us
  transfers between devices with their start and end apart: 2, of which 1 were waited for; matrix products, arithmetic and copies ran while one was open for 0% of the time, Pallas kernels for 3%

profile of v7, /device:TPU:1, one launch (start us, length us, event | category | flops | bytes accessed | tf_op | source)
XLA Modules:
  0.0 84.5 jit_solution(8475679924552892635)
XLA Ops:
  0.6 4.1 %shard_map.102 = (bf16[8,352,128]{2,1,0:T(8,128)(2,1)}, bf16[256,384]{1,0:T(8,128)(2,1)}, bf16[256,256]{1,0:T(8,128)(2,1)}, f32[256,16]{1,0:T(8,128)}) custom-call(bf16[256,768]{1,0:T(8,128)(2,1)} %bitcast.22, bf16[256,384]{1,0:T(8,128)(2,1)} %bitcast.23, bf16[384,768]{1,0:T(8,128)(2,1)} %refs_2_.1, f32[8,256]{1,0:T(8,128)} %bitcast.27, ...), custom_call_target="tpu_custom_call" | custom-call | flops 1000000000 | bytes 2000000 | tf_op jit(solution)/shard_map/pallas_call | solution.py:307
  4.7 0.0 copy-start.3
  4.7 0.0 copy-start.2
  4.7 0.0 copy-start.4
  4.7 0.0 copy-start.5
  4.7 10.5 %all-to-all-start = ((bf16[8,352,128]{2,1,0:T(8,128)(2,1)}), bf16[8,352,128]{2,1,0:T(8,128)(2,1)S(1)}, u32[]{:S(2)}, u32[]{:S(2)}) async-start(bf16[8,352,128]{2,1,0:T(8,128)(2,1)} %get-tuple-element.17), calls=%async_computation | async-start | bytes 1441792 | tf_op jit(solution)/shard_map/all_to_all | solution.py:326
  15.2 0.0 copy-start
  15.2 0.0 copy-start.1
  15.2 0.0 copy-done.3
  15.2 0.5 shard_map.103.pay_ref
  15.8 0.0 copy-done.2
  15.8 0.0 copy-done.4
  15.8 0.0 copy-done.5
  15.8 0.4 copy-done
  16.1 0.1 copy-done.1
  16.2 2.3 %shard_map.104 = (f32[256,384]{1,0:T(8,128)S(1)}, f32[256,384]{1,0:T(8,128)S(1)}, f32[256,384]{1,0:T(8,128)S(1)}) custom-call(bf16[256,384]{1,0:T(8,128)(2,1)S(1)} %bitcast.17, bf16[256,384]{1,0:T(8,128)(2,1)S(1)} %bitcast.19, bf16[256,384]{1,0:T(8,128)(2,1)S(1)} %bitcast.21, bf16[256,384]{1,0:T(8,128)(2,1)S(1)} %copy-done.4, f32[256,16]{1,0:T(8,128)S(1)} %copy-done.5), custom_call_target="tpu_custom_call" | custom-call | flops 1000000000 | bytes 2000000 | tf_op jit(solution)/shard_map/pallas_call | solution.py:307
  18.6 0.1 pad_add_fusion.where_ref
  18.6 8.2 %all-to-all-done.in_ref = bf16[8,352,128]{2,1,0:T(8,128)(2,1)S(1)} async-done(((bf16[8,352,128]{2,1,0:T(8,128)(2,1)}), bf16[8,352,128]{2,1,0:T(8,128)(2,1)S(1)}, u32[]{:S(2)}, u32[]{:S(2)}) %all-to-all-start) | async-done | bytes 720928 | tf_op jit(solution)/shard_map/all_to_all | solution.py:326
  26.8 1.2 %shard_map.105 = bf16[16,88,128]{2,1,0:T(8,128)(2,1)S(1)} custom-call(s32[3]{0:T(128)S(1)} %pad_add_fusion.where_ref, bf16[8,352,128]{2,1,0:T(8,128)(2,1)S(1)} %all-to-all-done.in_ref, bf16[8,88,128]{2,1,0:T(8,128)(2,1)S(1)} %shard_map.103.pay_ref, f32[256,384]{1,0:T(8,128)S(1)} %get-tuple-element.21._.dq_ref), custom_call_target="tpu_custom_call" | custom-call | flops 100000000 | bytes 2000000 | tf_op jit(solution)/shard_map/pallas_call | solution.py:307
  28.0 26.4 %all_to_all.15.in_ref = bf16[16,88,128]{2,1,0:T(8,128)(2,1)S(1)} all-to-all(bf16[16,88,128]{2,1,0:T(8,128)(2,1)S(1)} %shard_map.105), channel_id=1, replica_groups=mesh['y'=4,'c'=2,'x'=4,'zh'=2,'zl'=8] {'zh','zl'}, dimensions={0} | all-to-all | bytes 720896 | tf_op jit(solution)/shard_map/all_to_all | solution.py:326
  54.4 2.7 %shard_map.106 = (bf16[8,48,128]{2,1,0:T(8,128)(2,1)}, f32[24,128]{1,0:T(8,128)S(1)}) custom-call(s32[3]{0:T(128)S(1)} %pad_add_fusion.where_ref, bf16[16,88,128]{2,1,0:T(8,128)(2,1)S(1)} %all_to_all.15.in_ref), custom_call_target="tpu_custom_call" | custom-call | flops 200000000 | bytes 2000000 | tf_op jit(solution)/shard_map/pallas_call | solution.py:307
  57.1 11.9 %all-to-all-start.2 = ((bf16[8,48,128]{2,1,0:T(8,128)(2,1)}), bf16[8,48,128]{2,1,0:T(8,128)(2,1)S(1)}, u32[]{:S(2)}, u32[]{:S(2)}) async-start(bf16[8,48,128]{2,1,0:T(8,128)(2,1)} %get-tuple-element.22), calls=%async_computation.2 | async-start | bytes 196608 | tf_op jit(solution)/shard_map/all_to_all | solution.py:326
  69.0 14.2 %all-gather = f32[192,128]{1,0:T(8,128)S(1)} all-gather(f32[24,128]{1,0:T(8,128)S(1)} %get-tuple-element.25), channel_id=2, replica_groups=mesh['y'=4,'c'=2,'x'=4,'zh'=2,'zl'=8] {'y','c'}, dimensions={0}, use_global_device_ids=true | all-gather | bytes 110592 | tf_op jit(solution)/shard_map/all_gather | solution.py:361
  83.1 0.0 all-to-all-done.2.z_ref
  83.1 1.3 %shard_map.107 = (bf16[256,384]{1,0:T(8,128)(2,1)}, bf16[256,384]{1,0:T(8,128)(2,1)}, bf16[256,384]{1,0:T(8,128)(2,1)}, f32[6,768]{1,0:T(8,128)}) custom-call(bf16[8,48,128]{2,1,0:T(8,128)(2,1)S(1)} %all-to-all-done.2.z_ref, f32[256,384]{1,0:T(8,128)S(1)} %get-tuple-element.21._.dq_ref, f32[256,384]{1,0:T(8,128)S(1)} %get-tuple-element.23.dk_ref, ...), custom_call_target="tpu_custom_call" | custom-call | flops 300000000 | bytes 2000000 | tf_op jit(solution)/shard_map/pallas_call | solution.py:307
Async XLA Ops:
  4.7 10.5 %copy-start.3 = (bf16[256,256]{1,0:T(8,128)(2,1)S(1)}, bf16[256,256]{1,0:T(8,128)(2,1)}, u32[]{:S(2)}) copy-start(bf16[256,256]{1,0:T(8,128)(2,1)} %get-tuple-element.18.pay_ref) | copy-start | bytes 393220
  4.7 11.0 %copy-start.2 = (bf16[1,256,384]{2,1,0:T(8,128)(2,1)S(1)}, bf16[1,256,384]{2,1,0:T(8,128)(2,1)}, u32[]{:S(2)}) copy-start(bf16[1,256,384]{2,1,0:T(8,128)(2,1)} %param.9) | copy-start | bytes 589828
  4.7 11.0 %copy-start.4 = (bf16[256,384]{1,0:T(8,128)(2,1)S(1)}, bf16[256,384]{1,0:T(8,128)(2,1)}, u32[]{:S(2)}) copy-start(bf16[256,384]{1,0:T(8,128)(2,1)} %get-tuple-element.19.do_ref) | copy-start | bytes 589828
  4.7 11.0 %copy-start.5 = (f32[256,16]{1,0:T(8,128)S(1)}, f32[256,16]{1,0:T(8,128)}, u32[]{:S(2)}) copy-start(f32[256,16]{1,0:T(8,128)} %get-tuple-element.20.stat_ref) | copy-start | bytes 49156
  4.7 22.1 %all-to-all-start = ((bf16[8,352,128]{2,1,0:T(8,128)(2,1)}), bf16[8,352,128]{2,1,0:T(8,128)(2,1)S(1)}, u32[]{:S(2)}, u32[]{:S(2)}) async-start(bf16[8,352,128]{2,1,0:T(8,128)(2,1)} %get-tuple-element.17), calls=%async_computation | async-start | bytes 1441792 | tf_op jit(solution)/shard_map/all_to_all | solution.py:326
  15.2 0.9 %copy-start = (bf16[1,256,384]{2,1,0:T(8,128)(2,1)S(1)}, bf16[1,256,384]{2,1,0:T(8,128)(2,1)}, u32[]{:S(2)}) copy-start(bf16[1,256,384]{2,1,0:T(8,128)(2,1)} %param.7) | copy-start | bytes 589828
  15.2 1.0 %copy-start.1 = (bf16[1,256,384]{2,1,0:T(8,128)(2,1)S(1)}, bf16[1,256,384]{2,1,0:T(8,128)(2,1)}, u32[]{:S(2)}) copy-start(bf16[1,256,384]{2,1,0:T(8,128)(2,1)} %param.8) | copy-start | bytes 589828
  57.1 26.1 %all-to-all-start.2 = ((bf16[8,48,128]{2,1,0:T(8,128)(2,1)}), bf16[8,48,128]{2,1,0:T(8,128)(2,1)S(1)}, u32[]{:S(2)}, u32[]{:S(2)}) async-start(bf16[8,48,128]{2,1,0:T(8,128)(2,1)} %get-tuple-element.22), calls=%async_computation.2 | async-start | bytes 196608 | tf_op jit(solution)/shard_map/all_to_all | solution.py:326

commit v8 on v7

--- a/solution.py
+++ b/solution.py
@@ -49,9 +49,12 @@
     return (iota((source.shape[0], count), 1) == source).astype(BF)
 
 
-def stat_lanes(x):
-    row, lane = iota((128, 1), 0), iota((1, 128), 1)
-    return dot(x, ((row >= 64) & (row < 72) & ((row & 7) == (lane & 7))).astype(BF), 1, 0)
+def pieces(x):
+    parts = []
+    for _ in range(3):
+        parts.append(x.astype(BF).astype(F32))
+        x = x - parts[-1]
+    return parts
 
 
 def stat_rows(rows_of, source, group):
@@ -60,7 +63,7 @@
 
 
 def front_kernel(*refs):
-    hbm, (out_ref, do_ref, pay_ref, stat_ref), vmem, sems = refs[:7], refs[7:11], refs[11:18], refs[18]
+    hbm, (out_ref, do_ref, stat_ref), vmem, sems = refs[:7], refs[7:10], refs[10:17], refs[17]
     copies = [pltpu.make_async_copy(a, b, sems.at[n]) for n, (a, b) in enumerate(zip(hbm, vmem))]
     for copy in copies:
         copy.start()
@@ -69,7 +72,7 @@
     cols = dy_ref.shape[1]
     parts = out_ref.shape[0]
     count = width * cols // parts // 128
-    for copy in copies:
+    for copy in copies[:4]:
         copy.wait()
     out, dy = o_ref[...], dy_ref[...]
     d_out = dot(dy, w_ref[...], 1, 1).astype(BF)
@@ -79,37 +82,6 @@
     delta = (dot(hi, heads, 1, 0) + dot(lo, heads, 1, 0))[:, :HEADS]
     lse = jnp.transpose(lse_ref[...])
     stat_ref[...] = jnp.concatenate([delta, lse], axis=1)
-    mine = own_head(rows, width)
-    pay = jnp.zeros((rows, 256), F32)
-    for part, x in enumerate((q_ref[...], k_ref[...], v_ref[...], d_out)):
-        pay += dot(jnp.where(mine, x, jnp.zeros_like(x)), spread(part, 256, width), 1, 0)
-    pick = iota((1, HEADS), 1) == (iota((rows, 1), 0) & (GROUP - 1))
-    lane = iota((rows, 128), 1)
-    tail = pay[:, 128:]
-    wide = jnp.zeros_like(tail)
-    for base, x in ((64, lse), (67, delta)):
-        own = jnp.sum(jnp.where(pick, x, 0.0), axis=1, keepdims=True)
-        for n in range(3):
-            piece = own.astype(BF).astype(F32)
-            tail += jnp.where(lane == base + n, piece, 0.0)
-            wide += jnp.where((lane & 7) == base + n - 64, piece, 0.0)
-            own = own - piece
-    pay = jnp.concatenate([pay[:, :128], tail], axis=1).astype(BF)
-    pay_ref[...] = pay
-    lane = iota((1, 128), 1)
-    at = iota((4 * HEADS, 1), 0)
-    low = dot(selector(64 * (at & 3) + (at >> 2), rows), pay[:, :128], 1, 0)
-    at = iota((2 * HEADS, 1), 0)
-    token = 64 * (at & 1) + (at >> 1)
-    hi = jnp.where(lane < 64, tail, 0.0)
-    high = dot(selector(token, rows), hi.astype(BF), 1, 0)
-    hi = jnp.concatenate([hi[:, 64:], hi[:, :64]], axis=1)
-    high += dot(selector(token + 128, rows), hi.astype(BF), 1, 0)
-    wide = jnp.where(((lane >> 3) & 3) == (iota((rows, 1), 0) >> 6), wide, 0.0).astype(BF)
-    picked = ((iota((1, rows), 1) & 63) == iota((2 * HEADS, 1), 0)) & (iota((2 * HEADS, 1), 0) < HEADS)
-    top = jnp.concatenate([low, high, dot(picked.astype(BF), wide, 1, 0)], axis=0).astype(BF)
-    for n in range(parts):
-        out_ref[n, count:] = top
     each, half = width * CORES // parts, cols // CORES
     grad = dot(out, dy, 0, 0)
     for n in range(parts):
@@ -117,14 +89,49 @@
         for t in range(half // 128):
             tile = grad[each * x : each * (x + 1), half * c + 128 * t : half * c + 128 * (t + 1)]
             out_ref[n, each * t : each * (t + 1)] = tile.astype(BF)
-
-
-def pack_kernel(pay_ref, out_ref):
-    rows = pay_ref.shape[0]
-    pay = dot(selector(packed_token(iota((rows, 1), 0)), rows), pay_ref[...], 1, 0)
+    for copy in copies[4:]:
+        copy.wait()
+    at = iota((4 * HEADS, 1), 0)
+    lane = iota((1, 128), 1)
+    sel = selector(64 * (at & 3) + (at >> 2), rows)
+    mine = lax.div(iota((1, width), 1), HD) == (at >> 2)
+    pay = jnp.zeros((4 * HEADS, 256), F32)
+    for part, x in enumerate((q_ref[...], k_ref[...], v_ref[...], d_out)):
+        x = jnp.where(mine, dot(sel, x, 1, 0), 0.0).astype(BF)
+        pay += dot(x, spread(part, 256, width), 1, 0)
+    hi = jnp.where(lane < 64, pay[:, 128:], 0.0)
+    swapped = jnp.concatenate([hi[:, 64:], hi[:, :64]], axis=1)
+    row = iota((2 * HEADS, 1), 0)
+    row = 4 * (row >> 1) + (row & 1)
+    high = dot(selector(row, 4 * HEADS), hi.astype(BF), 1, 0)
+    high += dot(selector(row + 2, 4 * HEADS), swapped.astype(BF), 1, 0)
+    few = dot(sel, jnp.concatenate(pieces(lse) + pieces(delta), axis=1).astype(BF), 1, 0)
+    few = jnp.where((iota((1, 6 * HEADS), 1) & 7) == (at >> 2), few, 0.0).astype(BF)
+    wide = dot(few, ((iota((6 * HEADS, 1), 0) >> 3) == (lane & 7)).astype(BF), 1, 0)
+    wide = jnp.where(((lane >> 3) & 3) == (at & 3), wide, 0.0).astype(BF)
+    picked = (iota((1, 4 * HEADS), 1) >> 2) == iota((2 * HEADS, 1), 0)
+    top = jnp.concatenate([pay[:, :128], high, dot(picked.astype(BF), wide, 1, 0)], axis=0).astype(BF)
+    for n in range(parts):
+        out_ref[n, count:] = top
+
+
+def pack_kernel(q_ref, k_ref, v_ref, do_ref, stat_ref, out_ref):
+    rows, width = q_ref.shape
+    order = selector(packed_token(iota((rows, 1), 0)), rows)
+    mine = own_head(rows, width)
+    pay = jnp.zeros((rows, 256), F32)
+    for part, x in enumerate((q_ref[...], k_ref[...], v_ref[...], do_ref[...])):
+        pay += dot(jnp.where(mine, x, jnp.zeros_like(x)), spread(part, 256, width), 1, 0)
+    pay = dot(order, pay.astype(BF), 1, 0)
     lane = iota((1, 128), 1)
     token = iota((rows, 1), 0)
-    wide = stat_lanes(pay[:, 128:].astype(BF))
+    pick = iota((1, HEADS), 1) == (token & (GROUP - 1))
+    wide = jnp.zeros((rows, 128), F32)
+    for base, x in ((0, stat_ref[:, HEADS:]), (3, stat_ref[:, :HEADS])):
+        own = jnp.sum(jnp.where(pick, x, 0.0), axis=1, keepdims=True)
+        for n, piece in enumerate(pieces(own)):
+            wide += jnp.where((lane & 7) == base + n, piece, 0.0)
+    wide = dot(order, wide.astype(BF), 1, 0)
     wide = jnp.where((lane >> 3) == (token & 15), wide, 0.0).astype(BF)
     at, source = iota((40 * GROUP, 1), 0), iota((1, rows), 1)
     r = lax.div(at, 40)
@@ -231,8 +238,7 @@
 
 def packed_grads(lo, hi, stat):
     scale = float(HD) ** -0.5
-    one = eye(128)
-    x_t = jnp.concatenate([dot(one, lo, 1, 1), dot(one, hi, 1, 1)], axis=0).astype(BF)
+    x_t = jnp.concatenate([jnp.transpose(lo), jnp.transpose(hi)], axis=0)
     q_t, k_t, v_t, do_t = (x_t[HD * n : HD * (n + 1)] for n in range(4))
     piece = iota((128, 256), 0) & 7
     lse = dot(stat, (piece < 3).astype(BF), 1, 0)
@@ -252,11 +258,11 @@
 
 def sets_kernel(where_ref, in_ref, back_ref, grad_ref):
     own = pl.ds(GROUP * where_ref[1], GROUP)
-    rest = in_ref[:, 48:].astype(F32)
+    rest = in_ref[...][:, 48:].astype(F32)
     grad_ref[...] = jnp.sum(rest[:, 16:], axis=0)
     blank = jnp.zeros((256, 64), F32)
     token = iota((256, 1), 0)
-    mine = in_ref[own, 48:].astype(F32)[:, 16:24].reshape(8 * GROUP, 128).astype(BF)
+    mine = in_ref[own][:, 48:].astype(F32)[:, 16:24].reshape(8 * GROUP, 128).astype(BF)
     stat = stat_rows(mine, 8 * (token >> 5) + 3 + ((token >> 4) & 1), token & 15)
     pairs = in_ref[own, 32:48].astype(F32)
     hi = jnp.concatenate([pairs[:, :, :64], pairs[:, :, 64:]], axis=1).reshape(256, 64)
@@ -276,9 +282,8 @@
     far_token = iota((1, 256), 1)
     match = 128 * where_ref[1] + 16 * (token >> 5) + 12 + (token & 3)
     sel = ((far_token == match) & ((token & 31) < 4)).astype(BF)
-    turn = jnp.concatenate([eye(256), sel], axis=1)
-    hi, lo = split(jnp.concatenate([group, far], axis=1))
-    total = dot(turn, hi, 1, 1) + dot(turn, lo, 1, 1)
+    hi, lo = split(far)
+    total = jnp.transpose(group) + dot(sel, hi, 1, 1) + dot(sel, lo, 1, 1)
     for src in range(GROUP):
         rows = total[32 * src : 32 * (src + 1)]
         back_ref[src, :32] = rows[:, :128].astype(BF)
@@ -330,10 +335,9 @@
     outs = (
         shape((parts, width * cols // parts // 128 + 8 * HEADS, 128), BF),
         shape((rows, width), BF),
-        shape((rows, 256), BF),
         shape((rows, 2 * HEADS), F32),
     )
-    out, d_out, pay, stat = call(
+    out, d_out, stat = call(
         front_kernel,
         outs,
         *ins,
@@ -344,7 +348,7 @@
     )
     where = jnp.stack([lax.axis_index(a) for a in ("x", "zh", "c")]).astype(jnp.int32)
     over_x = exchange(out, ("x", "c"))
-    pay = call(pack_kernel, shape((GROUP, 88, 128), BF), pay, flops=100_000_000)
+    pay = call(pack_kernel, shape((GROUP, 88, 128), BF), q, k, v, d_out, stat, flops=300_000_000)
     near = call(
         local_kernel,
         (shape((rows, width), F32),) * 3,

time: 84.8 us -> 84.5 us (level)
  transfers between devices with their start and end apart: 2 -> 2, of which waited for: 1 -> 1; matrix products, arithmetic and copies ran while one was open for 0% -> 0% of each run, Pallas kernels for 3% -> 4%
where the time goes in v8:
time: 84.5 us; the launch traced here: 84.1 us
  blocking collectives  40.6 us (48%)
  starting transfers between devices  22.3 us (26%)
  Pallas kernels  12.3 us (15%)
  waiting for transfers between devices  8.09 us (10%)
    all_to_all x1, blocking collectives, exchange(): return lax.all_to_all(x, axes, 0, 0, tiled=True)  26.4 us
    all_to_all x2, starting transfers between devices, exchange(): return lax.all_to_all(x, axes, 0, 0, tiled=True)  22.3 us
    all_gather x1, blocking collectives, on_device(): grad = lax.all_gather(grad, ('y', 'c'), axis=0)  14.2 us
    pallas_call x6, Pallas kernels, call(): pl.pallas_call(kernel, out_shape=outs, in_specs=[pl.BlockSpec(memory_spac...  12.3 us
    all_to_all x2, waiting for transfers between devices, exchange(): return lax.all_to_all(x, axes, 0, 0, tiled=True)  8.09 us
  transfers between devices with their start and end apart: 2, of which 1 were waited for; matrix products, arithmetic and copies ran while one was open for 0% of the time, Pallas kernels for 4%

profile of v8, /device:TPU:1, one launch (start us, length us, event | category | flops | bytes accessed | tf_op | source)
XLA Modules:
  0.0 84.1 jit_solution(7358738493053738669)
XLA Ops:
  0.6 3.9 %shard_map.102 = (bf16[8,352,128]{2,1,0:T(8,128)(2,1)}, bf16[256,384]{1,0:T(8,128)(2,1)}, f32[256,16]{1,0:T(8,128)}) custom-call(bf16[256,768]{1,0:T(8,128)(2,1)} %bitcast.25, bf16[256,384]{1,0:T(8,128)(2,1)} %bitcast.26, bf16[384,768]{1,0:T(8,128)(2,1)} %refs_2_.1, f32[8,256]{1,0:T(8,128)} %bitcast.30, bf16[256,384]{1,0:T(8,128)(2,1)} %bitcast.16, ...), custom_call_target="tpu_custom_call" | custom-call | flops 1000000000 | bytes 2000000 | tf_op jit(solution)/shard_map/pallas_call | solution.py:312
  4.6 0.0 copy-start
  4.6 0.0 copy-start.1
  4.6 0.0 copy-start.2
  4.6 0.0 copy-start.3
  4.6 0.0 copy-start.4
  4.6 10.5 %all-to-all-start = ((bf16[8,352,128]{2,1,0:T(8,128)(2,1)}), bf16[8,352,128]{2,1,0:T(8,128)(2,1)S(1)}, u32[]{:S(2)}, u32[]{:S(2)}) async-start(bf16[8,352,128]{2,1,0:T(8,128)(2,1)} %get-tuple-element.16), calls=%async_computation | async-start | bytes 1441792 | tf_op jit(solution)/shard_map/all_to_all | solution.py:331
  15.1 0.0 copy-done
  15.1 0.0 copy-done.1
  15.1 0.0 copy-done.2
  15.1 0.0 copy-done.3
  15.1 0.0 copy-done.4
  15.1 1.1 %shard_map.103.pay_ref = bf16[8,88,128]{2,1,0:T(8,128)(2,1)S(1)} custom-call(bf16[256,384]{1,0:T(8,128)(2,1)S(1)} %bitcast.17, bf16[256,384]{1,0:T(8,128)(2,1)S(1)} %bitcast.20, bf16[256,384]{1,0:T(8,128)(2,1)S(1)} %bitcast.23, bf16[256,384]{1,0:T(8,128)(2,1)S(1)} %copy-done.3, f32[256,16]{1,0:T(8,128)S(1)} %copy-done.4), custom_call_target="tpu_custom_call" | custom-call | flops 300000000 | bytes 2000000 | tf_op jit(solution)/shard_map/pallas_call | solution.py:312
  16.2 2.3 %shard_map.104 = (f32[256,384]{1,0:T(8,128)S(1)}, f32[256,384]{1,0:T(8,128)S(1)}, f32[256,384]{1,0:T(8,128)S(1)}) custom-call(bf16[256,384]{1,0:T(8,128)(2,1)S(1)} %bitcast.18, bf16[256,384]{1,0:T(8,128)(2,1)S(1)} %bitcast.21, bf16[256,384]{1,0:T(8,128)(2,1)S(1)} %bitcast.24, bf16[256,384]{1,0:T(8,128)(2,1)S(1)} %copy-done.3, f32[256,16]{1,0:T(8,128)S(1)} %copy-done.4), custom_call_target="tpu_custom_call" | custom-call | flops 1000000000 | bytes 2000000 | tf_op jit(solution)/shard_map/pallas_call | solution.py:312
  18.5 0.1 pad_add_fusion.where_ref
  18.6 8.1 %all-to-all-done.in_ref = bf16[8,352,128]{2,1,0:T(8,128)(2,1)S(1)} async-done(((bf16[8,352,128]{2,1,0:T(8,128)(2,1)}), bf16[8,352,128]{2,1,0:T(8,128)(2,1)S(1)}, u32[]{:S(2)}, u32[]{:S(2)}) %all-to-all-start) | async-done | bytes 720928 | tf_op jit(solution)/shard_map/all_to_all | solution.py:331
  26.7 1.2 %shard_map.105 = bf16[16,88,128]{2,1,0:T(8,128)(2,1)S(1)} custom-call(s32[3]{0:T(128)S(1)} %pad_add_fusion.where_ref, bf16[8,352,128]{2,1,0:T(8,128)(2,1)S(1)} %all-to-all-done.in_ref, bf16[8,88,128]{2,1,0:T(8,128)(2,1)S(1)} %shard_map.103.pay_ref, f32[256,384]{1,0:T(8,128)S(1)} %get-tuple-element.19._.dq_ref), custom_call_target="tpu_custom_call" | custom-call | flops 100000000 | bytes 2000000 | tf_op jit(solution)/shard_map/pallas_call | solution.py:312
  27.9 26.4 %all_to_all.15.in_ref = bf16[16,88,128]{2,1,0:T(8,128)(2,1)S(1)} all-to-all(bf16[16,88,128]{2,1,0:T(8,128)(2,1)S(1)} %shard_map.105), channel_id=1, replica_groups=mesh['y'=4,'c'=2,'x'=4,'zh'=2,'zl'=8] {'zh','zl'}, dimensions={0} | all-to-all | bytes 720896 | tf_op jit(solution)/shard_map/all_to_all | solution.py:331
  54.3 2.5 %shard_map.106 = (bf16[8,48,128]{2,1,0:T(8,128)(2,1)}, f32[24,128]{1,0:T(8,128)S(1)}) custom-call(s32[3]{0:T(128)S(1)} %pad_add_fusion.where_ref, bf16[16,88,128]{2,1,0:T(8,128)(2,1)S(1)} %all_to_all.15.in_ref), custom_call_target="tpu_custom_call" | custom-call | flops 200000000 | bytes 2000000 | tf_op jit(solution)/shard_map/pallas_call | solution.py:312
  56.7 11.9 %all-to-all-start.2 = ((bf16[8,48,128]{2,1,0:T(8,128)(2,1)}), bf16[8,48,128]{2,1,0:T(8,128)(2,1)S(1)}, u32[]{:S(2)}, u32[]{:S(2)}) async-start(bf16[8,48,128]{2,1,0:T(8,128)(2,1)} %get-tuple-element.20), calls=%async_computation.2 | async-start | bytes 196608 | tf_op jit(solution)/shard_map/all_to_all | solution.py:331
  68.6 14.2 %all-gather = f32[192,128]{1,0:T(8,128)S(1)} all-gather(f32[24,128]{1,0:T(8,128)S(1)} %get-tuple-element.23), channel_id=2, replica_groups=mesh['y'=4,'c'=2,'x'=4,'zh'=2,'zl'=8] {'y','c'}, dimensions={0}, use_global_device_ids=true | all-gather | bytes 110592 | tf_op jit(solution)/shard_map/all_gather | solution.py:365
  82.8 0.0 all-to-all-done.2.z_ref
  82.8 1.3 %shard_map.107 = (bf16[256,384]{1,0:T(8,128)(2,1)}, bf16[256,384]{1,0:T(8,128)(2,1)}, bf16[256,384]{1,0:T(8,128)(2,1)}, f32[6,768]{1,0:T(8,128)}) custom-call(bf16[8,48,128]{2,1,0:T(8,128)(2,1)S(1)} %all-to-all-done.2.z_ref, f32[256,384]{1,0:T(8,128)S(1)} %get-tuple-element.19._.dq_ref, f32[256,384]{1,0:T(8,128)S(1)} %get-tuple-element.21.dk_ref, ...), custom_call_target="tpu_custom_call" | custom-call | flops 300000000 | bytes 2000000 | tf_op jit(solution)/shard_map/pallas_call | solution.py:312
Async XLA Ops:
  4.6 10.5 %copy-start = (bf16[1,256,384]{2,1,0:T(8,128)(2,1)S(1)}, bf16[1,256,384]{2,1,0:T(8,128)(2,1)}, u32[]{:S(2)}) copy-start(bf16[1,256,384]{2,1,0:T(8,128)(2,1)} %param.7) | copy-start | bytes 589828
  4.6 10.5 %copy-start.1 = (bf16[1,256,384]{2,1,0:T(8,128)(2,1)S(1)}, bf16[1,256,384]{2,1,0:T(8,128)(2,1)}, u32[]{:S(2)}) copy-start(bf16[1,256,384]{2,1,0:T(8,128)(2,1)} %param.8) | copy-start | bytes 589828
  4.6 10.5 %copy-start.2 = (bf16[1,256,384]{2,1,0:T(8,128)(2,1)S(1)}, bf16[1,256,384]{2,1,0:T(8,128)(2,1)}, u32[]{:S(2)}) copy-start(bf16[1,256,384]{2,1,0:T(8,128)(2,1)} %param.9) | copy-start | bytes 589828
  4.6 10.5 %copy-start.3 = (bf16[256,384]{1,0:T(8,128)(2,1)S(1)}, bf16[256,384]{1,0:T(8,128)(2,1)}, u32[]{:S(2)}) copy-start(bf16[256,384]{1,0:T(8,128)(2,1)} %get-tuple-element.17.do_ref) | copy-start | bytes 589828
  4.6 10.5 %copy-start.4 = (f32[256,16]{1,0:T(8,128)S(1)}, f32[256,16]{1,0:T(8,128)}, u32[]{:S(2)}) copy-start(f32[256,16]{1,0:T(8,128)} %get-tuple-element.18.stat_ref) | copy-start | bytes 49156
  4.6 22.1 %all-to-all-start = ((bf16[8,352,128]{2,1,0:T(8,128)(2,1)}), bf16[8,352,128]{2,1,0:T(8,128)(2,1)S(1)}, u32[]{:S(2)}, u32[]{:S(2)}) async-start(bf16[8,352,128]{2,1,0:T(8,128)(2,1)} %get-tuple-element.16), calls=%async_computation | async-start | bytes 1441792 | tf_op jit(solution)/shard_map/all_to_all | solution.py:331
  56.7 26.1 %all-to-all-start.2 = ((bf16[8,48,128]{2,1,0:T(8,128)(2,1)}), bf16[8,48,128]{2,1,0:T(8,128)(2,1)S(1)}, u32[]{:S(2)}, u32[]{:S(2)}) async-start(bf16[8,48,128]{2,1,0:T(8,128)(2,1)} %get-tuple-element.20), calls=%async_computation.2 | async-start | bytes 196608 | tf_op jit(solution)/shard_map/all_to_all | solution.py:331

commit v9 on v8

--- a/solution.py
+++ b/solution.py
@@ -11,6 +11,7 @@
 HD = 48
 GROUP = 8
 CORES = 2
+STEP = 7
 ROOM = 60
 BF = jnp.bfloat16
 F32 = jnp.float32
@@ -172,7 +173,7 @@
         own = pay_ref[r].astype(F32)
         for z in range(r, ring, GROUP):
             rest = own[48:] + top[40 * r : 40 * (r + 1)] + grad[40 * z : 40 * (z + 1)]
-            out_ref[z] = jnp.concatenate([own[:48], rest], axis=0).astype(BF)
+            out_ref[STEP * z % ring] = jnp.concatenate([own[:48], rest], axis=0).astype(BF)
 
 
 def weight_end(in_ref, out_ref):
@@ -257,17 +258,19 @@
 
 
 def sets_kernel(where_ref, in_ref, back_ref, grad_ref):
-    own = pl.ds(GROUP * where_ref[1], GROUP)
+    ring = in_ref.shape[0]
+    own = [in_ref[(GROUP * where_ref[1] + STEP * src) & (ring - 1)] for src in range(GROUP)]
+    own = jnp.concatenate([x[None] for x in own], axis=0)
     rest = in_ref[...][:, 48:].astype(F32)
     grad_ref[...] = jnp.sum(rest[:, 16:], axis=0)
     blank = jnp.zeros((256, 64), F32)
     token = iota((256, 1), 0)
-    mine = in_ref[own][:, 48:].astype(F32)[:, 16:24].reshape(8 * GROUP, 128).astype(BF)
+    mine = own[:, 48:].astype(F32)[:, 16:24].reshape(8 * GROUP, 128).astype(BF)
     stat = stat_rows(mine, 8 * (token >> 5) + 3 + ((token >> 4) & 1), token & 15)
-    pairs = in_ref[own, 32:48].astype(F32)
+    pairs = own[:, 32:48].astype(F32)
     hi = jnp.concatenate([pairs[:, :, :64], pairs[:, :, 64:]], axis=1).reshape(256, 64)
     hi = jnp.concatenate([hi, blank], axis=1)
-    group = packed_grads(in_ref[own, :32].reshape(256, 128), hi.astype(BF), stat)
+    group = packed_grads(own[:, :32].reshape(256, 128), hi.astype(BF), stat)
     n = token & 15
     h = (n >= 6).astype(jnp.int32)
     lanes = jnp.where(n < 12, 4 * ((n - 6 * h) >> 1) + (n & 1) + 2 * h, n - 12)
@@ -280,7 +283,8 @@
     hi = jnp.concatenate([hi, blank], axis=1)
     far = packed_grads(lo.astype(BF), hi.astype(BF), stat)
     far_token = iota((1, 256), 1)
-    match = 128 * where_ref[1] + 16 * (token >> 5) + 12 + (token & 3)
+    place = (GROUP * where_ref[1] + STEP * (token >> 5)) & (ring - 1)
+    match = 16 * place + 12 + (token & 3)
     sel = ((far_token == match) & ((token & 31) < 4)).astype(BF)
     hi, lo = split(far)
     total = jnp.transpose(group) + dot(sel, hi, 1, 1) + dot(sel, lo, 1, 1)
@@ -324,11 +328,14 @@
     q, k, v, o, dy, lse = (x[0] for x in (queries, keys, values, outputs, d_final, stats))
     rows, width = q.shape
     cols = dy.shape[1]
-    blocks, ring = lax.axis_size("x"), lax.axis_size(("zh", "zl"))
+    blocks, ring = lax.axis_size("x"), lax.axis_size("z")
     shape = jax.ShapeDtypeStruct
 
-    def exchange(x, axes):
-        return lax.all_to_all(x, axes, 0, 0, tiled=True)
+    def exchange(x, axes, groups=None):
+        return lax.all_to_all(x, axes, 0, 0, axis_index_groups=groups, tiled=True)
+
+    stepped = [[STEP * n % ring for n in range(ring)]]
+    halves = [list(range(n, n + GROUP)) for n in range(0, ring, GROUP)]
 
     ins = (dy, o, w_out, lse.T, q, k, v)
     parts = blocks * CORES
@@ -346,7 +353,8 @@
         scratch=[pltpu.VMEM(x.shape, x.dtype) for x in ins] + [pltpu.SemaphoreType.DMA((len(ins),))],
         flops=1_000_000_000,
     )
-    where = jnp.stack([lax.axis_index(a) for a in ("x", "zh", "c")]).astype(jnp.int32)
+    where = [lax.axis_index("x"), lax.axis_index("z") // GROUP, lax.axis_index("c")]
+    where = jnp.stack(where).astype(jnp.int32)
     over_x = exchange(out, ("x", "c"))
     pay = call(pack_kernel, shape((GROUP, 88, 128), BF), q, k, v, d_out, stat, flops=300_000_000)
     near = call(
@@ -357,11 +365,11 @@
         flops=1_000_000_000,
     )
     out = call(mid_kernel, shape((ring, 88, 128), BF), where, over_x, pay, near[0], smem=1, flops=100_000_000)
-    over_z = exchange(out, ("zh", "zl"))
+    over_z = exchange(out, "z", stepped)
     back, grad = call(
         sets_kernel, (shape((GROUP, 48, 128), BF), shape((24, 128), F32)), where, over_z, smem=1, flops=200_000_000
     )
-    z = exchange(back, "zl")
+    z = exchange(back, "z", halves)
     grad = lax.all_gather(grad, ("y", "c"), axis=0)
     d_q, d_k, d_v, grad = call(
         final_kernel,
@@ -375,9 +383,9 @@
 def solution(mesh):
     dp, seq = mesh.devices.shape
     fine = jax.sharding.Mesh(
-        mesh.devices.reshape(dp // CORES, CORES, seq // 16, 16 // GROUP, GROUP), ("y", "c", "x", "zh", "zl")
-    )
-    dp_axes, seq_axes = ("y", "c"), ("x", "zh", "zl")
+        mesh.devices.reshape(dp // CORES, CORES, seq // 16, 16), ("y", "c", "x", "z")
+    )
+    dp_axes, seq_axes = ("y", "c"), ("x", "z")
     placed = P(dp_axes, seq_axes, None)
     return jax.shard_map(
         on_device,

time: 84.5 us -> 84.5 us (level)
  blocking collectives: 40.6 us -> 39.3 us
  starting transfers between devices: 22.3 us -> 23.6 us
    all_to_all x2, starting transfers between devices: 22.3 us -> 23.6 us  [exchange(): return lax.all_to_all(x, axes, 0, 0, axis_index_groups=groups, tiled=True)]
    all_to_all x1, blocking collectives: 26.4 us -> 25.5 us  [exchange(): return lax.all_to_all(x, axes, 0, 0, axis_index_groups=groups, tiled=True)]
where the time goes in v9:
time: 84.5 us; the launch traced here: 84.1 us
  blocking collectives  39.3 us (47%)
  starting transfers between devices  23.6 us (28%)
  Pallas kernels  12.3 us (15%)
  waiting for transfers between devices  8.09 us (10%)
    all_to_all x1, blocking collectives, exchange(): return lax.all_to_all(x, axes, 0, 0, axis_index_groups=groups, tiled=True)  25.5 us
    all_to_all x2, starting transfers between devices, exchange(): return lax.all_to_all(x, axes, 0, 0, axis_index_groups=groups, tiled=True)  23.6 us
    all_gather x1, blocking collectives, on_device(): grad = lax.all_gather(grad, ('y', 'c'), axis=0)  13.8 us
    pallas_call x6, Pallas kernels, call(): pl.pallas_call(kernel, out_shape=outs, in_specs=[pl.BlockSpec(memory_spac...  12.3 us
    all_to_all x2, waiting for transfers between devices, exchange(): return lax.all_to_all(x, axes, 0, 0, axis_index_groups=groups, tiled=True)  8.09 us
  transfers between devices with their start and end apart: 2, of which 1 were waited for; matrix products, arithmetic and copies ran while one was open for 0% of the time, Pallas kernels for 4%

profile of v9, /device:TPU:1, one launch (start us, length us, event | category | flops | bytes accessed | tf_op | source)
XLA Modules:
  0.0 84.1 jit_solution(14816205787581326180)
XLA Ops:
  0.6 3.9 %shard_map.102 = (bf16[8,352,128]{2,1,0:T(8,128)(2,1)}, bf16[256,384]{1,0:T(8,128)(2,1)}, f32[256,16]{1,0:T(8,128)}) custom-call(bf16[256,768]{1,0:T(8,128)(2,1)} %bitcast.25, bf16[256,384]{1,0:T(8,128)(2,1)} %bitcast.26, bf16[384,768]{1,0:T(8,128)(2,1)} %refs_2_.1, f32[8,256]{1,0:T(8,128)} %bitcast.30, bf16[256,384]{1,0:T(8,128)(2,1)} %bitcast.16, ...), custom_call_target="tpu_custom_call" | custom-call | flops 1000000000 | bytes 2000000 | tf_op jit(solution)/shard_map/pallas_call | solution.py:316
  4.6 0.0 copy-start
  4.6 0.0 copy-start.1
  4.6 0.0 copy-start.2
  4.6 0.0 copy-start.3
  4.6 0.0 copy-start.4
  4.6 10.5 %all-to-all-start = ((bf16[8,352,128]{2,1,0:T(8,128)(2,1)}), bf16[8,352,128]{2,1,0:T(8,128)(2,1)S(1)}, u32[]{:S(2)}, u32[]{:S(2)}) async-start(bf16[8,352,128]{2,1,0:T(8,128)(2,1)} %get-tuple-element.16), calls=%async_computation | async-start | bytes 1441792 | tf_op jit(solution)/shard_map/all_to_all | solution.py:335
  15.1 0.0 copy-done
  15.1 0.0 copy-done.1
  15.1 0.0 copy-done.2
  15.1 0.0 copy-done.3
  15.1 0.0 copy-done.4
  15.1 1.1 %shard_map.103.pay_ref = bf16[8,88,128]{2,1,0:T(8,128)(2,1)S(1)} custom-call(bf16[256,384]{1,0:T(8,128)(2,1)S(1)} %bitcast.17, bf16[256,384]{1,0:T(8,128)(2,1)S(1)} %bitcast.20, bf16[256,384]{1,0:T(8,128)(2,1)S(1)} %bitcast.23, bf16[256,384]{1,0:T(8,128)(2,1)S(1)} %copy-done.3, f32[256,16]{1,0:T(8,128)S(1)} %copy-done.4), custom_call_target="tpu_custom_call" | custom-call | flops 300000000 | bytes 2000000 | tf_op jit(solution)/shard_map/pallas_call | solution.py:316
  16.2 2.3 %shard_map.104 = (f32[256,384]{1,0:T(8,128)S(1)}, f32[256,384]{1,0:T(8,128)S(1)}, f32[256,384]{1,0:T(8,128)S(1)}) custom-call(bf16[256,384]{1,0:T(8,128)(2,1)S(1)} %bitcast.18, bf16[256,384]{1,0:T(8,128)(2,1)S(1)} %bitcast.21, bf16[256,384]{1,0:T(8,128)(2,1)S(1)} %bitcast.24, bf16[256,384]{1,0:T(8,128)(2,1)S(1)} %copy-done.3, f32[256,16]{1,0:T(8,128)S(1)} %copy-done.4), custom_call_target="tpu_custom_call" | custom-call | flops 1000000000 | bytes 2000000 | tf_op jit(solution)/shard_map/pallas_call | solution.py:316
  18.5 0.1 pad_add_fusion.where_ref
  18.6 8.1 %all-to-all-done.in_ref = bf16[8,352,128]{2,1,0:T(8,128)(2,1)S(1)} async-done(((bf16[8,352,128]{2,1,0:T(8,128)(2,1)}), bf16[8,352,128]{2,1,0:T(8,128)(2,1)S(1)}, u32[]{:S(2)}, u32[]{:S(2)}) %all-to-all-start) | async-done | bytes 720928 | tf_op jit(solution)/shard_map/all_to_all | solution.py:335
  26.7 1.2 %shard_map.105 = bf16[16,88,128]{2,1,0:T(8,128)(2,1)S(1)} custom-call(s32[3]{0:T(128)S(1)} %pad_add_fusion.where_ref, bf16[8,352,128]{2,1,0:T(8,128)(2,1)S(1)} %all-to-all-done.in_ref, bf16[8,88,128]{2,1,0:T(8,128)(2,1)S(1)} %shard_map.103.pay_ref, f32[256,384]{1,0:T(8,128)S(1)} %get-tuple-element.19._.dq_ref), custom_call_target="tpu_custom_call" | custom-call | flops 100000000 | bytes 2000000 | tf_op jit(solution)/shard_map/pallas_call | solution.py:316
  27.9 25.5 %all_to_all.15.in_ref = bf16[16,88,128]{2,1,0:T(8,128)(2,1)S(1)} all-to-all(bf16[16,88,128]{2,1,0:T(8,128)(2,1)S(1)} %shard_map.105), channel_id=1, replica_groups={{0,7,14,5,12,3,10,1,8,15,6,13,4,11,2,9},{16,23,30,21,28,19,26,17,24,31,..., dimensions={0} | all-to-all | bytes 720896 | tf_op jit(solution)/shard_map/all_to_all | solution.py:335
  53.4 2.5 %shard_map.106 = (bf16[8,48,128]{2,1,0:T(8,128)(2,1)}, f32[24,128]{1,0:T(8,128)S(1)}) custom-call(s32[3]{0:T(128)S(1)} %pad_add_fusion.where_ref, bf16[16,88,128]{2,1,0:T(8,128)(2,1)S(1)} %all_to_all.15.in_ref), custom_call_target="tpu_custom_call" | custom-call | flops 200000000 | bytes 2000000 | tf_op jit(solution)/shard_map/pallas_call | solution.py:316
  55.8 13.1 %all-to-all-start.2 = ((bf16[8,48,128]{2,1,0:T(8,128)(2,1)}), bf16[8,48,128]{2,1,0:T(8,128)(2,1)S(1)}, u32[]{:S(2)}, u32[]{:S(2)}) async-start(bf16[8,48,128]{2,1,0:T(8,128)(2,1)} %get-tuple-element.20), calls=%async_computation.2 | async-start | bytes 196608 | tf_op jit(solution)/shard_map/all_to_all | solution.py:335
  68.9 13.8 %all-gather = f32[192,128]{1,0:T(8,128)S(1)} all-gather(f32[24,128]{1,0:T(8,128)S(1)} %get-tuple-element.23), channel_id=2, replica_groups=mesh['y'=4,'c'=2,'x'=4,'z'=16] {'y','c'}, dimensions={0}, use_global_device_ids=true | all-gather | bytes 110592 | tf_op jit(solution)/shard_map/all_gather | solution.py:373
  82.8 0.0 all-to-all-done.2.z_ref
  82.8 1.3 %shard_map.107 = (bf16[256,384]{1,0:T(8,128)(2,1)}, bf16[256,384]{1,0:T(8,128)(2,1)}, bf16[256,384]{1,0:T(8,128)(2,1)}, f32[6,768]{1,0:T(8,128)}) custom-call(bf16[8,48,128]{2,1,0:T(8,128)(2,1)S(1)} %all-to-all-done.2.z_ref, f32[256,384]{1,0:T(8,128)S(1)} %get-tuple-element.19._.dq_ref, f32[256,384]{1,0:T(8,128)S(1)} %get-tuple-element.21.dk_ref, ...), custom_call_target="tpu_custom_call" | custom-call | flops 300000000 | bytes 2000000 | tf_op jit(solution)/shard_map/pallas_call | solution.py:316
Async XLA Ops:
  4.6 10.5 %copy-start = (bf16[1,256,384]{2,1,0:T(8,128)(2,1)S(1)}, bf16[1,256,384]{2,1,0:T(8,128)(2,1)}, u32[]{:S(2)}) copy-start(bf16[1,256,384]{2,1,0:T(8,128)(2,1)} %param.7) | copy-start | bytes 589828
  4.6 10.5 %copy-start.1 = (bf16[1,256,384]{2,1,0:T(8,128)(2,1)S(1)}, bf16[1,256,384]{2,1,0:T(8,128)(2,1)}, u32[]{:S(2)}) copy-start(bf16[1,256,384]{2,1,0:T(8,128)(2,1)} %param.8) | copy-start | bytes 589828
  4.6 10.5 %copy-start.2 = (bf16[1,256,384]{2,1,0:T(8,128)(2,1)S(1)}, bf16[1,256,384]{2,1,0:T(8,128)(2,1)}, u32[]{:S(2)}) copy-start(bf16[1,256,384]{2,1,0:T(8,128)(2,1)} %param.9) | copy-start | bytes 589828
  4.6 10.5 %copy-start.3 = (bf16[256,384]{1,0:T(8,128)(2,1)S(1)}, bf16[256,384]{1,0:T(8,128)(2,1)}, u32[]{:S(2)}) copy-start(bf16[256,384]{1,0:T(8,128)(2,1)} %get-tuple-element.17.do_ref) | copy-start | bytes 589828
  4.6 10.5 %copy-start.4 = (f32[256,16]{1,0:T(8,128)S(1)}, f32[256,16]{1,0:T(8,128)}, u32[]{:S(2)}) copy-start(f32[256,16]{1,0:T(8,128)} %get-tuple-element.18.stat_ref) | copy-start | bytes 49156
  4.6 22.1 %all-to-all-start = ((bf16[8,352,128]{2,1,0:T(8,128)(2,1)}), bf16[8,352,128]{2,1,0:T(8,128)(2,1)S(1)}, u32[]{:S(2)}, u32[]{:S(2)}) async-start(bf16[8,352,128]{2,1,0:T(8,128)(2,1)} %get-tuple-element.16), calls=%async_computation | async-start | bytes 1441792 | tf_op jit(solution)/shard_map/all_to_all | solution.py:335
  55.8 27.0 %all-to-all-start.2 = ((bf16[8,48,128]{2,1,0:T(8,128)(2,1)}), bf16[8,48,128]{2,1,0:T(8,128)(2,1)S(1)}, u32[]{:S(2)}, u32[]{:S(2)}) async-start(bf16[8,48,128]{2,1,0:T(8,128)(2,1)} %get-tuple-element.20), calls=%async_computation.2 | async-start | bytes 196608 | tf_op jit(solution)/shard_map/all_to_all | solution.py:335
